TPU v7x, 32 devices: a whole 2x2x4 slice. The times are simulated.
32 devices in a mesh: page: 16 (over z, y, x), head: 2 (over core).
Axes of the slice: x: 2, y: 2, z: 4, core: 2. Of those that a mesh axis runs over, the one named last changes fastest.
Arguments:
- query: bfloat16 [16, 8192], P('page', 'head'), may hold values from -68 to 68
- key_codes: bfloat16 [128, 8, 1024, 128], P('page', 'head'), may hold values from -6 to 6
- value_codes: bfloat16 [128, 8, 1024, 128], P('page', 'head'), may hold values from -6 to 6
- key_scale: float32 [128, 8, 8], P('page', 'head'), may hold values from 0.5 to 2
- value_scale: float32 [128, 8, 8], P('page', 'head'), may hold values from 0.5 to 8
- out_weight: bfloat16 [8192, 8192], P('head', 'page'), may hold values from -0.0625 to 0.0625
- range_counts: int32 [16], replicated, may hold values from 1 to 16, 128 in all
- last_fill: int32 [16], replicated, may hold values from 1 to 1024
- slot_table: int32 [128], replicated, may hold values from 0 to 127, each once
Outputs:
- mixed: bfloat16 [16, 8192], P('head', 'page')
All inputs are finite; a program needn't handle non-finite values.
Results may differ from a plain program's by a relative error of at most 0.0056.
Values may be sent and summed in bfloat16 or wider, within the bound.
No kernel may reach another device: no remote copies, remote signals or barrier semaphores. Data moves between devices by JAX's collectives and lax.ppermute only.
A program may use at most 64 MiB of HBM per device.

v0:
```python
import jax
import jax.numpy as jnp
from jax import lax
from jax.sharding import PartitionSpec as P


def per_device(
    query,
    key_codes,
    value_codes,
    key_scale,
    value_scale,
    out_weight,
    range_counts,
    last_fill,
    slot_table,
):
    slot_count, head_local, range_tok, head_dim = key_codes.shape
    page_tok = range_tok // key_scale.shape[2]
    row_count = range_counts.shape[0]
    total_slots = slot_table.shape[0]
    query_heads = query.shape[1] // head_dim
    group = query_heads // head_local
    inclusive = jnp.cumsum(range_counts)
    exclusive = inclusive - range_counts
    lengths = (range_counts - 1) * range_tok + last_fill
    mine = lax.axis_index("page") * slot_count + jnp.arange(slot_count, dtype=jnp.int32)
    positions = jnp.arange(total_slots, dtype=jnp.int32)
    inverse = jnp.sum(
        jnp.where(slot_table[None, :] == mine[:, None], positions[None, :], 0), axis=1
    )
    slot_row = jnp.sum((inverse[:, None] >= inclusive[None, :]).astype(jnp.int32), axis=1)
    picked = slot_row[:, None] == jnp.arange(row_count, dtype=jnp.int32)[None, :]
    slot_range = inverse - jnp.sum(jnp.where(picked, exclusive[None, :], 0), axis=1)
    slot_len = jnp.sum(jnp.where(picked, lengths[None, :], 0), axis=1)
    every_query = lax.all_gather(query, "page", axis=0, tiled=True)
    chosen = jnp.dot(
        picked.astype(jnp.bfloat16), every_query, preferred_element_type=jnp.float32
    ).astype(jnp.bfloat16)
    chosen = chosen.reshape(slot_count, head_local, group, head_dim)
    dotted = jnp.einsum("skgd,sktd->skgt", chosen, key_codes, preferred_element_type=jnp.float32)
    key_token_rows = jnp.repeat(key_scale, page_tok, axis=2)
    scores = dotted * key_token_rows[:, :, None, :] * head_dim ** (-0.5)
    token_index = jnp.arange(range_tok, dtype=jnp.int32)
    live = slot_range[:, None] * range_tok + token_index[None, :] < slot_len[:, None]
    scores = jnp.where(live[:, None, None, :], scores, -jnp.inf)
    maxima = jnp.max(scores, axis=-1)
    expons = jnp.exp(scores - maxima[..., None])
    totals = jnp.sum(expons, axis=-1).reshape(slot_count, query_heads)
    value_tok = jnp.repeat(value_scale, page_tok, axis=2)
    weights = (expons * value_tok[:, :, None, :]).astype(jnp.bfloat16)
    partial_out = jnp.einsum(
        "skgt,sktd->skgd", weights, value_codes, preferred_element_type=jnp.float32
    )
    partial_out = partial_out.reshape(slot_count, query_heads * head_dim)
    maxima = maxima.reshape(slot_count, query_heads)
    local_top = jnp.max(jnp.where(picked[:, :, None], maxima[:, None, :], -jnp.inf), axis=0)
    picked_float = picked.astype(jnp.float32)
    highest = lax.pmax(local_top, "page")
    slot_top = jnp.sum(jnp.where(picked[:, :, None], highest[None, :, :], 0.0), axis=1)
    factor = jnp.exp(maxima - slot_top)
    numerator = jnp.dot(
        picked_float.T,
        jnp.repeat(factor, head_dim, axis=1) * partial_out,
        precision=lax.Precision.HIGHEST,
    )
    denominator = jnp.dot(picked_float.T, factor * totals, precision=lax.Precision.HIGHEST)
    numerator, denominator = (numerator, denominator)
    own_num, own_den = (
        lax.psum_scatter(numerator, "page", scatter_dimension=0, tiled=True),
        lax.psum_scatter(denominator, "page", scatter_dimension=0, tiled=True),
    )
    own_rows = own_num.shape[0]
    quotient = own_num.reshape(own_rows, query_heads, head_dim) / own_den[:, :, None]
    attention = quotient.reshape(own_rows, query_heads * head_dim).astype(jnp.bfloat16)
    attention_all = lax.all_gather(attention, "page", axis=0, tiled=True)
    mixed = lax.psum_scatter(
        jnp.dot(attention_all, out_weight, preferred_element_type=jnp.float32),
        "head",
        scatter_dimension=0,
        tiled=True,
    )
    return mixed.astype(jnp.bfloat16)


def solution(mesh):
    return jax.shard_map(
        per_device,
        mesh=mesh,
        in_specs=(
            P("page", "head"),
            P("page", "head", None, None),
            P("page", "head", None, None),
            P("page", "head", None),
            P("page", "head", None),
            P("head", "page"),
            P(),
            P(),
            P(),
        ),
        out_specs=P("head", "page"),
        check_vma=False,
    )
```

profile of v0, /device:TPU:0, one launch (start us, length us, event | category | flops | bytes accessed | tf_op | source)
XLA Modules:
  0.0 265.6 jit_solution(7515042440059257011)
XLA Ops:
  6.5 0.8 broadcast_in_dim.113
  7.4 44.0 %all-gather = bf16[16,1,4096]{2,1,0:T(2,128)(2,1)S(1)} all-gather(bf16[1,1,4096]{2,1,0:T(2,128)(2,1)} %bitcast.35), channel_id=1, replica_groups=mesh['page'=16,'head'=2] {'page'}, dimensions={0}, use_global_device_ids=true | all-gather | bytes 139264 | tf_op jit(solution)/shard_map/all_gather | solution.py:36
  51.4 0.7 copy.19
  52.2 0.1 reduce
  52.3 0.8 select_reduce_fusion.4
  53.2 0.2 convert_reduce_fusion
  53.4 0.3 convolution_convert_fusion
  53.7 0.7 multiply_add_fusion
  54.4 0.2 select_reduce_fusion.3
  54.6 5.7 %fusion.21 = (f32[8,4,8]{2,1,0:T(4,128)S(1)}, f32[8,4,8,1024]{3,2,1,0:T(8,128)S(1)}) fusion(f32[8,4,1024]{2,1,0:T(4,128)S(1)} %mul.49, bf16[8,4,1024,128]{3,2,1,0:T(8,128)(2,1)} %param.10, bf16[8,4,8,128]{3,0,2,1:T(8,128)(2,1)S(1)} %bitcast.33, pred[8,1024]{1,0:T(8,128)(4,1)S(1)} %add_compare_fusion), kind=kOutput, calls=%fused_computation.42 | convolution fusion | flops 68157184 | bytes 9643008 | tf_op jit(solution)/shard_map/skgd,sktd->skgt/dot_general | solution.py:41
  60.6 37.1 %pmax.7 = f32[16,32]{1,0:T(8,128)S(1)} all-reduce(f32[16,32]{1,0:T(8,128)S(1)} %select_reduce_fusion.1), channel_id=1, replica_groups=mesh['page'=16,'head'=2] {'page'}, use_global_device_ids=true, to_apply=%region_7.8 | all-reduce | flops 512 | bytes 4096 | tf_op jit(solution)/shard_map/pmax | solution.py:59
  98.0 4.6 %convolution_bitcast_fusion = f32[1,8,32,128]{3,2,1,0:T(8,128)S(1)} fusion(bf16[8,4,1024,128]{3,2,1,0:T(8,128)(2,1)} %param.11, f32[8,4,8,1024]{3,2,1,0:T(8,128)S(1)} %get-tuple-element.10, f32[8,4,1024]{2,1,0:T(4,128)S(1)} %mul.54, f32[8,4,8]{2,1,0:T(4,128)S(1)} %get-tuple-element.9), kind=kOutput, calls=%fused_computation.4 | convolution fusion | flops 67895296 | bytes 9700352 | tf_op jit(solution)/shard_map/skgt,sktd->skgd/dot_general | solution.py:52
  102.7 1.1 fusion.5
  103.8 0.3 fusion.2
  104.2 0.6 dynamic-slice
  104.8 0.3 fusion.15
  105.1 39.2 %all-reduce.1 = f32[16,32]{1,0:T(8,128)S(1)} all-reduce(f32[16,32]{1,0:T(8,128)S(1)} %fusion.15), channel_id=3, replica_groups=mesh['page'=16,'head'=2] {'page'}, use_global_device_ids=true, to_apply=%region_11.12.clone | all-reduce | flops 512 | bytes 4096
  144.3 0.7 fusion.20
  144.9 63.6 %all-reduce.4.cloned.1.call-done = f32[16,4096]{1,0:T(8,128)} async-done(((f32[16,4096]{1,0:T(8,128)}), f32[16,4096]{1,0:T(8,128)}) %all-reduce.4.cloned.1.call-update) | async-done | bytes 262160
  208.6 1.6 convert_bitcast_fusion
  210.2 40.3 %all-gather.1 = bf16[16,1,4096]{2,1,0:T(2,128)(2,1)S(1)} all-gather(bf16[1,1,4096]{2,1,0:T(2,128)(2,1)S(1)} %convert_bitcast_fusion), channel_id=1, replica_groups=mesh['page'=16,'head'=2] {'page'}, dimensions={0}, use_global_device_ids=true | all-gather | bytes 139264 | tf_op jit(solution)/shard_map/all_gather | solution.py:76
  250.5 3.4 %fusion.7 = f32[16,512]{1,0:T(8,128)} fusion(bf16[4096,512]{1,0:T(8,128)(2,1)} %param.14, bf16[16,1,4096]{2,1,0:T(2,128)(2,1)S(1)} %all-gather.1), kind=kOutput, calls=%fused_computation.13 | convolution fusion | flops 67108864 | bytes 4358144 | tf_op jit(solution)/shard_map/dot_general | solution.py:78
  254.0 3.5 %reduce-scatter.2.cloned.1.call-done = f32[8,512]{1,0:T(8,128)} async-done(((f32[16,512]{1,0:T(8,128)}), f32[8,512]{1,0:T(8,128)}) %reduce-scatter.2.cloned.1.call-update) | async-done | bytes 16400 | tf_op jit(solution)/shard_map/reduce_scatter | solution.py:77
  257.4 1.3 convert_element_type.23
  (23 shorter events, 1.0 us)
Async XLA Ops:
  6.5 91.2 %copy-start = (f32[8,4,8]{2,1,0:T(4,128)S(1)}, f32[8,4,8]{2,1,0:T(4,128)}, u32[]{:S(2)}) copy-start(f32[8,4,8]{2,1,0:T(4,128)} %param.13) | copy-start | bytes 3076
  6.5 202.0 %all-reduce.4.cloned.1.call-start = ((), (), s32[]{:S(2)}) async-start(), calls=%async_computation.2 | async-start | bytes 524288
  97.8 6.5 %copy-start.1 = (u32[32]{0:T(128)S(1)}, u32[32]{0:T(128)}, u32[]{:S(2)}) copy-start(u32[32]{0:T(128)} %constant.32) | copy-start | bytes 388
  103.8 153.6 %reduce-scatter.2.cloned.1.call-start = ((), (), s32[]{:S(2)}) async-start(), calls=%async_computation.1 | async-start | bytes 49152 | tf_op jit(solution)/shard_map/reduce_scatter | solution.py:77
Sparse Core Ops, SparseCore 0:
  103.9 104.5 all-reduce.3
  254.1 3.2 reduce-scatter.1
where the time goes:
time: 266 us
  blocking collectives  161 us (61%)
  waiting for transfers between devices  67.1 us (25%)
  matrix products  15.4 us (6%)
  between operations  13.5 us (5%)
  other arithmetic  5.61 us (2%)
  local copies, waits for them, and re-layouts  3.29 us (1%)
    unnamed x3, waiting for transfers between devices  63.7 us
    all_gather x1, blocking collectives, per_device(): every_query = lax.all_gather(query, 'page', axis=0, tiled=True)  44 us
    all_gather x1, blocking collectives, per_device(): attention_all = lax.all_gather(attention, 'page', axis=0, tiled=True)  40.3 us
    unnamed x1, blocking collectives  39.2 us
    pmax x1, blocking collectives, per_device(): highest = lax.pmax(local_top, 'page')  37.1 us
    dot_general x1, matrix products, per_device(): jnp.einsum('skgd,sktd->skgt', chosen, key_codes, preferred_element_type=j...  5.74 us
  transfers between devices with their start and end apart: 2, of which 2 were waited for; matrix products, arithmetic and copies ran while one was open for 1% of the time, Pallas kernels for 0%

commit v1 on v0

v1 whole, which is shorter than its diff:
```python
import functools

import jax
import jax.numpy as jnp
from jax import lax
from jax.experimental import pallas as pl
from jax.experimental.pallas import tpu as pltpu
from jax.sharding import PartitionSpec as P

LANES = 128
LOW = -1e30
MIB = 1 << 20
VMEM = pl.BlockSpec(memory_space=pltpu.VMEM)
SMEM = pl.BlockSpec(memory_space=pltpu.SMEM)


def exchange_rounds(devices):
    rounds, width = [], devices
    while width > 1:
        radix = 4 if width % 4 == 0 else 2
        width //= radix
        rounds.append([width * k for k in range(1, radix)])
    return rounds


def partner(value, mask, devices):
    return lax.ppermute(value, "page", [(i, i ^ mask) for i in range(devices)])


def stat_place(piece, entries):
    each = LANES // entries
    return piece // each, (piece % each) * entries


def stat_blocks(entries):
    return stat_place(2, entries)[0] + 1


def lane_index(shape):
    return lax.broadcasted_iota(jnp.int32, shape, 1)


def store_stats(out_ref, base, logs, entries, heads):
    high = logs.astype(jnp.bfloat16).astype(jnp.float32)
    middle = (logs - high).astype(jnp.bfloat16).astype(jnp.float32)
    low = logs - high - middle
    lane = lane_index((heads, LANES))
    blocks = [jnp.zeros((heads, LANES), jnp.float32) for _ in range(stat_blocks(entries))]
    for piece, value in enumerate((high, middle, low)):
        block, offset = stat_place(piece, entries)
        moved = pltpu.roll(value, offset, 1) if offset else value
        inside = (lane >= offset) & (lane < offset + entries)
        blocks[block] = jnp.where(inside, moved, blocks[block])
    table = jnp.concatenate(blocks, axis=0) if len(blocks) > 1 else blocks[0]
    out_ref[base : base + table.shape[0], :] = table.astype(jnp.bfloat16)


def load_stats(ref, base, entries, heads):
    rows = stat_blocks(entries) * heads
    table = ref[base : base + rows, :].astype(jnp.float32)
    total = None
    for piece in range(3):
        block, offset = stat_place(piece, entries)
        value = table[block * heads : (block + 1) * heads]
        value = pltpu.roll(value, LANES - offset, 1) if offset else value
        total = value if total is None else total + value
    return total


def load_entry(ref, index, heads):
    if heads % 16 == 0:
        return ref[index * heads : (index + 1) * heads, :].astype(jnp.float32)
    base = index * heads // 16 * 16
    block = ref[base : base + 16, :].astype(jnp.float32)
    return block[index * heads - base : (index + 1) * heads - base]


def attend_kernel(
    pieces, slots, kv_heads, group, tokens, pages, key_scaling,
    place_ref, live_ref, key_scale_ref, value_scale_ref, *refs,
):
    query_refs = refs[:pieces]
    key_ref, value_ref, out_ref, queries, outs = refs[pieces:]
    heads = kv_heads * group
    page_tokens = tokens // pages
    held = query_refs[0].shape[0]
    for piece, query_ref in enumerate(query_refs):
        block = query_ref[...].astype(jnp.float32)
        for head in range(heads):
            queries[pl.ds(piece * held * heads + head, held, stride=heads), :] = block[
                :, head * LANES : (head + 1) * LANES
            ]
    together = 2 if kv_heads % 2 == 0 else 1
    rows = together * group
    lane = lane_index((heads, LANES))
    logs = jnp.zeros((heads, LANES), jnp.float32)
    for slot in range(slots):
        start = pl.multiple_of(place_ref[slot] * heads, 8)
        query = queries[pl.ds(start, heads), :].astype(jnp.bfloat16)
        live = live_ref[slot]
        column = []
        for first in range(0, kv_heads, together):
            own = query[first * group : first * group + rows]
            if together == 2:
                upper = lax.broadcasted_iota(jnp.int32, (rows, LANES), 0) < group
                zero = jnp.zeros_like(own)
                own = jnp.concatenate(
                    [jnp.where(upper, own, zero), jnp.where(upper, zero, own)], axis=1
                )
                keys = jnp.concatenate([key_ref[slot, first], key_ref[slot, first + 1]], axis=1)
                values = jnp.concatenate(
                    [value_ref[slot, first], value_ref[slot, first + 1]], axis=1
                )
            else:
                keys, values = key_ref[slot, first], value_ref[slot, first]
            dotted = lax.dot_general(
                own, keys, (((1,), (1,)), ((), ())), preferred_element_type=jnp.float32
            )

            def by_page(scale_ref, page):
                parts = [
                    jnp.full((group, page_tokens), scale_ref[slot, first + k, page], jnp.float32)
                    for k in range(together)
                ]
                return jnp.concatenate(parts, axis=0) if together > 1 else parts[0]

            token = lane_index((rows, page_tokens))
            scores = []
            for page in range(pages):
                part = dotted[:, page * page_tokens : (page + 1) * page_tokens]
                part = part * (by_page(key_scale_ref, page) * key_scaling)
                scores.append(jnp.where(token + page * page_tokens < live, part, LOW))
            peak = functools.reduce(jnp.maximum, scores)
            peak = jnp.max(peak, axis=1, keepdims=True)
            total = None
            weights = []
            for page in range(pages):
                expon = jnp.exp(scores[page] - peak)
                total = expon if total is None else total + expon
                weights.append((expon * by_page(value_scale_ref, page)).astype(jnp.bfloat16))
            total = jnp.sum(total, axis=1, keepdims=True)
            partial = jnp.dot(
                jnp.concatenate(weights, axis=1), values, preferred_element_type=jnp.float32
            )
            if together == 2:
                partial = jnp.concatenate(
                    [partial[:group, :LANES], partial[group:, LANES:]], axis=0
                )
            at = slot * heads + first * group
            outs[at : at + rows, :] = partial / total
            column.append(peak + jnp.log(total))
        column = jnp.concatenate(column, axis=0) if len(column) > 1 else column[0]
        logs = jnp.where(lane == slot, column, logs)
    out_ref[: slots * heads, :] = outs[...].astype(jnp.bfloat16)
    store_stats(out_ref, slots * heads, logs, slots, heads)


def merge_slots_kernel(groups, slots, rows, heads, owner_ref, owner_lane_ref, *refs):
    out_ref, sums = refs[groups:]
    lane = lane_index((heads, LANES))
    owner = jnp.broadcast_to(owner_lane_ref[...], (heads, LANES))
    logs = jnp.full((heads, LANES), LOW, jnp.float32)
    for index in range(groups):
        own = load_stats(refs[index], slots * heads, slots, heads)
        own = pltpu.roll(own, index * slots, 1) if index else own
        inside = (lane >= index * slots) & (lane < (index + 1) * slots)
        logs = jnp.where(inside, own, logs)
    tops = jnp.zeros((heads, LANES), jnp.float32)
    row_top = []
    for row in range(rows):
        top = jnp.max(jnp.where(owner == row, logs, LOW), axis=1, keepdims=True)
        tops = jnp.where(owner == row, top, tops)
        row_top.append(top)
    factor = jnp.exp(logs - tops)
    totals = jnp.ones((heads, LANES), jnp.float32)
    row_logs = jnp.full((heads, LANES), LOW, jnp.float32)
    for row in range(rows):
        total = jnp.sum(jnp.where(owner == row, factor, 0.0), axis=1, keepdims=True)
        totals = jnp.where(owner == row, total, totals)
        held = total > 0.0
        value = jnp.where(held, row_top[row] + jnp.log(jnp.where(held, total, 1.0)), LOW)
        row_logs = jnp.where(lane == row, value, row_logs)
    weight = factor / totals
    sums[...] = jnp.zeros_like(sums)
    for index in range(groups):
        for slot in range(slots):
            at = index * slots + slot
            start = pl.multiple_of(owner_ref[at] * heads, 8)
            block = pl.ds(start, heads)
            sums[block, :] += weight[:, at : at + 1] * load_entry(refs[index], slot, heads)
    out_ref[: rows * heads, :] = sums[...].astype(jnp.bfloat16)
    store_stats(out_ref, rows * heads, row_logs, rows, heads)


def merge_rows(refs, rows, heads, sums):
    logs = [load_stats(ref, rows * heads, rows, heads) for ref in refs]
    top = functools.reduce(jnp.maximum, logs)
    factors = [jnp.exp(log - top) for log in logs]
    total = functools.reduce(jnp.add, factors)
    weights = [factor / total for factor in factors]
    for row in range(rows):
        parts = [
            weight[:, row : row + 1] * load_entry(ref, row, heads)
            for weight, ref in zip(weights, refs)
        ]
        sums[row * heads : (row + 1) * heads, :] = functools.reduce(jnp.add, parts)
    return top + jnp.log(total)


def merge_rows_kernel(groups, rows, heads, *refs):
    out_ref, sums = refs[groups:]
    logs = merge_rows(refs[:groups], rows, heads, sums)
    out_ref[: rows * heads, :] = sums[...].astype(jnp.bfloat16)
    store_stats(out_ref, rows * heads, logs, rows, heads)


def project_kernel(groups, rows, heads, *refs):
    weight_ref, out_ref, sums = refs[groups:]
    merge_rows(refs[:groups], rows, heads, sums)
    attention = jnp.concatenate(
        [sums[pl.ds(head, rows, stride=heads), :].astype(jnp.bfloat16) for head in range(heads)],
        axis=1,
    )
    out_ref[...] = jnp.dot(attention, weight_ref[...], preferred_element_type=jnp.float32)


def per_device(
    query,
    key_codes,
    value_codes,
    key_scale,
    value_scale,
    out_weight,
    range_counts,
    last_fill,
    slot_table,
    *,
    devices,
    head_devices,
):
    slots, kv_heads, tokens, head_dim = key_codes.shape
    pages = key_scale.shape[2]
    rows = range_counts.shape[0]
    all_slots = slot_table.shape[0]
    heads = query.shape[1] // head_dim
    group = heads // kv_heads
    own_rows = query.shape[0]
    columns = out_weight.shape[1]
    rounds = exchange_rounds(devices)
    me = lax.axis_index("page")

    inclusive = jnp.cumsum(range_counts)
    lengths = (range_counts - 1) * tokens + last_fill
    slot_ids = jnp.arange(all_slots, dtype=jnp.int32)
    inverse = jnp.sum(
        jnp.where(slot_table[None, :] == slot_ids[:, None], slot_ids[None, :], 0), axis=1
    )
    slot_row = jnp.sum((inverse[:, None] >= inclusive[None, :]).astype(jnp.int32), axis=1)
    picked = slot_row[:, None] == jnp.arange(rows, dtype=jnp.int32)[None, :]
    slot_end = jnp.sum(
        jnp.where(picked, (lengths + (inclusive - range_counts) * tokens)[None, :], 0), axis=1
    )
    slot_live = slot_end - inverse * tokens

    order = [0]
    held = [query]
    for masks in rounds:
        block = jnp.concatenate(held, axis=0) if len(held) > 1 else held[0]
        held = [block] + [partner(block, mask, devices) for mask in masks]
        order = [mask ^ old for mask in [0] + masks for old in order]
    place_of = [0] * devices
    for place, mask in enumerate(order):
        place_of[mask] = place
    own_slots = lax.dynamic_slice(slot_row, (me * slots,), (slots,))
    own_live = lax.dynamic_slice(slot_live, (me * slots,), (slots,))
    away = jnp.bitwise_xor(own_slots // own_rows, me)
    place = jnp.sum(
        jnp.where(
            away[:, None] == jnp.arange(devices, dtype=jnp.int32)[None, :],
            jnp.array(place_of, jnp.int32)[None, :],
            0,
        ),
        axis=1,
    )
    place = place * own_rows + own_slots % own_rows

    payload = (slots + stat_blocks(slots)) * heads
    held = [
        pl.pallas_call(
            functools.partial(
                attend_kernel, len(held), slots, kv_heads, group, tokens, pages, head_dim**-0.5
            ),
            out_shape=jax.ShapeDtypeStruct((payload, LANES), jnp.bfloat16),
            in_specs=[SMEM] * 4 + [VMEM] * (len(held) + 2),
            out_specs=VMEM,
            scratch_shapes=[
                pltpu.VMEM((rows * heads, LANES), jnp.float32),
                pltpu.VMEM((slots * heads, LANES), jnp.float32),
            ],
            compiler_params=pltpu.CompilerParams(vmem_limit_bytes=24 * MIB),
            name="attend",
        )(place, own_live, key_scale, value_scale, *held, key_codes, value_codes)
    ]

    payload = (rows + stat_blocks(rows)) * heads
    sums = pltpu.VMEM((rows * heads, LANES), jnp.float32)
    for turn, masks in enumerate(rounds):
        held = held + [partner(held[0], mask, devices) for mask in masks]
        groups = len(held)
        params = pltpu.CompilerParams(vmem_limit_bytes=16 * MIB)
        if turn == 0:
            sources = [me] + [jnp.bitwise_xor(me, mask) for mask in masks]
            owner = jnp.concatenate(
                [lax.dynamic_slice(slot_row, (source * slots,), (slots,)) for source in sources]
            )
            owner_lane = jnp.full((1, LANES), -1, jnp.int32).at[0, : groups * slots].set(owner)
            held = [
                pl.pallas_call(
                    functools.partial(merge_slots_kernel, groups, slots, rows, heads),
                    out_shape=jax.ShapeDtypeStruct((payload, LANES), jnp.bfloat16),
                    in_specs=[SMEM] + [VMEM] * (groups + 1),
                    out_specs=VMEM,
                    scratch_shapes=[sums],
                    compiler_params=params,
                    name="merge_slots",
                )(owner, owner_lane, *held)
            ]
        elif turn < len(rounds) - 1:
            held = [
                pl.pallas_call(
                    functools.partial(merge_rows_kernel, groups, rows, heads),
                    out_shape=jax.ShapeDtypeStruct((payload, LANES), jnp.bfloat16),
                    in_specs=[VMEM] * groups,
                    out_specs=VMEM,
                    scratch_shapes=[sums],
                    compiler_params=params,
                    name="merge_rows",
                )(*held)
            ]
    mixed = pl.pallas_call(
        functools.partial(project_kernel, len(held), rows, heads),
        out_shape=jax.ShapeDtypeStruct((rows, columns), jnp.float32),
        in_specs=[VMEM] * (len(held) + 1),
        out_specs=VMEM,
        scratch_shapes=[sums],
        compiler_params=pltpu.CompilerParams(vmem_limit_bytes=16 * MIB),
        name="project",
    )(*held, out_weight)
    if head_devices == 2:
        half = rows // 2
        side = lax.axis_index("head")
        keep = lax.dynamic_slice(mixed, (side * half, 0), (half, columns))
        give = lax.dynamic_slice(mixed, ((1 - side) * half, 0), (half, columns))
        mixed = keep + lax.ppermute(give, "head", [(0, 1), (1, 0)])
    else:
        mixed = lax.psum_scatter(mixed, "head", scatter_dimension=0, tiled=True)
    return mixed.astype(jnp.bfloat16)


def solution(mesh):
    return jax.shard_map(
        functools.partial(
            per_device, devices=mesh.shape["page"], head_devices=mesh.shape["head"]
        ),
        mesh=mesh,
        in_specs=(
            P("page", "head"),
            P("page", "head", None, None),
            P("page", "head", None, None),
            P("page", "head", None),
            P("page", "head", None),
            P("head", "page"),
            P(),
            P(),
            P(),
        ),
        out_specs=P("head", "page"),
        check_vma=False,
    )
```

time: 266 us -> 59.7 us (0.22)
  blocking collectives: 161 us -> 0 us
  waiting for transfers between devices: 67.1 us -> 15.3 us
  starting transfers between devices: 0.04 us -> 17.1 us
  matrix products: 15.4 us -> 0 us
  between operations: 13.5 us -> 0.06 us
  Pallas kernels: 0 us -> 9.92 us
  local copies, waits for them, and re-layouts: 3.29 us -> 11.2 us
    all_gather x2 -> x0, blocking collectives: 84.3 us -> none  [the longest x1 44 us: per_device(): every_query = lax.all_gather(query, 'page', axis=0, tiled=True)]
    unnamed x3 -> x0, waiting for transfers between devices: 63.7 us -> none
    unnamed x1 -> x0, blocking collectives: 39.2 us -> none
    pmax x1 -> x0, blocking collectives: 37.1 us -> none  [per_device(): highest = lax.pmax(local_top, 'page')]
    ppermute x0 -> x13, starting transfers between devices: none -> 17.1 us  [the longest x12 17.1 us: partner(): return lax.ppermute(value, 'page', [(i, i ^ mask) for i in range(devices)])]
    dot_general x6 -> x0, matrix products: 15.4 us -> none  [the longest x1 5.74 us: per_device(): jnp.einsum('skgd,sktd->skgt', chosen, key_codes, preferred_element_type=j...]
    ppermute x0 -> x13, waiting for transfers between devices: none -> 15.3 us  [the longest x12 14.1 us: partner(): return lax.ppermute(value, 'page', [(i, i ^ mask) for i in range(devices)])]
    pallas_call x0 -> x3, Pallas kernels: none -> 9.92 us  [the longest x1 7.53 us: per_device(): pl.pallas_call(functools.partial(attend_kernel, len(held), slots, kv_head...]
  transfers between devices with their start and end apart: 2 -> 13, of which waited for: 2 -> 9; matrix products, arithmetic and copies ran while one was open for 1% -> 8% of each run, Pallas kernels for 0% -> 0%
where the time goes in v1:
time: 59.7 us; the launch traced here: 59.2 us
  starting transfers between devices  17.1 us (29%)
  waiting for transfers between devices  15.3 us (26%)
  local copies, waits for them, and re-layouts  11.2 us (19%)
  Pallas kernels  9.92 us (17%)
  other arithmetic  5.55 us (9%)
    ppermute x12, starting transfers between devices, partner(): return lax.ppermute(value, 'page', [(i, i ^ mask) for i in range(devices)])  17.1 us
    ppermute x12, waiting for transfers between devices, partner(): return lax.ppermute(value, 'page', [(i, i ^ mask) for i in range(devices)])  14.1 us
    unnamed x10, local copies, waits for them, and re-layouts  10.4 us
    pallas_call x1, Pallas kernels, per_device(): pl.pallas_call(functools.partial(attend_kernel, len(held), slots, kv_head...  7.53 us
    another operation x4, other arithmetic  1.52 us
    pallas_call x1, Pallas kernels, per_device(): pl.pallas_call(functools.partial(merge_slots_kernel, groups, slots, rows,...  1.27 us
  transfers between devices with their start and end apart: 13, of which 9 were waited for; matrix products, arithmetic and copies ran while one was open for 8% of the time, Pallas kernels for 0%

profile of v1, /device:TPU:0, one launch (start us, length us, event | category | flops | bytes accessed | tf_op | source)
XLA Modules:
  0.0 59.2 jit_solution(10974292952992384727)
XLA Ops:
  0.0 3.0 %collective-permute-start = (bf16[1,4096]{1,0:T(2,128)(2,1)}, bf16[1,4096]{1,0:T(2,128)(2,1)S(1)}, u32[]{:S(2)}, u32[]{:S(2)}) collective-permute-start(bf16[1,4096]{1,0:T(2,128)(2,1)} %param.12), channel_id=1, source_target_pairs={{0,8},{2,10},{4,12},{6,14},{8,0},{10,2},{12,4},{14,6},{16,24},{18,... | collective-permute-start | bytes 24584 | tf_op jit(solution)/shard_map/ppermute | solution.py:27
  3.0 2.6 %collective-permute-start.1 = (bf16[1,4096]{1,0:T(2,128)(2,1)}, bf16[1,4096]{1,0:T(2,128)(2,1)S(1)}, u32[]{:S(2)}, u32[]{:S(2)}) collective-permute-start(bf16[1,4096]{1,0:T(2,128)(2,1)} %param.12), channel_id=1, source_target_pairs={{0,16},{2,18},{4,20},{6,22},{8,24},{10,26},{12,28},{14,30},{16,0},... | collective-permute-start | bytes 24584 | tf_op jit(solution)/shard_map/ppermute | solution.py:27
  8.2 0.8 %select_reduce_fusion.2.place_ref = s32[8]{0:T(128)S(1)} fusion(s32[16]{0:T(128)} %constant.83.clone, s32[8]{0:T(128)S(1)} %get-tuple-element.17), kind=kLoop, calls=%fused_computation.7 | loop fusion | flops 376 | bytes 128 | tf_op jit(solution)/shard_map/reduce_sum | solution.py:277
  9.7 1.6 %collective-permute-done.2 = bf16[1,4096]{1,0:T(2,128)(2,1)S(1)} collective-permute-done((bf16[1,4096]{1,0:T(2,128)(2,1)}, bf16[1,4096]{1,0:T(2,128)(2,1)S(1)}, u32[]{:S(2)}, u32[]{:S(2)}) %collective-permute-start.2) | collective-permute-done | bytes 8224 | tf_op jit(solution)/shard_map/ppermute | solution.py:27
  12.2 1.6 %collective-permute-start.3 = (bf16[4,4096]{1,0:T(4,128)(2,1)S(1)}, bf16[4,4096]{1,0:T(4,128)(2,1)S(1)}, u32[]{:S(2)}, u32[]{:S(2)}) collective-permute-start(bf16[4,4096]{1,0:T(4,128)(2,1)S(1)} %pad_maximum_fusion.refs_0_), channel_id=1, source_target_pairs={{0,2},{2,0},{4,6},{6,4},{8,10},{10,8},{12,14},{14,12},{16,18},{18,... | collective-permute-start | bytes 98312 | tf_op jit(solution)/shard_map/ppermute | solution.py:27
  13.7 1.5 %collective-permute-start.4 = (bf16[4,4096]{1,0:T(4,128)(2,1)S(1)}, bf16[4,4096]{1,0:T(4,128)(2,1)S(1)}, u32[]{:S(2)}, u32[]{:S(2)}) collective-permute-start(bf16[4,4096]{1,0:T(4,128)(2,1)S(1)} %pad_maximum_fusion.refs_0_), channel_id=1, source_target_pairs={{0,4},{2,6},{4,0},{6,2},{8,12},{10,14},{12,8},{14,10},{16,20},{18,... | collective-permute-start | bytes 98312 | tf_op jit(solution)/shard_map/ppermute | solution.py:27
  16.5 1.1 %collective-permute-done.4.refs_2_ = bf16[4,4096]{1,0:T(4,128)(2,1)S(1)} collective-permute-done((bf16[4,4096]{1,0:T(4,128)(2,1)S(1)}, bf16[4,4096]{1,0:T(4,128)(2,1)S(1)}, u32[]{:S(2)}, u32[]{:S(2)}) %collective-permute-start.4) | collective-permute-done | bytes 32800 | tf_op jit(solution)/shard_map/ppermute | solution.py:27
  17.6 2.4 %collective-permute-done.5.refs_3_ = bf16[4,4096]{1,0:T(4,128)(2,1)S(1)} collective-permute-done((bf16[4,4096]{1,0:T(4,128)(2,1)S(1)}, bf16[4,4096]{1,0:T(4,128)(2,1)S(1)}, u32[]{:S(2)}, u32[]{:S(2)}) %collective-permute-start.5) | collective-permute-done | bytes 32800 | tf_op jit(solution)/shard_map/ppermute | solution.py:27
  20.1 3.4 %copy-done = bf16[8,4,1024,128]{3,2,1,0:T(8,128)(2,1)S(1)} copy-done((bf16[8,4,1024,128]{3,2,1,0:T(8,128)(2,1)S(1)}, bf16[8,4,1024,128]{3,2,1,0:T(8,128)(2,1)}, u32[]{:S(2)}) %copy-start) | copy-done | bytes 8388632
  23.4 3.4 %copy-done.1 = bf16[8,4,1024,128]{3,2,1,0:T(8,128)(2,1)S(1)} copy-done((bf16[8,4,1024,128]{3,2,1,0:T(8,128)(2,1)S(1)}, bf16[8,4,1024,128]{3,2,1,0:T(8,128)(2,1)}, u32[]{:S(2)}) %copy-start.1) | copy-done | bytes 8388632
  28.3 7.5 %attend.1.refs_0_ = bf16[288,128]{1,0:T(8,128)(2,1)S(1)} custom-call(s32[8]{0:T(128)S(1)} %select_reduce_fusion.2.place_ref, s32[8]{0:T(128)S(1)} %dynamic_slice.26.live_ref, f32[8,4,8]{2,1,0:T(4,128)S(1)} %copy-done.3, f32[8,4,8]{2,1,0:T(4,128)S(1)} %copy-done.4, bf16[4,4096]{1,0:T(4,128)(2,1)S(1)} %pad_maximum_fusion.refs_0_, ...), custom_call_target="tpu_custom_call" | custom-call | tf_op jit(solution)/shard_map/attend/pallas_call | solution.py:289
  35.8 2.7 %collective-permute-start.7 = (bf16[288,128]{1,0:T(8,128)(2,1)S(1)}, bf16[288,128]{1,0:T(8,128)(2,1)S(1)}, u32[]{:S(2)}, u32[]{:S(2)}) collective-permute-start(bf16[288,128]{1,0:T(8,128)(2,1)S(1)} %attend.1.refs_0_), channel_id=1, source_target_pairs={{0,16},{2,18},{4,20},{6,22},{8,24},{10,26},{12,28},{14,30},{16,0},... | collective-permute-start | bytes 221192 | tf_op jit(solution)/shard_map/ppermute | solution.py:27
  38.6 1.6 %collective-permute-start.8 = (bf16[288,128]{1,0:T(8,128)(2,1)S(1)}, bf16[288,128]{1,0:T(8,128)(2,1)S(1)}, u32[]{:S(2)}, u32[]{:S(2)}) collective-permute-start(bf16[288,128]{1,0:T(8,128)(2,1)S(1)} %attend.1.refs_0_), channel_id=1, source_target_pairs={{0,24},{2,26},{4,28},{6,30},{8,16},{10,18},{12,20},{14,22},{16,8},... | collective-permute-start | bytes 221192 | tf_op jit(solution)/shard_map/ppermute | solution.py:27
  40.3 1.5 %collective-permute-done.6.refs_1_ = bf16[288,128]{1,0:T(8,128)(2,1)S(1)} collective-permute-done((bf16[288,128]{1,0:T(8,128)(2,1)S(1)}, bf16[288,128]{1,0:T(8,128)(2,1)S(1)}, u32[]{:S(2)}, u32[]{:S(2)}) %collective-permute-start.6) | collective-permute-done | bytes 73760 | tf_op jit(solution)/shard_map/ppermute | solution.py:27
  41.8 3.0 %collective-permute-done.8.refs_3_ = bf16[288,128]{1,0:T(8,128)(2,1)S(1)} collective-permute-done((bf16[288,128]{1,0:T(8,128)(2,1)S(1)}, bf16[288,128]{1,0:T(8,128)(2,1)S(1)}, u32[]{:S(2)}, u32[]{:S(2)}) %collective-permute-start.8) | collective-permute-done | bytes 73760 | tf_op jit(solution)/shard_map/ppermute | solution.py:27
  44.7 1.3 %merge_slots.1.refs_0_ = bf16[544,128]{1,0:T(8,128)(2,1)S(1)} custom-call(s32[32]{0:T(128)S(1)} %pad_add_fusion.owner_ref, s32[1,128]{1,0:T(1,128)S(1)} %scatter.4.owner_lane_ref, bf16[288,128]{1,0:T(8,128)(2,1)S(1)} %attend.1.refs_0_, bf16[288,128]{1,0:T(8,128)(2,1)S(1)} %collective-permute-done.6.refs_1_, ...), custom_call_target="tpu_custom_call" | custom-call | tf_op jit(solution)/shard_map/merge_slots/pallas_call | solution.py:318
  46.6 1.5 %collective-permute-start.11 = (bf16[544,128]{1,0:T(8,128)(2,1)S(1)}, bf16[544,128]{1,0:T(8,128)(2,1)S(1)}, u32[]{:S(2)}, u32[]{:S(2)}) collective-permute-start(bf16[544,128]{1,0:T(8,128)(2,1)S(1)} %merge_slots.1.refs_0_), channel_id=1, source_target_pairs={{0,6},{2,4},{4,2},{6,0},{8,14},{10,12},{12,10},{14,8},{16,22},{18,... | collective-permute-start | bytes 417800 | tf_op jit(solution)/shard_map/ppermute | solution.py:27
  48.1 1.5 %collective-permute-start.9 = (bf16[544,128]{1,0:T(8,128)(2,1)S(1)}, bf16[544,128]{1,0:T(8,128)(2,1)S(1)}, u32[]{:S(2)}, u32[]{:S(2)}) collective-permute-start(bf16[544,128]{1,0:T(8,128)(2,1)S(1)} %merge_slots.1.refs_0_), channel_id=1, source_target_pairs={{0,2},{2,0},{4,6},{6,4},{8,10},{10,8},{12,14},{14,12},{16,18},{18,... | collective-permute-start | bytes 417800 | tf_op jit(solution)/shard_map/ppermute | solution.py:27
  49.6 1.6 %collective-permute-done.10.refs_2_ = bf16[544,128]{1,0:T(8,128)(2,1)S(1)} collective-permute-done((bf16[544,128]{1,0:T(8,128)(2,1)S(1)}, bf16[544,128]{1,0:T(8,128)(2,1)S(1)}, u32[]{:S(2)}, u32[]{:S(2)}) %collective-permute-start.10) | collective-permute-done | bytes 139296 | tf_op jit(solution)/shard_map/ppermute | solution.py:27
  51.1 1.5 %collective-permute-done.11.refs_3_ = bf16[544,128]{1,0:T(8,128)(2,1)S(1)} collective-permute-done((bf16[544,128]{1,0:T(8,128)(2,1)S(1)}, bf16[544,128]{1,0:T(8,128)(2,1)S(1)}, u32[]{:S(2)}, u32[]{:S(2)}) %collective-permute-start.11) | collective-permute-done | bytes 139296 | tf_op jit(solution)/shard_map/ppermute | solution.py:27
  52.6 1.5 %collective-permute-done.9.refs_1_ = bf16[544,128]{1,0:T(8,128)(2,1)S(1)} collective-permute-done((bf16[544,128]{1,0:T(8,128)(2,1)S(1)}, bf16[544,128]{1,0:T(8,128)(2,1)S(1)}, u32[]{:S(2)}, u32[]{:S(2)}) %collective-permute-start.9) | collective-permute-done | bytes 139296 | tf_op jit(solution)/shard_map/ppermute | solution.py:27
  54.1 2.2 %copy-done.2 = bf16[4096,512]{1,0:T(8,128)(2,1)S(1)} copy-done((bf16[4096,512]{1,0:T(8,128)(2,1)S(1)}, bf16[4096,512]{1,0:T(8,128)(2,1)}, u32[]{:S(2)}) %copy-start.2) | copy-done | bytes 4194328
  56.3 1.1 %project.1 = f32[16,512]{1,0:T(8,128)S(1)} custom-call(bf16[544,128]{1,0:T(8,128)(2,1)S(1)} %merge_slots.1.refs_0_, bf16[544,128]{1,0:T(8,128)(2,1)S(1)} %collective-permute-done.9.refs_1_, bf16[544,128]{1,0:T(8,128)(2,1)S(1)} %collective-permute-done.10.refs_2_, bf16[544,128]{1,0:T(8,128)(2,1)S(1)} %collective-permute-done.11.refs_3_, ...), custom_call_target="tpu_custom_call" | custom-call | tf_op jit(solution)/shard_map/project/pallas_call | solution.py:340
  57.4 1.2 %collective-permute-done.12 = f32[8,512]{1,0:T(8,128)S(1)} collective-permute-done((f32[8,512]{1,0:T(8,128)S(1)}, f32[8,512]{1,0:T(8,128)S(1)}, u32[]{:S(2)}, u32[]{:S(2)}) %collective-permute-start.12) | collective-permute-done | bytes 16416 | tf_op jit(solution)/shard_map/ppermute | solution.py:354
  (33 shorter events, 8.1 us)
Async XLA Ops:
  0.0 9.7 %collective-permute-start = (bf16[1,4096]{1,0:T(2,128)(2,1)}, bf16[1,4096]{1,0:T(2,128)(2,1)S(1)}, u32[]{:S(2)}, u32[]{:S(2)}) collective-permute-start(bf16[1,4096]{1,0:T(2,128)(2,1)} %param.12), channel_id=1, source_target_pairs={{0,8},{2,10},{4,12},{6,14},{8,0},{10,2},{12,4},{14,6},{16,24},{18,... | collective-permute-start | bytes 24584 | tf_op jit(solution)/shard_map/ppermute | solution.py:27
  3.0 6.7 %collective-permute-start.1 = (bf16[1,4096]{1,0:T(2,128)(2,1)}, bf16[1,4096]{1,0:T(2,128)(2,1)S(1)}, u32[]{:S(2)}, u32[]{:S(2)}) collective-permute-start(bf16[1,4096]{1,0:T(2,128)(2,1)} %param.12), channel_id=1, source_target_pairs={{0,16},{2,18},{4,20},{6,22},{8,24},{10,26},{12,28},{14,30},{16,0},... | collective-permute-start | bytes 24584 | tf_op jit(solution)/shard_map/ppermute | solution.py:27
  5.6 5.7 %collective-permute-start.2 = (bf16[1,4096]{1,0:T(2,128)(2,1)}, bf16[1,4096]{1,0:T(2,128)(2,1)S(1)}, u32[]{:S(2)}, u32[]{:S(2)}) collective-permute-start(bf16[1,4096]{1,0:T(2,128)(2,1)} %param.12), channel_id=1, source_target_pairs={{0,24},{2,26},{4,28},{6,30},{8,16},{10,18},{12,20},{14,22},{16,8},... | collective-permute-start | bytes 24584 | tf_op jit(solution)/shard_map/ppermute | solution.py:27
  12.2 4.4 %collective-permute-start.3 = (bf16[4,4096]{1,0:T(4,128)(2,1)S(1)}, bf16[4,4096]{1,0:T(4,128)(2,1)S(1)}, u32[]{:S(2)}, u32[]{:S(2)}) collective-permute-start(bf16[4,4096]{1,0:T(4,128)(2,1)S(1)} %pad_maximum_fusion.refs_0_), channel_id=1, source_target_pairs={{0,2},{2,0},{4,6},{6,4},{8,10},{10,8},{12,14},{14,12},{16,18},{18,... | collective-permute-start | bytes 98312 | tf_op jit(solution)/shard_map/ppermute | solution.py:27
  13.7 3.9 %collective-permute-start.4 = (bf16[4,4096]{1,0:T(4,128)(2,1)S(1)}, bf16[4,4096]{1,0:T(4,128)(2,1)S(1)}, u32[]{:S(2)}, u32[]{:S(2)}) collective-permute-start(bf16[4,4096]{1,0:T(4,128)(2,1)S(1)} %pad_maximum_fusion.refs_0_), channel_id=1, source_target_pairs={{0,4},{2,6},{4,0},{6,2},{8,12},{10,14},{12,8},{14,10},{16,20},{18,... | collective-permute-start | bytes 98312 | tf_op jit(solution)/shard_map/ppermute | solution.py:27
  15.2 4.8 %collective-permute-start.5 = (bf16[4,4096]{1,0:T(4,128)(2,1)S(1)}, bf16[4,4096]{1,0:T(4,128)(2,1)S(1)}, u32[]{:S(2)}, u32[]{:S(2)}) collective-permute-start(bf16[4,4096]{1,0:T(4,128)(2,1)S(1)} %pad_maximum_fusion.refs_0_), channel_id=1, source_target_pairs={{0,6},{2,4},{4,2},{6,0},{8,14},{10,12},{12,10},{14,8},{16,22},{18,... | collective-permute-start | bytes 98312 | tf_op jit(solution)/shard_map/ppermute | solution.py:27
  20.1 3.4 %copy-start = (bf16[8,4,1024,128]{3,2,1,0:T(8,128)(2,1)S(1)}, bf16[8,4,1024,128]{3,2,1,0:T(8,128)(2,1)}, u32[]{:S(2)}) copy-start(bf16[8,4,1024,128]{3,2,1,0:T(8,128)(2,1)} %refs_4_.2) | copy-start | bytes 25165828
  23.4 3.4 %copy-start.1 = (bf16[8,4,1024,128]{3,2,1,0:T(8,128)(2,1)S(1)}, bf16[8,4,1024,128]{3,2,1,0:T(8,128)(2,1)}, u32[]{:S(2)}) copy-start(bf16[8,4,1024,128]{3,2,1,0:T(8,128)(2,1)} %refs_5_.1) | copy-start | bytes 25165828
  26.8 0.7 %copy-start.3 = (f32[8,4,8]{2,1,0:T(4,128)S(1)}, f32[8,4,8]{2,1,0:T(4,128)}, u32[]{:S(2)}) copy-start(f32[8,4,8]{2,1,0:T(4,128)} %key_scale_ref.1) | copy-start | bytes 3076
  27.5 0.7 %copy-start.4 = (f32[8,4,8]{2,1,0:T(4,128)S(1)}, f32[8,4,8]{2,1,0:T(4,128)}, u32[]{:S(2)}) copy-start(f32[8,4,8]{2,1,0:T(4,128)} %value_scale_ref.1) | copy-start | bytes 3076
  35.8 6.0 %collective-permute-start.6 = (bf16[288,128]{1,0:T(8,128)(2,1)S(1)}, bf16[288,128]{1,0:T(8,128)(2,1)S(1)}, u32[]{:S(2)}, u32[]{:S(2)}) collective-permute-start(bf16[288,128]{1,0:T(8,128)(2,1)S(1)} %attend.1.refs_0_), channel_id=1, source_target_pairs={{0,8},{2,10},{4,12},{6,14},{8,0},{10,2},{12,4},{14,6},{16,24},{18,... | collective-permute-start | bytes 221192 | tf_op jit(solution)/shard_map/ppermute | solution.py:27
  35.8 5.9 %collective-permute-start.7 = (bf16[288,128]{1,0:T(8,128)(2,1)S(1)}, bf16[288,128]{1,0:T(8,128)(2,1)S(1)}, u32[]{:S(2)}, u32[]{:S(2)}) collective-permute-start(bf16[288,128]{1,0:T(8,128)(2,1)S(1)} %attend.1.refs_0_), channel_id=1, source_target_pairs={{0,16},{2,18},{4,20},{6,22},{8,24},{10,26},{12,28},{14,30},{16,0},... | collective-permute-start | bytes 221192 | tf_op jit(solution)/shard_map/ppermute | solution.py:27
  38.6 6.2 %collective-permute-start.8 = (bf16[288,128]{1,0:T(8,128)(2,1)S(1)}, bf16[288,128]{1,0:T(8,128)(2,1)S(1)}, u32[]{:S(2)}, u32[]{:S(2)}) collective-permute-start(bf16[288,128]{1,0:T(8,128)(2,1)S(1)} %attend.1.refs_0_), channel_id=1, source_target_pairs={{0,24},{2,26},{4,28},{6,30},{8,16},{10,18},{12,20},{14,22},{16,8},... | collective-permute-start | bytes 221192 | tf_op jit(solution)/shard_map/ppermute | solution.py:27
  46.0 5.1 %collective-permute-start.10 = (bf16[544,128]{1,0:T(8,128)(2,1)S(1)}, bf16[544,128]{1,0:T(8,128)(2,1)S(1)}, u32[]{:S(2)}, u32[]{:S(2)}) collective-permute-start(bf16[544,128]{1,0:T(8,128)(2,1)S(1)} %merge_slots.1.refs_0_), channel_id=1, source_target_pairs={{0,4},{2,6},{4,0},{6,2},{8,12},{10,14},{12,8},{14,10},{16,20},{18,... | collective-permute-start | bytes 417800 | tf_op jit(solution)/shard_map/ppermute | solution.py:27
  46.6 6.0 %collective-permute-start.11 = (bf16[544,128]{1,0:T(8,128)(2,1)S(1)}, bf16[544,128]{1,0:T(8,128)(2,1)S(1)}, u32[]{:S(2)}, u32[]{:S(2)}) collective-permute-start(bf16[544,128]{1,0:T(8,128)(2,1)S(1)} %merge_slots.1.refs_0_), channel_id=1, source_target_pairs={{0,6},{2,4},{4,2},{6,0},{8,14},{10,12},{12,10},{14,8},{16,22},{18,... | collective-permute-start | bytes 417800 | tf_op jit(solution)/shard_map/ppermute | solution.py:27
  48.1 6.0 %collective-permute-start.9 = (bf16[544,128]{1,0:T(8,128)(2,1)S(1)}, bf16[544,128]{1,0:T(8,128)(2,1)S(1)}, u32[]{:S(2)}, u32[]{:S(2)}) collective-permute-start(bf16[544,128]{1,0:T(8,128)(2,1)S(1)} %merge_slots.1.refs_0_), channel_id=1, source_target_pairs={{0,2},{2,0},{4,6},{6,4},{8,10},{10,8},{12,14},{14,12},{16,18},{18,... | collective-permute-start | bytes 417800 | tf_op jit(solution)/shard_map/ppermute | solution.py:27
  54.1 2.2 %copy-start.2 = (bf16[4096,512]{1,0:T(8,128)(2,1)S(1)}, bf16[4096,512]{1,0:T(8,128)(2,1)}, u32[]{:S(2)}) copy-start(bf16[4096,512]{1,0:T(8,128)(2,1)} %refs_4_.3) | copy-start | bytes 12582916
  57.4 1.2 %collective-permute-start.12 = (f32[8,512]{1,0:T(8,128)S(1)}, f32[8,512]{1,0:T(8,128)S(1)}, u32[]{:S(2)}, u32[]{:S(2)}) collective-permute-start(f32[8,512]{1,0:T(8,128)S(1)} %constant_dynamic-slice_fusion), channel_id=1, source_target_pairs={{0,1},{1,0},{2,3},{3,2},{4,5},{5,4},{6,7},{7,6},{8,9},{9,8},{10,11... | collective-permute-start | bytes 49160 | tf_op jit(solution)/shard_map/ppermute | solution.py:354

commit v2 on v1

--- a/solution.py
+++ b/solution.py
@@ -9,15 +9,18 @@
 
 LANES = 128
 LOW = -1e30
+LOCATE_FLOPS = 20_000_000_000
+ATTEND_FLOPS = 5_000_000_000
+MERGE_FLOPS = 20_000_000_000
 MIB = 1 << 20
 VMEM = pl.BlockSpec(memory_space=pltpu.VMEM)
 SMEM = pl.BlockSpec(memory_space=pltpu.SMEM)
 
 
-def exchange_rounds(devices):
+def exchange_rounds(devices, most):
     rounds, width = [], devices
     while width > 1:
-        radix = 4 if width % 4 == 0 else 2
+        radix = most if width % most == 0 else 2
         width //= radix
         rounds.append([width * k for k in range(1, radix)])
     return rounds
@@ -73,6 +76,43 @@
     base = index * heads // 16 * 16
     block = ref[base : base + 16, :].astype(jnp.float32)
     return block[index * heads - base : (index + 1) * heads - base]
+
+
+def locate_kernel(
+    rounds, near, slots, rows, all_slots, own_rows, tokens,
+    table_ref, place_ref, live_ref, owner_ref, position_of, first_of,
+):
+    me = lax.axis_index("page")
+    fills, entries = rows, 2 * rows
+
+    def note(position, carry):
+        position_of[table_ref[entries + position]] = position
+        return carry
+
+    lax.fori_loop(0, all_slots, note, 0, unroll=16)
+    ends, end = [], jnp.int32(0)
+    for row in range(rows):
+        first_of[row] = end
+        end = end + table_ref[row]
+        ends.append(end)
+    for index, mask in enumerate(near):
+        source = jnp.bitwise_xor(me, mask)
+        for slot in range(slots):
+            position = position_of[source * slots + slot]
+            row = functools.reduce(
+                jnp.add, [(position >= end).astype(jnp.int32) for end in ends[:-1]]
+            )
+            owner_ref[index * slots + slot] = row
+            if index == 0:
+                away = jnp.bitwise_xor(row // own_rows, me)
+                place, step_size = row % own_rows, own_rows
+                for masks in rounds:
+                    radix = len(masks) + 1
+                    place += away // masks[0] % radix * step_size
+                    step_size *= radix
+                place_ref[slot] = place
+                before = position - first_of[row]
+                live_ref[slot] = (table_ref[row] - 1 - before) * tokens + table_ref[fills + row]
 
 
 def attend_kernel(
@@ -155,10 +195,13 @@
     store_stats(out_ref, slots * heads, logs, slots, heads)
 
 
-def merge_slots_kernel(groups, slots, rows, heads, owner_ref, owner_lane_ref, *refs):
+def merge_slots_kernel(groups, slots, rows, heads, owner_ref, *refs):
     out_ref, sums = refs[groups:]
     lane = lane_index((heads, LANES))
-    owner = jnp.broadcast_to(owner_lane_ref[...], (heads, LANES))
+    owner = jnp.full((8, LANES), -1, jnp.int32)
+    for at in range(groups * slots):
+        owner = jnp.where(lane[:8] == at, owner_ref[at], owner)
+    owner = jnp.concatenate([owner] * (heads // 8), axis=0)
     logs = jnp.full((heads, LANES), LOW, jnp.float32)
     for index in range(groups):
         own = load_stats(refs[index], slots * heads, slots, heads)
@@ -214,14 +257,21 @@
     store_stats(out_ref, rows * heads, logs, rows, heads)
 
 
-def project_kernel(groups, rows, heads, *refs):
-    weight_ref, out_ref, sums = refs[groups:]
+def project_kernel(groups, rows, heads, halves, *refs):
+    weight_ref, *out_refs, sums = refs[groups:]
     merge_rows(refs[:groups], rows, heads, sums)
     attention = jnp.concatenate(
         [sums[pl.ds(head, rows, stride=heads), :].astype(jnp.bfloat16) for head in range(heads)],
         axis=1,
     )
-    out_ref[...] = jnp.dot(attention, weight_ref[...], preferred_element_type=jnp.float32)
+    mixed = jnp.dot(attention, weight_ref[...], preferred_element_type=jnp.float32)
+    if halves:
+        first = lax.axis_index("head") == 0
+        lower, upper = mixed[: rows // 2], mixed[rows // 2 :]
+        out_refs[0][...] = jnp.where(first, lower, upper)
+        out_refs[1][...] = jnp.where(first, upper, lower)
+    else:
+        out_refs[0][...] = mixed
 
 
 def per_device(
@@ -246,43 +296,37 @@
     group = heads // kv_heads
     own_rows = query.shape[0]
     columns = out_weight.shape[1]
-    rounds = exchange_rounds(devices)
-    me = lax.axis_index("page")
-
-    inclusive = jnp.cumsum(range_counts)
-    lengths = (range_counts - 1) * tokens + last_fill
-    slot_ids = jnp.arange(all_slots, dtype=jnp.int32)
-    inverse = jnp.sum(
-        jnp.where(slot_table[None, :] == slot_ids[:, None], slot_ids[None, :], 0), axis=1
-    )
-    slot_row = jnp.sum((inverse[:, None] >= inclusive[None, :]).astype(jnp.int32), axis=1)
-    picked = slot_row[:, None] == jnp.arange(rows, dtype=jnp.int32)[None, :]
-    slot_end = jnp.sum(
-        jnp.where(picked, (lengths + (inclusive - range_counts) * tokens)[None, :], 0), axis=1
-    )
-    slot_live = slot_end - inverse * tokens
-
-    order = [0]
+    spread = exchange_rounds(devices, 2)
+    rounds = exchange_rounds(devices, 4)
+
+    near = [0] + rounds[0]
+    own_slots = jax.ShapeDtypeStruct((slots,), jnp.int32)
+    place, live, owner = pl.pallas_call(
+        functools.partial(
+            locate_kernel, spread, near, slots, rows, all_slots, own_rows, tokens
+        ),
+        out_shape=[own_slots, own_slots, jax.ShapeDtypeStruct((len(near) * slots,), jnp.int32)],
+        in_specs=[SMEM],
+        out_specs=[SMEM] * 3,
+        scratch_shapes=[
+            pltpu.SMEM((all_slots,), jnp.int32),
+            pltpu.SMEM((rows,), jnp.int32),
+        ],
+        cost_estimate=pl.CostEstimate(
+            flops=LOCATE_FLOPS, bytes_accessed=4 * all_slots, transcendentals=0
+        ),
+        compiler_params=pltpu.CompilerParams(vmem_limit_bytes=MIB),
+        name="locate",
+    )(jnp.concatenate([range_counts, last_fill, slot_table]))
+
     held = [query]
-    for masks in rounds:
+    for turn, masks in enumerate(spread):
         block = jnp.concatenate(held, axis=0) if len(held) > 1 else held[0]
+        if turn == 1:
+            block, place, live, owner = lax.optimization_barrier((block, place, live, owner))
+        elif turn > 1:
+            block = lax.optimization_barrier(block)
         held = [block] + [partner(block, mask, devices) for mask in masks]
-        order = [mask ^ old for mask in [0] + masks for old in order]
-    place_of = [0] * devices
-    for place, mask in enumerate(order):
-        place_of[mask] = place
-    own_slots = lax.dynamic_slice(slot_row, (me * slots,), (slots,))
-    own_live = lax.dynamic_slice(slot_live, (me * slots,), (slots,))
-    away = jnp.bitwise_xor(own_slots // own_rows, me)
-    place = jnp.sum(
-        jnp.where(
-            away[:, None] == jnp.arange(devices, dtype=jnp.int32)[None, :],
-            jnp.array(place_of, jnp.int32)[None, :],
-            0,
-        ),
-        axis=1,
-    )
-    place = place * own_rows + own_slots % own_rows
 
     payload = (slots + stat_blocks(slots)) * heads
     held = [
@@ -297,9 +341,14 @@
                 pltpu.VMEM((rows * heads, LANES), jnp.float32),
                 pltpu.VMEM((slots * heads, LANES), jnp.float32),
             ],
-            compiler_params=pltpu.CompilerParams(vmem_limit_bytes=24 * MIB),
+            compiler_params=pltpu.CompilerParams(vmem_limit_bytes=8 * MIB),
+            cost_estimate=pl.CostEstimate(
+                flops=ATTEND_FLOPS,
+                bytes_accessed=4 * slots * kv_heads * tokens * head_dim,
+                transcendentals=slots * heads * tokens,
+            ),
             name="attend",
-        )(place, own_live, key_scale, value_scale, *held, key_codes, value_codes)
+        )(place, live, key_scale, value_scale, *held, key_codes, value_codes)
     ]
 
     payload = (rows + stat_blocks(rows)) * heads
@@ -307,23 +356,21 @@
     for turn, masks in enumerate(rounds):
         held = held + [partner(held[0], mask, devices) for mask in masks]
         groups = len(held)
-        params = pltpu.CompilerParams(vmem_limit_bytes=16 * MIB)
+        params = pltpu.CompilerParams(vmem_limit_bytes=8 * MIB)
         if turn == 0:
-            sources = [me] + [jnp.bitwise_xor(me, mask) for mask in masks]
-            owner = jnp.concatenate(
-                [lax.dynamic_slice(slot_row, (source * slots,), (slots,)) for source in sources]
-            )
-            owner_lane = jnp.full((1, LANES), -1, jnp.int32).at[0, : groups * slots].set(owner)
             held = [
                 pl.pallas_call(
                     functools.partial(merge_slots_kernel, groups, slots, rows, heads),
                     out_shape=jax.ShapeDtypeStruct((payload, LANES), jnp.bfloat16),
-                    in_specs=[SMEM] + [VMEM] * (groups + 1),
+                    in_specs=[SMEM] + [VMEM] * groups,
                     out_specs=VMEM,
                     scratch_shapes=[sums],
                     compiler_params=params,
+                    cost_estimate=pl.CostEstimate(
+                        flops=MERGE_FLOPS, bytes_accessed=2 * payload * LANES, transcendentals=0
+                    ),
                     name="merge_slots",
-                )(owner, owner_lane, *held)
+                )(owner, *held)
             ]
         elif turn < len(rounds) - 1:
             held = [
@@ -337,21 +384,19 @@
                     name="merge_rows",
                 )(*held)
             ]
-    mixed = pl.pallas_call(
-        functools.partial(project_kernel, len(held), rows, heads),
-        out_shape=jax.ShapeDtypeStruct((rows, columns), jnp.float32),
+    halves = head_devices == 2
+    mixed_shape = jax.ShapeDtypeStruct((rows // (1 + halves), columns), jnp.float32)
+    mixed, *give = pl.pallas_call(
+        functools.partial(project_kernel, len(held), rows, heads, halves),
+        out_shape=[mixed_shape] * (1 + halves),
         in_specs=[VMEM] * (len(held) + 1),
-        out_specs=VMEM,
+        out_specs=[VMEM] * (1 + halves),
         scratch_shapes=[sums],
-        compiler_params=pltpu.CompilerParams(vmem_limit_bytes=16 * MIB),
+        compiler_params=pltpu.CompilerParams(vmem_limit_bytes=8 * MIB),
         name="project",
     )(*held, out_weight)
-    if head_devices == 2:
-        half = rows // 2
-        side = lax.axis_index("head")
-        keep = lax.dynamic_slice(mixed, (side * half, 0), (half, columns))
-        give = lax.dynamic_slice(mixed, ((1 - side) * half, 0), (half, columns))
-        mixed = keep + lax.ppermute(give, "head", [(0, 1), (1, 0)])
+    if halves:
+        mixed = mixed + lax.ppermute(give[0], "head", [(0, 1), (1, 0)])
     else:
         mixed = lax.psum_scatter(mixed, "head", scatter_dimension=0, tiled=True)
     return mixed.astype(jnp.bfloat16)

time: 59.7 us -> 47.6 us (0.80)
  local copies, waits for them, and re-layouts: 11.2 us -> 0.03 us
  other arithmetic: 5.55 us -> 1.49 us
  Pallas kernels: 9.92 us -> 12.2 us
  waiting for transfers between devices: 15.3 us -> 16.8 us
    unnamed x10 -> x12, local copies, waits for them, and re-layouts: 10.4 us -> 0.03 us
    pallas_call x1 -> x2, Pallas kernels: 1.13 us -> 3.31 us  [the longest x1 2.18 us: per_device(): pl.pallas_call(functools.partial(locate_kernel, spread, near, slots, rows...]
    reduce_sum x4 -> x0, other arithmetic: 1.77 us -> none  [the longest x1 0.84 us: per_device(): jnp.sum(jnp.where(away[:, None] == jnp.arange(devices, dtype=jnp.int32)[N...]
    another operation x4 -> x0, other arithmetic: 1.52 us -> none
    ppermute x12 -> x10, waiting for transfers between devices: 14.1 us -> 15.6 us  [partner(): return lax.ppermute(value, 'page', [(i, i ^ mask) for i in range(devices)])]
    another operation x1 -> x0, local copies, waits for them, and re-layouts: 0.73 us -> none
    add x1 -> x0, other arithmetic: 0.69 us -> none  [per_device(): lengths + (inclusive - range_counts) * tokens]
    concatenate x1, other arithmetic: 0.08 us -> 0.76 us  [per_device(): jnp.concatenate([range_counts, last_fill, slot_table])]
  transfers between devices with their start and end apart: 13 -> 11, of which waited for: 9 -> 9; matrix products, arithmetic and copies ran while one was open for 8% -> 2% of each run, Pallas kernels for 0% -> 5%
where the time goes in v2:
time: 47.6 us; the launch traced here: 47.5 us
  starting transfers between devices  16.8 us (35%)
  waiting for transfers between devices  16.8 us (35%)
  Pallas kernels  12.2 us (26%)
  other arithmetic  1.49 us (3%)
    ppermute x10, starting transfers between devices, partner(): return lax.ppermute(value, 'page', [(i, i ^ mask) for i in range(devices)])  16.8 us
    ppermute x10, waiting for transfers between devices, partner(): return lax.ppermute(value, 'page', [(i, i ^ mask) for i in range(devices)])  15.6 us
    pallas_call x1, Pallas kernels, per_device(): pl.pallas_call(functools.partial(attend_kernel, len(held), slots, kv_head...  7.58 us
    pallas_call x1, Pallas kernels, per_device(): pl.pallas_call(functools.partial(locate_kernel, spread, near, slots, rows...  2.18 us
    pallas_call x1, Pallas kernels, per_device(): pl.pallas_call(functools.partial(merge_slots_kernel, groups, slots, rows,...  1.28 us
    ppermute x1, waiting for transfers between devices, per_device(): mixed = mixed + lax.ppermute(give[0], 'head', [(0, 1), (1, 0)])  1.19 us
    pallas_call x1, Pallas kernels, per_device(): pl.pallas_call(functools.partial(project_kernel, len(held), rows, heads,...  1.13 us
  transfers between devices with their start and end apart: 11, of which 9 were waited for; matrix products, arithmetic and copies ran while one was open for 2% of the time, Pallas kernels for 5%

profile of v2, /device:TPU:0, one launch (start us, length us, event | category | flops | bytes accessed | tf_op | source)
XLA Modules:
  0.0 47.5 jit_solution(917740392500959338)
XLA Ops:
  0.0 4.0 %collective-permute-start = (bf16[1,4096]{1,0:T(2,128)(2,1)}, bf16[1,4096]{1,0:T(2,128)(2,1)S(1)}, u32[]{:S(2)}, u32[]{:S(2)}) collective-permute-start(bf16[1,4096]{1,0:T(2,128)(2,1)} %param.9), channel_id=1, source_target_pairs={{0,16},{2,18},{4,20},{6,22},{8,24},{10,26},{12,28},{14,30},{16,0},... | collective-permute-start | bytes 24584 | tf_op jit(solution)/shard_map/ppermute | solution.py:30
  4.0 0.8 %pad_add_fusion.table_ref = s32[160]{0:T(256)S(1)} fusion(s32[128]{0:T(128)} %param.17, s32[16]{0:T(128)} %param.16, s32[16]{0:T(128)} %param.15), kind=kLoop, calls=%fused_computation.4 | loop fusion | flops 320 | bytes 1280 | tf_op jit(solution)/shard_map/concatenate | solution.py:320
  4.8 2.2 %locate.1 = (s32[8]{0:T(128)S(1)}, s32[8]{0:T(128)S(1)}, s32[32]{0:T(128)S(1)}) custom-call(s32[160]{0:T(256)S(1)} %pad_add_fusion.table_ref), custom_call_target="tpu_custom_call" | custom-call | flops 20000000000 | bytes 512 | tf_op jit(solution)/shard_map/locate/pallas_call | solution.py:304
  7.1 1.6 %collective-permute-start.1 = (bf16[2,4096]{1,0:T(2,128)(2,1)S(1)}, bf16[2,4096]{1,0:T(2,128)(2,1)S(1)}, u32[]{:S(2)}, u32[]{:S(2)}) collective-permute-start(bf16[2,4096]{1,0:T(2,128)(2,1)S(1)} %pad_maximum_fusion.2), channel_id=1, source_target_pairs={{0,8},{2,10},{4,12},{6,14},{8,0},{10,2},{12,4},{14,6},{16,24},{18,... | collective-permute-start | bytes 49160 | tf_op jit(solution)/shard_map/ppermute | solution.py:30
  8.7 2.2 %collective-permute-done.1 = bf16[2,4096]{1,0:T(2,128)(2,1)S(1)} collective-permute-done((bf16[2,4096]{1,0:T(2,128)(2,1)S(1)}, bf16[2,4096]{1,0:T(2,128)(2,1)S(1)}, u32[]{:S(2)}, u32[]{:S(2)}) %collective-permute-start.1) | collective-permute-done | bytes 16416 | tf_op jit(solution)/shard_map/ppermute | solution.py:30
  10.9 1.6 %collective-permute-start.2 = (bf16[4,4096]{1,0:T(4,128)(2,1)S(1)}, bf16[4,4096]{1,0:T(4,128)(2,1)S(1)}, u32[]{:S(2)}, u32[]{:S(2)}) collective-permute-start(bf16[4,4096]{1,0:T(4,128)(2,1)S(1)} %pad_maximum_fusion.1), channel_id=1, source_target_pairs={{0,4},{2,6},{4,0},{6,2},{8,12},{10,14},{12,8},{14,10},{16,20},{18,... | collective-permute-start | bytes 98312 | tf_op jit(solution)/shard_map/ppermute | solution.py:30
  12.5 2.4 %collective-permute-done.2 = bf16[4,4096]{1,0:T(4,128)(2,1)S(1)} collective-permute-done((bf16[4,4096]{1,0:T(4,128)(2,1)S(1)}, bf16[4,4096]{1,0:T(4,128)(2,1)S(1)}, u32[]{:S(2)}, u32[]{:S(2)}) %collective-permute-start.2) | collective-permute-done | bytes 32800 | tf_op jit(solution)/shard_map/ppermute | solution.py:30
  15.0 1.6 %collective-permute-start.3 = (bf16[8,4096]{1,0:T(8,128)(2,1)S(1)}, bf16[8,4096]{1,0:T(8,128)(2,1)S(1)}, u32[]{:S(2)}, u32[]{:S(2)}) collective-permute-start(bf16[8,4096]{1,0:T(8,128)(2,1)S(1)} %pad_maximum_fusion.refs_0_), channel_id=1, source_target_pairs={{0,2},{2,0},{4,6},{6,4},{8,10},{10,8},{12,14},{14,12},{16,18},{18,... | collective-permute-start | bytes 196616 | tf_op jit(solution)/shard_map/ppermute | solution.py:30
  16.5 2.8 %collective-permute-done.3.refs_1_ = bf16[8,4096]{1,0:T(8,128)(2,1)S(1)} collective-permute-done((bf16[8,4096]{1,0:T(8,128)(2,1)S(1)}, bf16[8,4096]{1,0:T(8,128)(2,1)S(1)}, u32[]{:S(2)}, u32[]{:S(2)}) %collective-permute-start.3) | collective-permute-done | bytes 65568 | tf_op jit(solution)/shard_map/ppermute | solution.py:30
  19.3 7.6 %attend.1.refs_0_ = bf16[288,128]{1,0:T(8,128)(2,1)S(1)} custom-call(s32[8]{0:T(128)S(1)} %get-tuple-element.18.place_ref, s32[8]{0:T(128)S(1)} %get-tuple-element.19.live_ref, f32[8,4,8]{2,1,0:T(4,128)S(1)} %copy-done.3, f32[8,4,8]{2,1,0:T(4,128)S(1)} %copy-done.4, bf16[8,4096]{1,0:T(8,128)(2,1)S(1)} %pad_maximum_fusion.refs_0_, ...), custom_call_target="tpu_custom_call" | custom-call | flops 5000000000 | bytes 16777216 | tf_op jit(solution)/shard_map/attend/pallas_call | solution.py:333
  26.9 3.0 %collective-permute-start.6 = (bf16[288,128]{1,0:T(8,128)(2,1)S(1)}, bf16[288,128]{1,0:T(8,128)(2,1)S(1)}, u32[]{:S(2)}, u32[]{:S(2)}) collective-permute-start(bf16[288,128]{1,0:T(8,128)(2,1)S(1)} %attend.1.refs_0_), channel_id=1, source_target_pairs={{0,24},{2,26},{4,28},{6,30},{8,16},{10,18},{12,20},{14,22},{16,8},... | collective-permute-start | bytes 221192 | tf_op jit(solution)/shard_map/ppermute | solution.py:30
  30.0 1.3 %collective-permute-start.4 = (bf16[288,128]{1,0:T(8,128)(2,1)S(1)}, bf16[288,128]{1,0:T(8,128)(2,1)S(1)}, u32[]{:S(2)}, u32[]{:S(2)}) collective-permute-start(bf16[288,128]{1,0:T(8,128)(2,1)S(1)} %attend.1.refs_0_), channel_id=1, source_target_pairs={{0,8},{2,10},{4,12},{6,14},{8,0},{10,2},{12,4},{14,6},{16,24},{18,... | collective-permute-start | bytes 221192 | tf_op jit(solution)/shard_map/ppermute | solution.py:30
  31.4 1.8 %collective-permute-done.6.refs_3_ = bf16[288,128]{1,0:T(8,128)(2,1)S(1)} collective-permute-done((bf16[288,128]{1,0:T(8,128)(2,1)S(1)}, bf16[288,128]{1,0:T(8,128)(2,1)S(1)}, u32[]{:S(2)}, u32[]{:S(2)}) %collective-permute-start.6) | collective-permute-done | bytes 73760 | tf_op jit(solution)/shard_map/ppermute | solution.py:30
  33.1 2.0 %collective-permute-done.5.refs_2_ = bf16[288,128]{1,0:T(8,128)(2,1)S(1)} collective-permute-done((bf16[288,128]{1,0:T(8,128)(2,1)S(1)}, bf16[288,128]{1,0:T(8,128)(2,1)S(1)}, u32[]{:S(2)}, u32[]{:S(2)}) %collective-permute-start.5) | collective-permute-done | bytes 73760 | tf_op jit(solution)/shard_map/ppermute | solution.py:30
  35.2 1.3 %merge_slots.1.refs_0_ = bf16[544,128]{1,0:T(8,128)(2,1)S(1)} custom-call(s32[32]{0:T(128)S(1)} %get-tuple-element.17.owner_ref, bf16[288,128]{1,0:T(8,128)(2,1)S(1)} %attend.1.refs_0_, bf16[288,128]{1,0:T(8,128)(2,1)S(1)} %collective-permute-done.4.refs_1_, bf16[288,128]{1,0:T(8,128)(2,1)S(1)} %collective-permute-done.5.refs_2_, ...), custom_call_target="tpu_custom_call" | custom-call | flops 20000000000 | bytes 139264 | tf_op jit(solution)/shard_map/merge_slots/pallas_call | solution.py:362
  36.5 2.5 %collective-permute-start.9 = (bf16[544,128]{1,0:T(8,128)(2,1)S(1)}, bf16[544,128]{1,0:T(8,128)(2,1)S(1)}, u32[]{:S(2)}, u32[]{:S(2)}) collective-permute-start(bf16[544,128]{1,0:T(8,128)(2,1)S(1)} %merge_slots.1.refs_0_), channel_id=1, source_target_pairs={{0,6},{2,4},{4,2},{6,0},{8,14},{10,12},{12,10},{14,8},{16,22},{18,... | collective-permute-start | bytes 417800 | tf_op jit(solution)/shard_map/ppermute | solution.py:30
  39.0 0.5 %collective-permute-start.8 = (bf16[544,128]{1,0:T(8,128)(2,1)S(1)}, bf16[544,128]{1,0:T(8,128)(2,1)S(1)}, u32[]{:S(2)}, u32[]{:S(2)}) collective-permute-start(bf16[544,128]{1,0:T(8,128)(2,1)S(1)} %merge_slots.1.refs_0_), channel_id=1, source_target_pairs={{0,4},{2,6},{4,0},{6,2},{8,12},{10,14},{12,8},{14,10},{16,20},{18,... | collective-permute-start | bytes 417800 | tf_op jit(solution)/shard_map/ppermute | solution.py:30
  39.5 0.5 %collective-permute-start.7 = (bf16[544,128]{1,0:T(8,128)(2,1)S(1)}, bf16[544,128]{1,0:T(8,128)(2,1)S(1)}, u32[]{:S(2)}, u32[]{:S(2)}) collective-permute-start(bf16[544,128]{1,0:T(8,128)(2,1)S(1)} %merge_slots.1.refs_0_), channel_id=1, source_target_pairs={{0,2},{2,0},{4,6},{6,4},{8,10},{10,8},{12,14},{14,12},{16,18},{18,... | collective-permute-start | bytes 417800 | tf_op jit(solution)/shard_map/ppermute | solution.py:30
  40.0 2.5 %collective-permute-done.9.refs_3_ = bf16[544,128]{1,0:T(8,128)(2,1)S(1)} collective-permute-done((bf16[544,128]{1,0:T(8,128)(2,1)S(1)}, bf16[544,128]{1,0:T(8,128)(2,1)S(1)}, u32[]{:S(2)}, u32[]{:S(2)}) %collective-permute-start.9) | collective-permute-done | bytes 139296 | tf_op jit(solution)/shard_map/ppermute | solution.py:30
  42.5 1.5 %collective-permute-done.8.refs_2_ = bf16[544,128]{1,0:T(8,128)(2,1)S(1)} collective-permute-done((bf16[544,128]{1,0:T(8,128)(2,1)S(1)}, bf16[544,128]{1,0:T(8,128)(2,1)S(1)}, u32[]{:S(2)}, u32[]{:S(2)}) %collective-permute-start.8) | collective-permute-done | bytes 139296 | tf_op jit(solution)/shard_map/ppermute | solution.py:30
  44.0 0.5 %collective-permute-done.7.refs_1_ = bf16[544,128]{1,0:T(8,128)(2,1)S(1)} collective-permute-done((bf16[544,128]{1,0:T(8,128)(2,1)S(1)}, bf16[544,128]{1,0:T(8,128)(2,1)S(1)}, u32[]{:S(2)}, u32[]{:S(2)}) %collective-permute-start.7) | collective-permute-done | bytes 139296 | tf_op jit(solution)/shard_map/ppermute | solution.py:30
  44.5 1.1 %project.1 = (f32[8,512]{1,0:T(8,128)S(1)}, f32[8,512]{1,0:T(8,128)S(1)}) custom-call(bf16[544,128]{1,0:T(8,128)(2,1)S(1)} %merge_slots.1.refs_0_, bf16[544,128]{1,0:T(8,128)(2,1)S(1)} %collective-permute-done.7.refs_1_, bf16[544,128]{1,0:T(8,128)(2,1)S(1)} %collective-permute-done.8.refs_2_, bf16[544,128]{1,0:T(8,128)(2,1)S(1)} %collective-permute-done.9.refs_3_, ...), custom_call_target="tpu_custom_call" | custom-call | tf_op jit(solution)/shard_map/project/pallas_call | solution.py:389
  45.7 1.2 %collective-permute-done.10 = f32[8,512]{1,0:T(8,128)S(1)} collective-permute-done((f32[8,512]{1,0:T(8,128)S(1)}, f32[8,512]{1,0:T(8,128)S(1)}, u32[]{:S(2)}, u32[]{:S(2)}) %collective-permute-start.10) | collective-permute-done | bytes 16416 | tf_op jit(solution)/shard_map/ppermute | solution.py:399
  46.9 0.6 %add_convert_fusion = bf16[8,512]{1,0:T(8,128)(2,1)} fusion(f32[8,512]{1,0:T(8,128)S(1)} %get-tuple-element.21, f32[8,512]{1,0:T(8,128)S(1)} %collective-permute-done.10), kind=kLoop, calls=%fused_computation.3 | loop fusion | flops 8192 | bytes 40960 | tf_op jit(solution)/shard_map/convert_element_type | solution.py:402
  (19 shorter events, 0.3 us)
Async XLA Ops:
  0.0 7.0 %collective-permute-start = (bf16[1,4096]{1,0:T(2,128)(2,1)}, bf16[1,4096]{1,0:T(2,128)(2,1)S(1)}, u32[]{:S(2)}, u32[]{:S(2)}) collective-permute-start(bf16[1,4096]{1,0:T(2,128)(2,1)} %param.9), channel_id=1, source_target_pairs={{0,16},{2,18},{4,20},{6,22},{8,24},{10,26},{12,28},{14,30},{16,0},... | collective-permute-start | bytes 24584 | tf_op jit(solution)/shard_map/ppermute | solution.py:30
  4.8 2.2 %copy-start.5 = (bf16[1,4096]{1,0:T(2,128)(2,1)S(1)}, bf16[1,4096]{1,0:T(2,128)(2,1)}, u32[]{:S(2)}) copy-start(bf16[1,4096]{1,0:T(2,128)(2,1)} %param.9) | copy-start | bytes 24580
  4.8 14.5 %copy-start.1 = (bf16[8,4,1024,128]{3,2,1,0:T(8,128)(2,1)S(1)}, bf16[8,4,1024,128]{3,2,1,0:T(8,128)(2,1)}, u32[]{:S(2)}) copy-start(bf16[8,4,1024,128]{3,2,1,0:T(8,128)(2,1)} %refs_2_.1) | copy-start | bytes 25165828
  4.8 14.5 %copy-start.2 = (bf16[8,4,1024,128]{3,2,1,0:T(8,128)(2,1)S(1)}, bf16[8,4,1024,128]{3,2,1,0:T(8,128)(2,1)}, u32[]{:S(2)}) copy-start(bf16[8,4,1024,128]{3,2,1,0:T(8,128)(2,1)} %refs_3_.1) | copy-start | bytes 25165828
  4.8 14.5 %copy-start.3 = (f32[8,4,8]{2,1,0:T(4,128)S(1)}, f32[8,4,8]{2,1,0:T(4,128)}, u32[]{:S(2)}) copy-start(f32[8,4,8]{2,1,0:T(4,128)} %key_scale_ref.1) | copy-start | bytes 3076
  4.8 14.5 %copy-start.4 = (f32[8,4,8]{2,1,0:T(4,128)S(1)}, f32[8,4,8]{2,1,0:T(4,128)}, u32[]{:S(2)}) copy-start(f32[8,4,8]{2,1,0:T(4,128)} %value_scale_ref.1) | copy-start | bytes 3076
  7.1 3.8 %collective-permute-start.1 = (bf16[2,4096]{1,0:T(2,128)(2,1)S(1)}, bf16[2,4096]{1,0:T(2,128)(2,1)S(1)}, u32[]{:S(2)}, u32[]{:S(2)}) collective-permute-start(bf16[2,4096]{1,0:T(2,128)(2,1)S(1)} %pad_maximum_fusion.2), channel_id=1, source_target_pairs={{0,8},{2,10},{4,12},{6,14},{8,0},{10,2},{12,4},{14,6},{16,24},{18,... | collective-permute-start | bytes 49160 | tf_op jit(solution)/shard_map/ppermute | solution.py:30
  10.9 4.0 %collective-permute-start.2 = (bf16[4,4096]{1,0:T(4,128)(2,1)S(1)}, bf16[4,4096]{1,0:T(4,128)(2,1)S(1)}, u32[]{:S(2)}, u32[]{:S(2)}) collective-permute-start(bf16[4,4096]{1,0:T(4,128)(2,1)S(1)} %pad_maximum_fusion.1), channel_id=1, source_target_pairs={{0,4},{2,6},{4,0},{6,2},{8,12},{10,14},{12,8},{14,10},{16,20},{18,... | collective-permute-start | bytes 98312 | tf_op jit(solution)/shard_map/ppermute | solution.py:30
  15.0 4.3 %collective-permute-start.3 = (bf16[8,4096]{1,0:T(8,128)(2,1)S(1)}, bf16[8,4096]{1,0:T(8,128)(2,1)S(1)}, u32[]{:S(2)}, u32[]{:S(2)}) collective-permute-start(bf16[8,4096]{1,0:T(8,128)(2,1)S(1)} %pad_maximum_fusion.refs_0_), channel_id=1, source_target_pairs={{0,2},{2,0},{4,6},{6,4},{8,10},{10,8},{12,14},{14,12},{16,18},{18,... | collective-permute-start | bytes 196616 | tf_op jit(solution)/shard_map/ppermute | solution.py:30
  26.9 17.6 %copy-start = (bf16[4096,512]{1,0:T(8,128)(2,1)S(1)}, bf16[4096,512]{1,0:T(8,128)(2,1)}, u32[]{:S(2)}) copy-start(bf16[4096,512]{1,0:T(8,128)(2,1)} %refs_4_.1) | copy-start | bytes 12582916
  26.9 6.2 %collective-permute-start.6 = (bf16[288,128]{1,0:T(8,128)(2,1)S(1)}, bf16[288,128]{1,0:T(8,128)(2,1)S(1)}, u32[]{:S(2)}, u32[]{:S(2)}) collective-permute-start(bf16[288,128]{1,0:T(8,128)(2,1)S(1)} %attend.1.refs_0_), channel_id=1, source_target_pairs={{0,24},{2,26},{4,28},{6,30},{8,16},{10,18},{12,20},{14,22},{16,8},... | collective-permute-start | bytes 221192 | tf_op jit(solution)/shard_map/ppermute | solution.py:30
  29.9 5.3 %collective-permute-start.5 = (bf16[288,128]{1,0:T(8,128)(2,1)S(1)}, bf16[288,128]{1,0:T(8,128)(2,1)S(1)}, u32[]{:S(2)}, u32[]{:S(2)}) collective-permute-start(bf16[288,128]{1,0:T(8,128)(2,1)S(1)} %attend.1.refs_0_), channel_id=1, source_target_pairs={{0,16},{2,18},{4,20},{6,22},{8,24},{10,26},{12,28},{14,30},{16,0},... | collective-permute-start | bytes 221192 | tf_op jit(solution)/shard_map/ppermute | solution.py:30
  30.0 5.1 %collective-permute-start.4 = (bf16[288,128]{1,0:T(8,128)(2,1)S(1)}, bf16[288,128]{1,0:T(8,128)(2,1)S(1)}, u32[]{:S(2)}, u32[]{:S(2)}) collective-permute-start(bf16[288,128]{1,0:T(8,128)(2,1)S(1)} %attend.1.refs_0_), channel_id=1, source_target_pairs={{0,8},{2,10},{4,12},{6,14},{8,0},{10,2},{12,4},{14,6},{16,24},{18,... | collective-permute-start | bytes 221192 | tf_op jit(solution)/shard_map/ppermute | solution.py:30
  36.5 6.0 %collective-permute-start.9 = (bf16[544,128]{1,0:T(8,128)(2,1)S(1)}, bf16[544,128]{1,0:T(8,128)(2,1)S(1)}, u32[]{:S(2)}, u32[]{:S(2)}) collective-permute-start(bf16[544,128]{1,0:T(8,128)(2,1)S(1)} %merge_slots.1.refs_0_), channel_id=1, source_target_pairs={{0,6},{2,4},{4,2},{6,0},{8,14},{10,12},{12,10},{14,8},{16,22},{18,... | collective-permute-start | bytes 417800 | tf_op jit(solution)/shard_map/ppermute | solution.py:30
  39.0 5.1 %collective-permute-start.8 = (bf16[544,128]{1,0:T(8,128)(2,1)S(1)}, bf16[544,128]{1,0:T(8,128)(2,1)S(1)}, u32[]{:S(2)}, u32[]{:S(2)}) collective-permute-start(bf16[544,128]{1,0:T(8,128)(2,1)S(1)} %merge_slots.1.refs_0_), channel_id=1, source_target_pairs={{0,4},{2,6},{4,0},{6,2},{8,12},{10,14},{12,8},{14,10},{16,20},{18,... | collective-permute-start | bytes 417800 | tf_op jit(solution)/shard_map/ppermute | solution.py:30
  39.5 5.1 %collective-permute-start.7 = (bf16[544,128]{1,0:T(8,128)(2,1)S(1)}, bf16[544,128]{1,0:T(8,128)(2,1)S(1)}, u32[]{:S(2)}, u32[]{:S(2)}) collective-permute-start(bf16[544,128]{1,0:T(8,128)(2,1)S(1)} %merge_slots.1.refs_0_), channel_id=1, source_target_pairs={{0,2},{2,0},{4,6},{6,4},{8,10},{10,8},{12,14},{14,12},{16,18},{18,... | collective-permute-start | bytes 417800 | tf_op jit(solution)/shard_map/ppermute | solution.py:30
  45.7 1.2 %collective-permute-start.10 = (f32[8,512]{1,0:T(8,128)S(1)}, f32[8,512]{1,0:T(8,128)S(1)}, u32[]{:S(2)}, u32[]{:S(2)}) collective-permute-start(f32[8,512]{1,0:T(8,128)S(1)} %get-tuple-element.22), channel_id=1, source_target_pairs={{0,1},{1,0},{2,3},{3,2},{4,5},{5,4},{6,7},{7,6},{8,9},{9,8},{10,11... | collective-permute-start | bytes 49160 | tf_op jit(solution)/shard_map/ppermute | solution.py:399

commit v3 on v2

--- a/solution.py
+++ b/solution.py
@@ -115,8 +115,26 @@
                 live_ref[slot] = (table_ref[row] - 1 - before) * tokens + table_ref[fills + row]
 
 
+def columns_kernel(group, factor, *refs):
+    for scale_ref, out_ref, multiplier in zip(refs[:2], refs[2:], (factor, 1.0)):
+        slots, kv_heads, pages = scale_ref.shape
+        batches = out_ref.shape[0]
+        each = slots // batches
+        for batch in range(batches):
+            parts = []
+            for index in range(each):
+                scale = scale_ref[batch * each + index] * multiplier
+                for kv in range(kv_heads):
+                    parts.append(jnp.broadcast_to(scale[kv : kv + 1], (group, pages)))
+            table = jnp.concatenate(parts, axis=0)
+            for page in range(pages):
+                out_ref[batch, page] = jnp.broadcast_to(
+                    table[:, page : page + 1], (table.shape[0], LANES)
+                )
+
+
 def attend_kernel(
-    pieces, slots, kv_heads, group, tokens, pages, key_scaling,
+    pieces, slots, kv_heads, group, tokens, pages,
     place_ref, live_ref, key_scale_ref, value_scale_ref, *refs,
 ):
     query_refs = refs[:pieces]
@@ -131,66 +149,76 @@
                 :, head * LANES : (head + 1) * LANES
             ]
     together = 2 if kv_heads % 2 == 0 else 1
+    each = min(slots, LANES // heads)
     rows = together * group
     lane = lane_index((heads, LANES))
+    token = lane_index((heads, page_tokens))
+    upper = lax.broadcasted_iota(jnp.int32, (rows, LANES), 0) < group
+    zero = jnp.zeros((rows, LANES), jnp.bfloat16)
     logs = jnp.zeros((heads, LANES), jnp.float32)
-    for slot in range(slots):
-        start = pl.multiple_of(place_ref[slot] * heads, 8)
-        query = queries[pl.ds(start, heads), :].astype(jnp.bfloat16)
-        live = live_ref[slot]
-        column = []
-        for first in range(0, kv_heads, together):
-            own = query[first * group : first * group + rows]
-            if together == 2:
-                upper = lax.broadcasted_iota(jnp.int32, (rows, LANES), 0) < group
-                zero = jnp.zeros_like(own)
-                own = jnp.concatenate(
-                    [jnp.where(upper, own, zero), jnp.where(upper, zero, own)], axis=1
+
+    def joined(ref, slot, kv):
+        if together == 1:
+            return ref[slot, kv]
+        return jnp.concatenate([ref[slot, kv], ref[slot, kv + 1]], axis=1)
+
+    for batch in range(slots // each):
+        dotted = []
+        for index in range(each):
+            slot = batch * each + index
+            start = pl.multiple_of(place_ref[slot] * heads, 8)
+            query = queries[pl.ds(start, heads), :].astype(jnp.bfloat16)
+            for kv in range(0, kv_heads, together):
+                own = query[kv * group : kv * group + rows]
+                if together == 2:
+                    own = jnp.concatenate(
+                        [jnp.where(upper, own, zero), jnp.where(upper, zero, own)], axis=1
+                    )
+                dotted.append(
+                    lax.dot_general(
+                        own,
+                        joined(key_ref, slot, kv),
+                        (((1,), (1,)), ((), ())),
+                        preferred_element_type=jnp.float32,
+                    )
                 )
-                keys = jnp.concatenate([key_ref[slot, first], key_ref[slot, first + 1]], axis=1)
-                values = jnp.concatenate(
-                    [value_ref[slot, first], value_ref[slot, first + 1]], axis=1
+        dotted = jnp.concatenate(dotted, axis=0)
+        scores = []
+        for page in range(pages):
+            part = dotted[:, page * page_tokens : (page + 1) * page_tokens]
+            part = part * key_scale_ref[batch, page]
+            masked = []
+            for index in range(each):
+                own = part[index * heads : (index + 1) * heads]
+                live = live_ref[batch * each + index] - page * page_tokens
+                masked.append(jnp.where(token < live, own, LOW))
+            scores.append(jnp.concatenate(masked, axis=0) if each > 1 else masked[0])
+        peak = jnp.max(functools.reduce(jnp.maximum, scores), axis=1, keepdims=True)
+        total, weights = None, []
+        for page in range(pages):
+            expon = jnp.exp(scores[page] - peak)
+            total = expon if total is None else total + expon
+            weights.append((expon * value_scale_ref[batch, page]).astype(jnp.bfloat16))
+        total = jnp.sum(total, axis=1, keepdims=True)
+        weights = jnp.concatenate(weights, axis=1)
+        scale = 1.0 / total
+        log = peak + jnp.log(total)
+        for index in range(each):
+            slot = batch * each + index
+            for kv in range(0, kv_heads, together):
+                first = index * heads + kv * group
+                partial = jnp.dot(
+                    weights[first : first + rows],
+                    joined(value_ref, slot, kv),
+                    preferred_element_type=jnp.float32,
                 )
-            else:
-                keys, values = key_ref[slot, first], value_ref[slot, first]
-            dotted = lax.dot_general(
-                own, keys, (((1,), (1,)), ((), ())), preferred_element_type=jnp.float32
-            )
-
-            def by_page(scale_ref, page):
-                parts = [
-                    jnp.full((group, page_tokens), scale_ref[slot, first + k, page], jnp.float32)
-                    for k in range(together)
-                ]
-                return jnp.concatenate(parts, axis=0) if together > 1 else parts[0]
-
-            token = lane_index((rows, page_tokens))
-            scores = []
-            for page in range(pages):
-                part = dotted[:, page * page_tokens : (page + 1) * page_tokens]
-                part = part * (by_page(key_scale_ref, page) * key_scaling)
-                scores.append(jnp.where(token + page * page_tokens < live, part, LOW))
-            peak = functools.reduce(jnp.maximum, scores)
-            peak = jnp.max(peak, axis=1, keepdims=True)
-            total = None
-            weights = []
-            for page in range(pages):
-                expon = jnp.exp(scores[page] - peak)
-                total = expon if total is None else total + expon
-                weights.append((expon * by_page(value_scale_ref, page)).astype(jnp.bfloat16))
-            total = jnp.sum(total, axis=1, keepdims=True)
-            partial = jnp.dot(
-                jnp.concatenate(weights, axis=1), values, preferred_element_type=jnp.float32
-            )
-            if together == 2:
-                partial = jnp.concatenate(
-                    [partial[:group, :LANES], partial[group:, LANES:]], axis=0
-                )
-            at = slot * heads + first * group
-            outs[at : at + rows, :] = partial / total
-            column.append(peak + jnp.log(total))
-        column = jnp.concatenate(column, axis=0) if len(column) > 1 else column[0]
-        logs = jnp.where(lane == slot, column, logs)
+                if together == 2:
+                    partial = jnp.concatenate(
+                        [partial[:group, :LANES], partial[group:, LANES:]], axis=0
+                    )
+                at = slot * heads + kv * group
+                outs[at : at + rows, :] = partial * scale[first : first + rows]
+            logs = jnp.where(lane == slot, log[index * heads : (index + 1) * heads], logs)
     out_ref[: slots * heads, :] = outs[...].astype(jnp.bfloat16)
     store_stats(out_ref, slots * heads, logs, slots, heads)
 
@@ -300,6 +328,7 @@
     rounds = exchange_rounds(devices, 4)
 
     near = [0] + rounds[0]
+    tables = jnp.concatenate([range_counts, last_fill, slot_table])
     own_slots = jax.ShapeDtypeStruct((slots,), jnp.int32)
     place, live, owner = pl.pallas_call(
         functools.partial(
@@ -317,7 +346,22 @@
         ),
         compiler_params=pltpu.CompilerParams(vmem_limit_bytes=MIB),
         name="locate",
-    )(jnp.concatenate([range_counts, last_fill, slot_table]))
+    )(tables)
+
+    batches = slots // min(slots, LANES // heads)
+    scales = pl.pallas_call(
+        functools.partial(columns_kernel, group, head_dim**-0.5),
+        out_shape=[
+            jax.ShapeDtypeStruct(
+                (batches, pages, slots // batches * heads, LANES), jnp.float32
+            )
+        ]
+        * 2,
+        in_specs=[VMEM] * 2,
+        out_specs=[VMEM] * 2,
+        compiler_params=pltpu.CompilerParams(vmem_limit_bytes=2 * MIB),
+        name="columns",
+    )(key_scale, value_scale)
 
     held = [query]
     for turn, masks in enumerate(spread):
@@ -332,10 +376,10 @@
     held = [
         pl.pallas_call(
             functools.partial(
-                attend_kernel, len(held), slots, kv_heads, group, tokens, pages, head_dim**-0.5
+                attend_kernel, len(held), slots, kv_heads, group, tokens, pages
             ),
             out_shape=jax.ShapeDtypeStruct((payload, LANES), jnp.bfloat16),
-            in_specs=[SMEM] * 4 + [VMEM] * (len(held) + 2),
+            in_specs=[SMEM] * 2 + [VMEM] * (len(held) + 4),
             out_specs=VMEM,
             scratch_shapes=[
                 pltpu.VMEM((rows * heads, LANES), jnp.float32),
@@ -348,7 +392,14 @@
                 transcendentals=slots * heads * tokens,
             ),
             name="attend",
-        )(place, live, key_scale, value_scale, *held, key_codes, value_codes)
+        )(
+            place,
+            live,
+            *scales,
+            *held,
+            key_codes,
+            value_codes,
+        )
     ]
 
     payload = (rows + stat_blocks(rows)) * heads

time: 47.6 us -> 44 us (0.924)
  Pallas kernels: 12.2 us -> 9.32 us
  waiting for transfers between devices: 16.8 us -> 16.2 us
    pallas_call x1, Pallas kernels: 7.58 us -> 4.08 us  [per_device(): pl.pallas_call(functools.partial(attend_kernel, len(held), slots, kv_head...]
    ppermute x10, waiting for transfers between devices: 15.6 us -> 15 us  [partner(): return lax.ppermute(value, 'page', [(i, i ^ mask) for i in range(devices)])]
    pallas_call x0 -> x1, Pallas kernels: none -> 0.64 us  [per_device(): pl.pallas_call(functools.partial(columns_kernel, group, head_dim ** (-0.5...]
  transfers between devices with their start and end apart: 11 -> 11, of which waited for: 9 -> 9; matrix products, arithmetic and copies ran while one was open for 2% -> 2% of each run, Pallas kernels for 5% -> 6%
where the time goes in v3:
time: 44 us; the launch traced here: 43.9 us
  starting transfers between devices  16.8 us (38%)
  waiting for transfers between devices  16.2 us (37%)
  Pallas kernels  9.32 us (21%)
  other arithmetic  1.49 us (3%)
    ppermute x10, starting transfers between devices, partner(): return lax.ppermute(value, 'page', [(i, i ^ mask) for i in range(devices)])  16.8 us
    ppermute x10, waiting for transfers between devices, partner(): return lax.ppermute(value, 'page', [(i, i ^ mask) for i in range(devices)])  15 us
    pallas_call x1, Pallas kernels, per_device(): pl.pallas_call(functools.partial(attend_kernel, len(held), slots, kv_head...  4.08 us
    pallas_call x1, Pallas kernels, per_device(): pl.pallas_call(functools.partial(locate_kernel, spread, near, slots, rows...  2.18 us
    pallas_call x1, Pallas kernels, per_device(): pl.pallas_call(functools.partial(merge_slots_kernel, groups, slots, rows,...  1.28 us
    ppermute x1, waiting for transfers between devices, per_device(): mixed = mixed + lax.ppermute(give[0], 'head', [(0, 1), (1, 0)])  1.19 us
    pallas_call x1, Pallas kernels, per_device(): pl.pallas_call(functools.partial(project_kernel, len(held), rows, heads,...  1.13 us
  transfers between devices with their start and end apart: 11, of which 9 were waited for; matrix products, arithmetic and copies ran while one was open for 2% of the time, Pallas kernels for 6%

profile of v3, /device:TPU:0, one launch (start us, length us, event | category | flops | bytes accessed | tf_op | source)
XLA Modules:
  0.0 43.9 jit_solution(7618509193271094847)
XLA Ops:
  0.0 4.0 %collective-permute-start = (bf16[1,4096]{1,0:T(2,128)(2,1)}, bf16[1,4096]{1,0:T(2,128)(2,1)S(1)}, u32[]{:S(2)}, u32[]{:S(2)}) collective-permute-start(bf16[1,4096]{1,0:T(2,128)(2,1)} %param.9), channel_id=1, source_target_pairs={{0,16},{2,18},{4,20},{6,22},{8,24},{10,26},{12,28},{14,30},{16,0},... | collective-permute-start | bytes 24584 | tf_op jit(solution)/shard_map/ppermute | solution.py:30
  4.0 0.8 %pad_add_fusion.table_ref = s32[160]{0:T(256)S(1)} fusion(s32[128]{0:T(128)} %param.17, s32[16]{0:T(128)} %param.16, s32[16]{0:T(128)} %param.15), kind=kLoop, calls=%fused_computation.4 | loop fusion | flops 320 | bytes 1280 | tf_op jit(solution)/shard_map/concatenate | solution.py:331
  4.8 2.2 %locate.1 = (s32[8]{0:T(128)S(1)}, s32[8]{0:T(128)S(1)}, s32[32]{0:T(128)S(1)}) custom-call(s32[160]{0:T(256)S(1)} %pad_add_fusion.table_ref), custom_call_target="tpu_custom_call" | custom-call | flops 20000000000 | bytes 512 | tf_op jit(solution)/shard_map/locate/pallas_call | solution.py:333
  7.1 1.6 %collective-permute-start.1 = (bf16[2,4096]{1,0:T(2,128)(2,1)S(1)}, bf16[2,4096]{1,0:T(2,128)(2,1)S(1)}, u32[]{:S(2)}, u32[]{:S(2)}) collective-permute-start(bf16[2,4096]{1,0:T(2,128)(2,1)S(1)} %pad_maximum_fusion.2), channel_id=1, source_target_pairs={{0,8},{2,10},{4,12},{6,14},{8,0},{10,2},{12,4},{14,6},{16,24},{18,... | collective-permute-start | bytes 49160 | tf_op jit(solution)/shard_map/ppermute | solution.py:30
  8.7 2.2 %collective-permute-done.1 = bf16[2,4096]{1,0:T(2,128)(2,1)S(1)} collective-permute-done((bf16[2,4096]{1,0:T(2,128)(2,1)S(1)}, bf16[2,4096]{1,0:T(2,128)(2,1)S(1)}, u32[]{:S(2)}, u32[]{:S(2)}) %collective-permute-start.1) | collective-permute-done | bytes 16416 | tf_op jit(solution)/shard_map/ppermute | solution.py:30
  10.9 1.6 %collective-permute-start.2 = (bf16[4,4096]{1,0:T(4,128)(2,1)S(1)}, bf16[4,4096]{1,0:T(4,128)(2,1)S(1)}, u32[]{:S(2)}, u32[]{:S(2)}) collective-permute-start(bf16[4,4096]{1,0:T(4,128)(2,1)S(1)} %pad_maximum_fusion.1), channel_id=1, source_target_pairs={{0,4},{2,6},{4,0},{6,2},{8,12},{10,14},{12,8},{14,10},{16,20},{18,... | collective-permute-start | bytes 98312 | tf_op jit(solution)/shard_map/ppermute | solution.py:30
  12.5 2.4 %collective-permute-done.2 = bf16[4,4096]{1,0:T(4,128)(2,1)S(1)} collective-permute-done((bf16[4,4096]{1,0:T(4,128)(2,1)S(1)}, bf16[4,4096]{1,0:T(4,128)(2,1)S(1)}, u32[]{:S(2)}, u32[]{:S(2)}) %collective-permute-start.2) | collective-permute-done | bytes 32800 | tf_op jit(solution)/shard_map/ppermute | solution.py:30
  15.0 1.6 %collective-permute-start.3 = (bf16[8,4096]{1,0:T(8,128)(2,1)S(1)}, bf16[8,4096]{1,0:T(8,128)(2,1)S(1)}, u32[]{:S(2)}, u32[]{:S(2)}) collective-permute-start(bf16[8,4096]{1,0:T(8,128)(2,1)S(1)} %pad_maximum_fusion.refs_0_), channel_id=1, source_target_pairs={{0,2},{2,0},{4,6},{6,4},{8,10},{10,8},{12,14},{14,12},{16,18},{18,... | collective-permute-start | bytes 196616 | tf_op jit(solution)/shard_map/ppermute | solution.py:30
  16.5 0.6 %columns.1 = (f32[2,8,128,128]{3,2,1,0:T(8,128)S(1)}, f32[2,8,128,128]{3,2,1,0:T(8,128)S(1)}) custom-call(f32[8,4,8]{2,1,0:T(4,128)S(1)} %copy-done.3, f32[8,4,8]{2,1,0:T(4,128)S(1)} %copy-done.4), custom_call_target="tpu_custom_call" | custom-call | tf_op jit(solution)/shard_map/columns/pallas_call | solution.py:352
  17.2 2.1 %collective-permute-done.3.refs_1_ = bf16[8,4096]{1,0:T(8,128)(2,1)S(1)} collective-permute-done((bf16[8,4096]{1,0:T(8,128)(2,1)S(1)}, bf16[8,4096]{1,0:T(8,128)(2,1)S(1)}, u32[]{:S(2)}, u32[]{:S(2)}) %collective-permute-start.3) | collective-permute-done | bytes 65568 | tf_op jit(solution)/shard_map/ppermute | solution.py:30
  19.3 4.1 %attend.1.refs_0_ = bf16[288,128]{1,0:T(8,128)(2,1)S(1)} custom-call(s32[8]{0:T(128)S(1)} %get-tuple-element.20.place_ref, s32[8]{0:T(128)S(1)} %get-tuple-element.21.live_ref, f32[2,8,128,128]{3,2,1,0:T(8,128)S(1)} %get-tuple-element.22.key_scale_ref, f32[2,8,128,128]{3,2,1,0:T(8,128)S(1)} %get-tuple-element.23.value_scale_ref, ...), custom_call_target="tpu_custom_call" | custom-call | flops 5000000000 | bytes 16777216 | tf_op jit(solution)/shard_map/attend/pallas_call | solution.py:377
  23.4 2.9 %collective-permute-start.6 = (bf16[288,128]{1,0:T(8,128)(2,1)S(1)}, bf16[288,128]{1,0:T(8,128)(2,1)S(1)}, u32[]{:S(2)}, u32[]{:S(2)}) collective-permute-start(bf16[288,128]{1,0:T(8,128)(2,1)S(1)} %attend.1.refs_0_), channel_id=1, source_target_pairs={{0,24},{2,26},{4,28},{6,30},{8,16},{10,18},{12,20},{14,22},{16,8},... | collective-permute-start | bytes 221192 | tf_op jit(solution)/shard_map/ppermute | solution.py:30
  26.4 1.3 %collective-permute-start.4 = (bf16[288,128]{1,0:T(8,128)(2,1)S(1)}, bf16[288,128]{1,0:T(8,128)(2,1)S(1)}, u32[]{:S(2)}, u32[]{:S(2)}) collective-permute-start(bf16[288,128]{1,0:T(8,128)(2,1)S(1)} %attend.1.refs_0_), channel_id=1, source_target_pairs={{0,8},{2,10},{4,12},{6,14},{8,0},{10,2},{12,4},{14,6},{16,24},{18,... | collective-permute-start | bytes 221192 | tf_op jit(solution)/shard_map/ppermute | solution.py:30
  27.8 1.8 %collective-permute-done.6.refs_3_ = bf16[288,128]{1,0:T(8,128)(2,1)S(1)} collective-permute-done((bf16[288,128]{1,0:T(8,128)(2,1)S(1)}, bf16[288,128]{1,0:T(8,128)(2,1)S(1)}, u32[]{:S(2)}, u32[]{:S(2)}) %collective-permute-start.6) | collective-permute-done | bytes 73760 | tf_op jit(solution)/shard_map/ppermute | solution.py:30
  29.6 2.0 %collective-permute-done.5.refs_2_ = bf16[288,128]{1,0:T(8,128)(2,1)S(1)} collective-permute-done((bf16[288,128]{1,0:T(8,128)(2,1)S(1)}, bf16[288,128]{1,0:T(8,128)(2,1)S(1)}, u32[]{:S(2)}, u32[]{:S(2)}) %collective-permute-start.5) | collective-permute-done | bytes 73760 | tf_op jit(solution)/shard_map/ppermute | solution.py:30
  31.6 1.3 %merge_slots.1.refs_0_ = bf16[544,128]{1,0:T(8,128)(2,1)S(1)} custom-call(s32[32]{0:T(128)S(1)} %get-tuple-element.19.owner_ref, bf16[288,128]{1,0:T(8,128)(2,1)S(1)} %attend.1.refs_0_, bf16[288,128]{1,0:T(8,128)(2,1)S(1)} %collective-permute-done.4.refs_1_, bf16[288,128]{1,0:T(8,128)(2,1)S(1)} %collective-permute-done.5.refs_2_, ...), custom_call_target="tpu_custom_call" | custom-call | flops 20000000000 | bytes 139264 | tf_op jit(solution)/shard_map/merge_slots/pallas_call | solution.py:413
  32.9 2.5 %collective-permute-start.9 = (bf16[544,128]{1,0:T(8,128)(2,1)S(1)}, bf16[544,128]{1,0:T(8,128)(2,1)S(1)}, u32[]{:S(2)}, u32[]{:S(2)}) collective-permute-start(bf16[544,128]{1,0:T(8,128)(2,1)S(1)} %merge_slots.1.refs_0_), channel_id=1, source_target_pairs={{0,6},{2,4},{4,2},{6,0},{8,14},{10,12},{12,10},{14,8},{16,22},{18,... | collective-permute-start | bytes 417800 | tf_op jit(solution)/shard_map/ppermute | solution.py:30
  35.4 0.5 %collective-permute-start.8 = (bf16[544,128]{1,0:T(8,128)(2,1)S(1)}, bf16[544,128]{1,0:T(8,128)(2,1)S(1)}, u32[]{:S(2)}, u32[]{:S(2)}) collective-permute-start(bf16[544,128]{1,0:T(8,128)(2,1)S(1)} %merge_slots.1.refs_0_), channel_id=1, source_target_pairs={{0,4},{2,6},{4,0},{6,2},{8,12},{10,14},{12,8},{14,10},{16,20},{18,... | collective-permute-start | bytes 417800 | tf_op jit(solution)/shard_map/ppermute | solution.py:30
  35.9 0.5 %collective-permute-start.7 = (bf16[544,128]{1,0:T(8,128)(2,1)S(1)}, bf16[544,128]{1,0:T(8,128)(2,1)S(1)}, u32[]{:S(2)}, u32[]{:S(2)}) collective-permute-start(bf16[544,128]{1,0:T(8,128)(2,1)S(1)} %merge_slots.1.refs_0_), channel_id=1, source_target_pairs={{0,2},{2,0},{4,6},{6,4},{8,10},{10,8},{12,14},{14,12},{16,18},{18,... | collective-permute-start | bytes 417800 | tf_op jit(solution)/shard_map/ppermute | solution.py:30
  36.4 2.5 %collective-permute-done.9.refs_3_ = bf16[544,128]{1,0:T(8,128)(2,1)S(1)} collective-permute-done((bf16[544,128]{1,0:T(8,128)(2,1)S(1)}, bf16[544,128]{1,0:T(8,128)(2,1)S(1)}, u32[]{:S(2)}, u32[]{:S(2)}) %collective-permute-start.9) | collective-permute-done | bytes 139296 | tf_op jit(solution)/shard_map/ppermute | solution.py:30
  38.9 1.5 %collective-permute-done.8.refs_2_ = bf16[544,128]{1,0:T(8,128)(2,1)S(1)} collective-permute-done((bf16[544,128]{1,0:T(8,128)(2,1)S(1)}, bf16[544,128]{1,0:T(8,128)(2,1)S(1)}, u32[]{:S(2)}, u32[]{:S(2)}) %collective-permute-start.8) | collective-permute-done | bytes 139296 | tf_op jit(solution)/shard_map/ppermute | solution.py:30
  41.0 1.1 %project.1 = (f32[8,512]{1,0:T(8,128)S(1)}, f32[8,512]{1,0:T(8,128)S(1)}) custom-call(bf16[544,128]{1,0:T(8,128)(2,1)S(1)} %merge_slots.1.refs_0_, bf16[544,128]{1,0:T(8,128)(2,1)S(1)} %collective-permute-done.7.refs_1_, bf16[544,128]{1,0:T(8,128)(2,1)S(1)} %collective-permute-done.8.refs_2_, bf16[544,128]{1,0:T(8,128)(2,1)S(1)} %collective-permute-done.9.refs_3_, ...), custom_call_target="tpu_custom_call" | custom-call | tf_op jit(solution)/shard_map/project/pallas_call | solution.py:440
  42.1 1.2 %collective-permute-done.10 = f32[8,512]{1,0:T(8,128)S(1)} collective-permute-done((f32[8,512]{1,0:T(8,128)S(1)}, f32[8,512]{1,0:T(8,128)S(1)}, u32[]{:S(2)}, u32[]{:S(2)}) %collective-permute-start.10) | collective-permute-done | bytes 16416 | tf_op jit(solution)/shard_map/ppermute | solution.py:450
  43.3 0.6 %add_convert_fusion = bf16[8,512]{1,0:T(8,128)(2,1)} fusion(f32[8,512]{1,0:T(8,128)S(1)} %get-tuple-element.25, f32[8,512]{1,0:T(8,128)S(1)} %collective-permute-done.10), kind=kLoop, calls=%fused_computation.3 | loop fusion | flops 8192 | bytes 40960 | tf_op jit(solution)/shard_map/convert_element_type | solution.py:453
  (20 shorter events, 0.8 us)
Async XLA Ops:
  0.0 7.0 %collective-permute-start = (bf16[1,4096]{1,0:T(2,128)(2,1)}, bf16[1,4096]{1,0:T(2,128)(2,1)S(1)}, u32[]{:S(2)}, u32[]{:S(2)}) collective-permute-start(bf16[1,4096]{1,0:T(2,128)(2,1)} %param.9), channel_id=1, source_target_pairs={{0,16},{2,18},{4,20},{6,22},{8,24},{10,26},{12,28},{14,30},{16,0},... | collective-permute-start | bytes 24584 | tf_op jit(solution)/shard_map/ppermute | solution.py:30
  4.8 2.2 %copy-start.5 = (bf16[1,4096]{1,0:T(2,128)(2,1)S(1)}, bf16[1,4096]{1,0:T(2,128)(2,1)}, u32[]{:S(2)}) copy-start(bf16[1,4096]{1,0:T(2,128)(2,1)} %param.9) | copy-start | bytes 24580
  4.8 11.7 %copy-start.3 = (f32[8,4,8]{2,1,0:T(4,128)S(1)}, f32[8,4,8]{2,1,0:T(4,128)}, u32[]{:S(2)}) copy-start(f32[8,4,8]{2,1,0:T(4,128)} %refs_0_.1) | copy-start | bytes 3076
  4.8 11.7 %copy-start.4 = (f32[8,4,8]{2,1,0:T(4,128)S(1)}, f32[8,4,8]{2,1,0:T(4,128)}, u32[]{:S(2)}) copy-start(f32[8,4,8]{2,1,0:T(4,128)} %refs_1_.1) | copy-start | bytes 3076
  4.8 14.5 %copy-start = (bf16[8,4,1024,128]{3,2,1,0:T(8,128)(2,1)S(1)}, bf16[8,4,1024,128]{3,2,1,0:T(8,128)(2,1)}, u32[]{:S(2)}) copy-start(bf16[8,4,1024,128]{3,2,1,0:T(8,128)(2,1)} %refs_2_.1) | copy-start | bytes 25165828
  4.8 14.5 %copy-start.1 = (bf16[8,4,1024,128]{3,2,1,0:T(8,128)(2,1)S(1)}, bf16[8,4,1024,128]{3,2,1,0:T(8,128)(2,1)}, u32[]{:S(2)}) copy-start(bf16[8,4,1024,128]{3,2,1,0:T(8,128)(2,1)} %refs_3_.1) | copy-start | bytes 25165828
  7.1 3.8 %collective-permute-start.1 = (bf16[2,4096]{1,0:T(2,128)(2,1)S(1)}, bf16[2,4096]{1,0:T(2,128)(2,1)S(1)}, u32[]{:S(2)}, u32[]{:S(2)}) collective-permute-start(bf16[2,4096]{1,0:T(2,128)(2,1)S(1)} %pad_maximum_fusion.2), channel_id=1, source_target_pairs={{0,8},{2,10},{4,12},{6,14},{8,0},{10,2},{12,4},{14,6},{16,24},{18,... | collective-permute-start | bytes 49160 | tf_op jit(solution)/shard_map/ppermute | solution.py:30
  10.9 4.0 %collective-permute-start.2 = (bf16[4,4096]{1,0:T(4,128)(2,1)S(1)}, bf16[4,4096]{1,0:T(4,128)(2,1)S(1)}, u32[]{:S(2)}, u32[]{:S(2)}) collective-permute-start(bf16[4,4096]{1,0:T(4,128)(2,1)S(1)} %pad_maximum_fusion.1), channel_id=1, source_target_pairs={{0,4},{2,6},{4,0},{6,2},{8,12},{10,14},{12,8},{14,10},{16,20},{18,... | collective-permute-start | bytes 98312 | tf_op jit(solution)/shard_map/ppermute | solution.py:30
  15.0 4.3 %collective-permute-start.3 = (bf16[8,4096]{1,0:T(8,128)(2,1)S(1)}, bf16[8,4096]{1,0:T(8,128)(2,1)S(1)}, u32[]{:S(2)}, u32[]{:S(2)}) collective-permute-start(bf16[8,4096]{1,0:T(8,128)(2,1)S(1)} %pad_maximum_fusion.refs_0_), channel_id=1, source_target_pairs={{0,2},{2,0},{4,6},{6,4},{8,10},{10,8},{12,14},{14,12},{16,18},{18,... | collective-permute-start | bytes 196616 | tf_op jit(solution)/shard_map/ppermute | solution.py:30
  23.4 17.6 %copy-start.2 = (bf16[4096,512]{1,0:T(8,128)(2,1)S(1)}, bf16[4096,512]{1,0:T(8,128)(2,1)}, u32[]{:S(2)}) copy-start(bf16[4096,512]{1,0:T(8,128)(2,1)} %refs_4_.1) | copy-start | bytes 12582916
  23.4 6.2 %collective-permute-start.6 = (bf16[288,128]{1,0:T(8,128)(2,1)S(1)}, bf16[288,128]{1,0:T(8,128)(2,1)S(1)}, u32[]{:S(2)}, u32[]{:S(2)}) collective-permute-start(bf16[288,128]{1,0:T(8,128)(2,1)S(1)} %attend.1.refs_0_), channel_id=1, source_target_pairs={{0,24},{2,26},{4,28},{6,30},{8,16},{10,18},{12,20},{14,22},{16,8},... | collective-permute-start | bytes 221192 | tf_op jit(solution)/shard_map/ppermute | solution.py:30
  26.3 5.3 %collective-permute-start.5 = (bf16[288,128]{1,0:T(8,128)(2,1)S(1)}, bf16[288,128]{1,0:T(8,128)(2,1)S(1)}, u32[]{:S(2)}, u32[]{:S(2)}) collective-permute-start(bf16[288,128]{1,0:T(8,128)(2,1)S(1)} %attend.1.refs_0_), channel_id=1, source_target_pairs={{0,16},{2,18},{4,20},{6,22},{8,24},{10,26},{12,28},{14,30},{16,0},... | collective-permute-start | bytes 221192 | tf_op jit(solution)/shard_map/ppermute | solution.py:30
  26.4 5.1 %collective-permute-start.4 = (bf16[288,128]{1,0:T(8,128)(2,1)S(1)}, bf16[288,128]{1,0:T(8,128)(2,1)S(1)}, u32[]{:S(2)}, u32[]{:S(2)}) collective-permute-start(bf16[288,128]{1,0:T(8,128)(2,1)S(1)} %attend.1.refs_0_), channel_id=1, source_target_pairs={{0,8},{2,10},{4,12},{6,14},{8,0},{10,2},{12,4},{14,6},{16,24},{18,... | collective-permute-start | bytes 221192 | tf_op jit(solution)/shard_map/ppermute | solution.py:30
  32.9 6.0 %collective-permute-start.9 = (bf16[544,128]{1,0:T(8,128)(2,1)S(1)}, bf16[544,128]{1,0:T(8,128)(2,1)S(1)}, u32[]{:S(2)}, u32[]{:S(2)}) collective-permute-start(bf16[544,128]{1,0:T(8,128)(2,1)S(1)} %merge_slots.1.refs_0_), channel_id=1, source_target_pairs={{0,6},{2,4},{4,2},{6,0},{8,14},{10,12},{12,10},{14,8},{16,22},{18,... | collective-permute-start | bytes 417800 | tf_op jit(solution)/shard_map/ppermute | solution.py:30
  35.4 5.1 %collective-permute-start.8 = (bf16[544,128]{1,0:T(8,128)(2,1)S(1)}, bf16[544,128]{1,0:T(8,128)(2,1)S(1)}, u32[]{:S(2)}, u32[]{:S(2)}) collective-permute-start(bf16[544,128]{1,0:T(8,128)(2,1)S(1)} %merge_slots.1.refs_0_), channel_id=1, source_target_pairs={{0,4},{2,6},{4,0},{6,2},{8,12},{10,14},{12,8},{14,10},{16,20},{18,... | collective-permute-start | bytes 417800 | tf_op jit(solution)/shard_map/ppermute | solution.py:30
  35.9 5.1 %collective-permute-start.7 = (bf16[544,128]{1,0:T(8,128)(2,1)S(1)}, bf16[544,128]{1,0:T(8,128)(2,1)S(1)}, u32[]{:S(2)}, u32[]{:S(2)}) collective-permute-start(bf16[544,128]{1,0:T(8,128)(2,1)S(1)} %merge_slots.1.refs_0_), channel_id=1, source_target_pairs={{0,2},{2,0},{4,6},{6,4},{8,10},{10,8},{12,14},{14,12},{16,18},{18,... | collective-permute-start | bytes 417800 | tf_op jit(solution)/shard_map/ppermute | solution.py:30
  42.1 1.2 %collective-permute-start.10 = (f32[8,512]{1,0:T(8,128)S(1)}, f32[8,512]{1,0:T(8,128)S(1)}, u32[]{:S(2)}, u32[]{:S(2)}) collective-permute-start(f32[8,512]{1,0:T(8,128)S(1)} %get-tuple-element.26), channel_id=1, source_target_pairs={{0,1},{1,0},{2,3},{3,2},{4,5},{5,4},{6,7},{7,6},{8,9},{9,8},{10,11... | collective-permute-start | bytes 49160 | tf_op jit(solution)/shard_map/ppermute | solution.py:450

commit v4 on v3

--- a/solution.py
+++ b/solution.py
@@ -17,13 +17,22 @@
 SMEM = pl.BlockSpec(memory_space=pltpu.SMEM)
 
 
-def exchange_rounds(devices, most):
-    rounds, width = [], devices
-    while width > 1:
-        radix = most if width % most == 0 else 2
-        width //= radix
-        rounds.append([width * k for k in range(1, radix)])
-    return rounds
+def exchange_masks(bits):
+    masks = [0]
+    for bit in bits:
+        masks += [mask + bit for mask in masks]
+    return masks[1:]
+
+
+def spread_rounds(devices):
+    bits = [1 << k for k in range(devices.bit_length() - 1)]
+    return [[bit] for bit in reversed(bits[2:])] + [bits[:2]]
+
+
+def merge_rounds(devices):
+    bits = [1 << k for k in range(devices.bit_length() - 1)]
+    pairs = [[bits[k], bits[-1 - k]] for k in range(len(bits) // 2)]
+    return pairs + ([[bits[len(bits) // 2]]] if len(bits) % 2 else [])
 
 
 def partner(value, mask, devices):
@@ -79,7 +88,7 @@
 
 
 def locate_kernel(
-    rounds, near, slots, rows, all_slots, own_rows, tokens,
+    bits, near, slots, rows, all_slots, own_rows, tokens,
     table_ref, place_ref, live_ref, owner_ref, position_of, first_of,
 ):
     me = lax.axis_index("page")
@@ -106,10 +115,9 @@
             if index == 0:
                 away = jnp.bitwise_xor(row // own_rows, me)
                 place, step_size = row % own_rows, own_rows
-                for masks in rounds:
-                    radix = len(masks) + 1
-                    place += away // masks[0] % radix * step_size
-                    step_size *= radix
+                for bit in bits:
+                    place += away // bit % 2 * step_size
+                    step_size *= 2
                 place_ref[slot] = place
                 before = position - first_of[row]
                 live_ref[slot] = (table_ref[row] - 1 - before) * tokens + table_ref[fills + row]
@@ -149,7 +157,7 @@
                 :, head * LANES : (head + 1) * LANES
             ]
     together = 2 if kv_heads % 2 == 0 else 1
-    each = min(slots, LANES // heads)
+    each = slots // key_scale_ref.shape[0]
     rows = together * group
     lane = lane_index((heads, LANES))
     token = lane_index((heads, page_tokens))
@@ -162,7 +170,7 @@
             return ref[slot, kv]
         return jnp.concatenate([ref[slot, kv], ref[slot, kv + 1]], axis=1)
 
-    for batch in range(slots // each):
+    def products(batch):
         dotted = []
         for index in range(each):
             slot = batch * each + index
@@ -182,7 +190,9 @@
                         preferred_element_type=jnp.float32,
                     )
                 )
-        dotted = jnp.concatenate(dotted, axis=0)
+        return jnp.concatenate(dotted, axis=0)
+
+    def softmax(batch, dotted):
         scores = []
         for page in range(pages):
             part = dotted[:, page * page_tokens : (page + 1) * page_tokens]
@@ -200,9 +210,9 @@
             total = expon if total is None else total + expon
             weights.append((expon * value_scale_ref[batch, page]).astype(jnp.bfloat16))
         total = jnp.sum(total, axis=1, keepdims=True)
-        weights = jnp.concatenate(weights, axis=1)
-        scale = 1.0 / total
-        log = peak + jnp.log(total)
+        return jnp.concatenate(weights, axis=1), 1.0 / total, peak + jnp.log(total)
+
+    def sums(batch, weights, scale):
         for index in range(each):
             slot = batch * each + index
             for kv in range(0, kv_heads, together):
@@ -218,7 +228,18 @@
                     )
                 at = slot * heads + kv * group
                 outs[at : at + rows, :] = partial * scale[first : first + rows]
+
+    batches = key_scale_ref.shape[0]
+    ready = products(0)
+    for batch in range(batches):
+        following = products(batch + 1) if batch + 1 < batches else None
+        weights, scale, log = softmax(batch, ready)
+        sums(batch, weights, scale)
+        ready = following
+        for index in range(each):
+            slot = batch * each + index
             logs = jnp.where(lane == slot, log[index * heads : (index + 1) * heads], logs)
+
     out_ref[: slots * heads, :] = outs[...].astype(jnp.bfloat16)
     store_stats(out_ref, slots * heads, logs, slots, heads)
 
@@ -324,15 +345,15 @@
     group = heads // kv_heads
     own_rows = query.shape[0]
     columns = out_weight.shape[1]
-    spread = exchange_rounds(devices, 2)
-    rounds = exchange_rounds(devices, 4)
+    spread = spread_rounds(devices)
+    rounds = [exchange_masks(bits) for bits in merge_rounds(devices)]
 
     near = [0] + rounds[0]
     tables = jnp.concatenate([range_counts, last_fill, slot_table])
     own_slots = jax.ShapeDtypeStruct((slots,), jnp.int32)
     place, live, owner = pl.pallas_call(
         functools.partial(
-            locate_kernel, spread, near, slots, rows, all_slots, own_rows, tokens
+            locate_kernel, sum(spread, []), near, slots, rows, all_slots, own_rows, tokens
         ),
         out_shape=[own_slots, own_slots, jax.ShapeDtypeStruct((len(near) * slots,), jnp.int32)],
         in_specs=[SMEM],
@@ -348,7 +369,7 @@
         name="locate",
     )(tables)
 
-    batches = slots // min(slots, LANES // heads)
+    batches = slots // 2 if slots % 2 == 0 else slots
     scales = pl.pallas_call(
         functools.partial(columns_kernel, group, head_dim**-0.5),
         out_shape=[
@@ -364,13 +385,13 @@
     )(key_scale, value_scale)
 
     held = [query]
-    for turn, masks in enumerate(spread):
+    for turn, bits in enumerate(spread):
         block = jnp.concatenate(held, axis=0) if len(held) > 1 else held[0]
         if turn == 1:
             block, place, live, owner = lax.optimization_barrier((block, place, live, owner))
         elif turn > 1:
             block = lax.optimization_barrier(block)
-        held = [block] + [partner(block, mask, devices) for mask in masks]
+        held = [block] + [partner(block, mask, devices) for mask in exchange_masks(bits)]
 
     payload = (slots + stat_blocks(slots)) * heads
     held = [

time: 44 us -> 41.9 us (0.952)
  waiting for transfers between devices: 16.2 us -> 13.3 us
  starting transfers between devices: 16.8 us -> 17.5 us
    ppermute x10 -> x11, waiting for transfers between devices: 15 us -> 12.1 us  [partner(): return lax.ppermute(value, 'page', [(i, i ^ mask) for i in range(devices)])]
    ppermute x10 -> x11, starting transfers between devices: 16.8 us -> 17.5 us  [partner(): return lax.ppermute(value, 'page', [(i, i ^ mask) for i in range(devices)])]
  transfers between devices with their start and end apart: 11 -> 12, of which waited for: 9 -> 10; matrix products, arithmetic and copies ran while one was open for 2% -> 2% of each run, Pallas kernels for 6% -> 7%
where the time goes in v4:
time: 41.9 us; the launch traced here: 41.8 us
  starting transfers between devices  17.5 us (42%)
  waiting for transfers between devices  13.3 us (32%)
  Pallas kernels  9.37 us (22%)
  other arithmetic  1.45 us (3%)
    ppermute x11, starting transfers between devices, partner(): return lax.ppermute(value, 'page', [(i, i ^ mask) for i in range(devices)])  17.5 us
    ppermute x11, waiting for transfers between devices, partner(): return lax.ppermute(value, 'page', [(i, i ^ mask) for i in range(devices)])  12.1 us
    pallas_call x1, Pallas kernels, per_device(): pl.pallas_call(functools.partial(attend_kernel, len(held), slots, kv_head...  4.07 us
    pallas_call x1, Pallas kernels, per_device(): pl.pallas_call(functools.partial(locate_kernel, sum(spread, []), near, sl...  2.19 us
    pallas_call x1, Pallas kernels, per_device(): pl.pallas_call(functools.partial(merge_slots_kernel, groups, slots, rows,...  1.28 us
    ppermute x1, waiting for transfers between devices, per_device(): mixed = mixed + lax.ppermute(give[0], 'head', [(0, 1), (1, 0)])  1.19 us
    pallas_call x1, Pallas kernels, per_device(): pl.pallas_call(functools.partial(project_kernel, len(held), rows, heads,...  1.13 us
  transfers between devices with their start and end apart: 12, of which 10 were waited for; matrix products, arithmetic and copies ran while one was open for 2% of the time, Pallas kernels for 7%

profile of v4, /device:TPU:0, one launch (start us, length us, event | category | flops | bytes accessed | tf_op | source)
XLA Modules:
  0.0 41.8 jit_solution(10588929347679282916)
XLA Ops:
  0.0 4.0 %collective-permute-start = (bf16[1,4096]{1,0:T(2,128)(2,1)}, bf16[1,4096]{1,0:T(2,128)(2,1)S(1)}, u32[]{:S(2)}, u32[]{:S(2)}) collective-permute-start(bf16[1,4096]{1,0:T(2,128)(2,1)} %param.9), channel_id=1, source_target_pairs={{0,16},{2,18},{4,20},{6,22},{8,24},{10,26},{12,28},{14,30},{16,0},... | collective-permute-start | bytes 24584 | tf_op jit(solution)/shard_map/ppermute | solution.py:39
  4.0 0.8 %pad_add_fusion.table_ref = s32[160]{0:T(256)S(1)} fusion(s32[128]{0:T(128)} %param.17, s32[16]{0:T(128)} %param.16, s32[16]{0:T(128)} %param.15), kind=kLoop, calls=%fused_computation.3 | loop fusion | flops 320 | bytes 1280 | tf_op jit(solution)/shard_map/concatenate | solution.py:352
  4.8 2.2 %locate.1 = (s32[8]{0:T(128)S(1)}, s32[8]{0:T(128)S(1)}, s32[32]{0:T(128)S(1)}) custom-call(s32[160]{0:T(256)S(1)} %pad_add_fusion.table_ref), custom_call_target="tpu_custom_call" | custom-call | flops 20000000000 | bytes 512 | tf_op jit(solution)/shard_map/locate/pallas_call | solution.py:354
  7.1 1.6 %collective-permute-start.1 = (bf16[2,4096]{1,0:T(2,128)(2,1)S(1)}, bf16[2,4096]{1,0:T(2,128)(2,1)S(1)}, u32[]{:S(2)}, u32[]{:S(2)}) collective-permute-start(bf16[2,4096]{1,0:T(2,128)(2,1)S(1)} %pad_maximum_fusion.1), channel_id=1, source_target_pairs={{0,8},{2,10},{4,12},{6,14},{8,0},{10,2},{12,4},{14,6},{16,24},{18,... | collective-permute-start | bytes 49160 | tf_op jit(solution)/shard_map/ppermute | solution.py:39
  8.7 2.2 %collective-permute-done.1 = bf16[2,4096]{1,0:T(2,128)(2,1)S(1)} collective-permute-done((bf16[2,4096]{1,0:T(2,128)(2,1)S(1)}, bf16[2,4096]{1,0:T(2,128)(2,1)S(1)}, u32[]{:S(2)}, u32[]{:S(2)}) %collective-permute-start.1) | collective-permute-done | bytes 16416 | tf_op jit(solution)/shard_map/ppermute | solution.py:39
  11.0 2.5 %collective-permute-start.4 = (bf16[4,4096]{1,0:T(4,128)(2,1)S(1)}, bf16[4,4096]{1,0:T(4,128)(2,1)S(1)}, u32[]{:S(2)}, u32[]{:S(2)}) collective-permute-start(bf16[4,4096]{1,0:T(4,128)(2,1)S(1)} %pad_maximum_fusion.refs_0_), channel_id=1, source_target_pairs={{0,6},{2,4},{4,2},{6,0},{8,14},{10,12},{12,10},{14,8},{16,22},{18,... | collective-permute-start | bytes 98312 | tf_op jit(solution)/shard_map/ppermute | solution.py:39
  14.0 0.5 %collective-permute-start.2 = (bf16[4,4096]{1,0:T(4,128)(2,1)S(1)}, bf16[4,4096]{1,0:T(4,128)(2,1)S(1)}, u32[]{:S(2)}, u32[]{:S(2)}) collective-permute-start(bf16[4,4096]{1,0:T(4,128)(2,1)S(1)} %pad_maximum_fusion.refs_0_), channel_id=1, source_target_pairs={{0,2},{2,0},{4,6},{6,4},{8,10},{10,8},{12,14},{14,12},{16,18},{18,... | collective-permute-start | bytes 98312 | tf_op jit(solution)/shard_map/ppermute | solution.py:39
  14.5 0.7 %columns.1 = (f32[4,8,64,128]{3,2,1,0:T(8,128)S(1)}, f32[4,8,64,128]{3,2,1,0:T(8,128)S(1)}) custom-call(f32[8,4,8]{2,1,0:T(4,128)S(1)} %copy-done.3, f32[8,4,8]{2,1,0:T(4,128)S(1)} %copy-done.4), custom_call_target="tpu_custom_call" | custom-call | tf_op jit(solution)/shard_map/columns/pallas_call | solution.py:373
  15.2 0.9 %collective-permute-done.4.refs_3_ = bf16[4,4096]{1,0:T(4,128)(2,1)S(1)} collective-permute-done((bf16[4,4096]{1,0:T(4,128)(2,1)S(1)}, bf16[4,4096]{1,0:T(4,128)(2,1)S(1)}, u32[]{:S(2)}, u32[]{:S(2)}) %collective-permute-start.4) | collective-permute-done | bytes 32800 | tf_op jit(solution)/shard_map/ppermute | solution.py:39
  16.1 1.3 %collective-permute-done.3.refs_2_ = bf16[4,4096]{1,0:T(4,128)(2,1)S(1)} collective-permute-done((bf16[4,4096]{1,0:T(4,128)(2,1)S(1)}, bf16[4,4096]{1,0:T(4,128)(2,1)S(1)}, u32[]{:S(2)}, u32[]{:S(2)}) %collective-permute-start.3) | collective-permute-done | bytes 32800 | tf_op jit(solution)/shard_map/ppermute | solution.py:39
  17.9 4.1 %attend.1.refs_0_ = bf16[288,128]{1,0:T(8,128)(2,1)S(1)} custom-call(s32[8]{0:T(128)S(1)} %get-tuple-element.20.place_ref, s32[8]{0:T(128)S(1)} %get-tuple-element.21.live_ref, f32[4,8,64,128]{3,2,1,0:T(8,128)S(1)} %get-tuple-element.22.key_scale_ref, f32[4,8,64,128]{3,2,1,0:T(8,128)S(1)} %get-tuple-element.23.value_scale_ref, ...), custom_call_target="tpu_custom_call" | custom-call | flops 5000000000 | bytes 16777216 | tf_op jit(solution)/shard_map/attend/pallas_call | solution.py:398
  22.0 1.8 %collective-permute-start.7 = (bf16[288,128]{1,0:T(8,128)(2,1)S(1)}, bf16[288,128]{1,0:T(8,128)(2,1)S(1)}, u32[]{:S(2)}, u32[]{:S(2)}) collective-permute-start(bf16[288,128]{1,0:T(8,128)(2,1)S(1)} %attend.1.refs_0_), channel_id=1, source_target_pairs={{0,18},{2,16},{4,22},{6,20},{8,26},{10,24},{12,30},{14,28},{16,2},... | collective-permute-start | bytes 221192 | tf_op jit(solution)/shard_map/ppermute | solution.py:39
  23.8 1.1 %collective-permute-start.6 = (bf16[288,128]{1,0:T(8,128)(2,1)S(1)}, bf16[288,128]{1,0:T(8,128)(2,1)S(1)}, u32[]{:S(2)}, u32[]{:S(2)}) collective-permute-start(bf16[288,128]{1,0:T(8,128)(2,1)S(1)} %attend.1.refs_0_), channel_id=1, source_target_pairs={{0,16},{2,18},{4,20},{6,22},{8,24},{10,26},{12,28},{14,30},{16,0},... | collective-permute-start | bytes 221192 | tf_op jit(solution)/shard_map/ppermute | solution.py:39
  24.9 1.5 %collective-permute-start.5 = (bf16[288,128]{1,0:T(8,128)(2,1)S(1)}, bf16[288,128]{1,0:T(8,128)(2,1)S(1)}, u32[]{:S(2)}, u32[]{:S(2)}) collective-permute-start(bf16[288,128]{1,0:T(8,128)(2,1)S(1)} %attend.1.refs_0_), channel_id=1, source_target_pairs={{0,2},{2,0},{4,6},{6,4},{8,10},{10,8},{12,14},{14,12},{16,18},{18,... | collective-permute-start | bytes 221192 | tf_op jit(solution)/shard_map/ppermute | solution.py:39
  26.4 1.8 %collective-permute-done.7.refs_3_ = bf16[288,128]{1,0:T(8,128)(2,1)S(1)} collective-permute-done((bf16[288,128]{1,0:T(8,128)(2,1)S(1)}, bf16[288,128]{1,0:T(8,128)(2,1)S(1)}, u32[]{:S(2)}, u32[]{:S(2)}) %collective-permute-start.7) | collective-permute-done | bytes 73760 | tf_op jit(solution)/shard_map/ppermute | solution.py:39
  28.1 0.9 %collective-permute-done.6.refs_2_ = bf16[288,128]{1,0:T(8,128)(2,1)S(1)} collective-permute-done((bf16[288,128]{1,0:T(8,128)(2,1)S(1)}, bf16[288,128]{1,0:T(8,128)(2,1)S(1)}, u32[]{:S(2)}, u32[]{:S(2)}) %collective-permute-start.6) | collective-permute-done | bytes 73760 | tf_op jit(solution)/shard_map/ppermute | solution.py:39
  29.2 1.3 %merge_slots.1.refs_0_ = bf16[544,128]{1,0:T(8,128)(2,1)S(1)} custom-call(s32[32]{0:T(128)S(1)} %get-tuple-element.19.owner_ref, bf16[288,128]{1,0:T(8,128)(2,1)S(1)} %attend.1.refs_0_, bf16[288,128]{1,0:T(8,128)(2,1)S(1)} %collective-permute-done.5.refs_1_, bf16[288,128]{1,0:T(8,128)(2,1)S(1)} %collective-permute-done.6.refs_2_, ...), custom_call_target="tpu_custom_call" | custom-call | flops 20000000000 | bytes 139264 | tf_op jit(solution)/shard_map/merge_slots/pallas_call | solution.py:434
  30.5 3.3 %collective-permute-start.10 = (bf16[544,128]{1,0:T(8,128)(2,1)S(1)}, bf16[544,128]{1,0:T(8,128)(2,1)S(1)}, u32[]{:S(2)}, u32[]{:S(2)}) collective-permute-start(bf16[544,128]{1,0:T(8,128)(2,1)S(1)} %merge_slots.1.refs_0_), channel_id=1, source_target_pairs={{0,12},{2,14},{4,8},{6,10},{8,4},{10,6},{12,0},{14,2},{16,28},{18,... | collective-permute-start | bytes 417800 | tf_op jit(solution)/shard_map/ppermute | solution.py:39
  33.8 0.6 %collective-permute-start.8 = (bf16[544,128]{1,0:T(8,128)(2,1)S(1)}, bf16[544,128]{1,0:T(8,128)(2,1)S(1)}, u32[]{:S(2)}, u32[]{:S(2)}) collective-permute-start(bf16[544,128]{1,0:T(8,128)(2,1)S(1)} %merge_slots.1.refs_0_), channel_id=1, source_target_pairs={{0,4},{2,6},{4,0},{6,2},{8,12},{10,14},{12,8},{14,10},{16,20},{18,... | collective-permute-start | bytes 417800 | tf_op jit(solution)/shard_map/ppermute | solution.py:39
  34.4 2.4 %collective-permute-done.10.refs_3_ = bf16[544,128]{1,0:T(8,128)(2,1)S(1)} collective-permute-done((bf16[544,128]{1,0:T(8,128)(2,1)S(1)}, bf16[544,128]{1,0:T(8,128)(2,1)S(1)}, u32[]{:S(2)}, u32[]{:S(2)}) %collective-permute-start.10) | collective-permute-done | bytes 139296 | tf_op jit(solution)/shard_map/ppermute | solution.py:39
  36.8 2.0 %collective-permute-done.9.refs_2_ = bf16[544,128]{1,0:T(8,128)(2,1)S(1)} collective-permute-done((bf16[544,128]{1,0:T(8,128)(2,1)S(1)}, bf16[544,128]{1,0:T(8,128)(2,1)S(1)}, u32[]{:S(2)}, u32[]{:S(2)}) %collective-permute-start.9) | collective-permute-done | bytes 139296 | tf_op jit(solution)/shard_map/ppermute | solution.py:39
  38.9 1.1 %project.1 = (f32[8,512]{1,0:T(8,128)S(1)}, f32[8,512]{1,0:T(8,128)S(1)}) custom-call(bf16[544,128]{1,0:T(8,128)(2,1)S(1)} %merge_slots.1.refs_0_, bf16[544,128]{1,0:T(8,128)(2,1)S(1)} %collective-permute-done.8.refs_1_, bf16[544,128]{1,0:T(8,128)(2,1)S(1)} %collective-permute-done.9.refs_2_, bf16[544,128]{1,0:T(8,128)(2,1)S(1)} %collective-permute-done.10.refs_3_, ...), custom_call_target="tpu_custom_call" | custom-call | tf_op jit(solution)/shard_map/project/pallas_call | solution.py:461
  40.0 1.2 %collective-permute-done.11 = f32[8,512]{1,0:T(8,128)S(1)} collective-permute-done((f32[8,512]{1,0:T(8,128)S(1)}, f32[8,512]{1,0:T(8,128)S(1)}, u32[]{:S(2)}, u32[]{:S(2)}) %collective-permute-start.11) | collective-permute-done | bytes 16416 | tf_op jit(solution)/shard_map/ppermute | solution.py:471
  41.2 0.6 %add_convert_fusion = bf16[8,512]{1,0:T(8,128)(2,1)} fusion(f32[8,512]{1,0:T(8,128)S(1)} %get-tuple-element.25, f32[8,512]{1,0:T(8,128)S(1)} %collective-permute-done.11), kind=kLoop, calls=%fused_computation.2 | loop fusion | flops 8192 | bytes 40960 | tf_op jit(solution)/shard_map/convert_element_type | solution.py:474
  (21 shorter events, 1.3 us)
Async XLA Ops:
  0.0 7.0 %collective-permute-start = (bf16[1,4096]{1,0:T(2,128)(2,1)}, bf16[1,4096]{1,0:T(2,128)(2,1)S(1)}, u32[]{:S(2)}, u32[]{:S(2)}) collective-permute-start(bf16[1,4096]{1,0:T(2,128)(2,1)} %param.9), channel_id=1, source_target_pairs={{0,16},{2,18},{4,20},{6,22},{8,24},{10,26},{12,28},{14,30},{16,0},... | collective-permute-start | bytes 24584 | tf_op jit(solution)/shard_map/ppermute | solution.py:39
  4.8 2.2 %copy-start.5 = (bf16[1,4096]{1,0:T(2,128)(2,1)S(1)}, bf16[1,4096]{1,0:T(2,128)(2,1)}, u32[]{:S(2)}) copy-start(bf16[1,4096]{1,0:T(2,128)(2,1)} %param.9) | copy-start | bytes 24580
  4.8 9.7 %copy-start.3 = (f32[8,4,8]{2,1,0:T(4,128)S(1)}, f32[8,4,8]{2,1,0:T(4,128)}, u32[]{:S(2)}) copy-start(f32[8,4,8]{2,1,0:T(4,128)} %refs_0_.1) | copy-start | bytes 3076
  4.8 9.7 %copy-start.4 = (f32[8,4,8]{2,1,0:T(4,128)S(1)}, f32[8,4,8]{2,1,0:T(4,128)}, u32[]{:S(2)}) copy-start(f32[8,4,8]{2,1,0:T(4,128)} %refs_1_.1) | copy-start | bytes 3076
  4.8 13.1 %copy-start = (bf16[8,4,1024,128]{3,2,1,0:T(8,128)(2,1)S(1)}, bf16[8,4,1024,128]{3,2,1,0:T(8,128)(2,1)}, u32[]{:S(2)}) copy-start(bf16[8,4,1024,128]{3,2,1,0:T(8,128)(2,1)} %refs_4_.2) | copy-start | bytes 25165828
  4.8 13.1 %copy-start.1 = (bf16[8,4,1024,128]{3,2,1,0:T(8,128)(2,1)S(1)}, bf16[8,4,1024,128]{3,2,1,0:T(8,128)(2,1)}, u32[]{:S(2)}) copy-start(bf16[8,4,1024,128]{3,2,1,0:T(8,128)(2,1)} %refs_5_.1) | copy-start | bytes 25165828
  7.1 3.8 %collective-permute-start.1 = (bf16[2,4096]{1,0:T(2,128)(2,1)S(1)}, bf16[2,4096]{1,0:T(2,128)(2,1)S(1)}, u32[]{:S(2)}, u32[]{:S(2)}) collective-permute-start(bf16[2,4096]{1,0:T(2,128)(2,1)S(1)} %pad_maximum_fusion.1), channel_id=1, source_target_pairs={{0,8},{2,10},{4,12},{6,14},{8,0},{10,2},{12,4},{14,6},{16,24},{18,... | collective-permute-start | bytes 49160 | tf_op jit(solution)/shard_map/ppermute | solution.py:39
  11.0 5.1 %collective-permute-start.4 = (bf16[4,4096]{1,0:T(4,128)(2,1)S(1)}, bf16[4,4096]{1,0:T(4,128)(2,1)S(1)}, u32[]{:S(2)}, u32[]{:S(2)}) collective-permute-start(bf16[4,4096]{1,0:T(4,128)(2,1)S(1)} %pad_maximum_fusion.refs_0_), channel_id=1, source_target_pairs={{0,6},{2,4},{4,2},{6,0},{8,14},{10,12},{12,10},{14,8},{16,22},{18,... | collective-permute-start | bytes 98312 | tf_op jit(solution)/shard_map/ppermute | solution.py:39
  13.5 3.9 %collective-permute-start.3 = (bf16[4,4096]{1,0:T(4,128)(2,1)S(1)}, bf16[4,4096]{1,0:T(4,128)(2,1)S(1)}, u32[]{:S(2)}, u32[]{:S(2)}) collective-permute-start(bf16[4,4096]{1,0:T(4,128)(2,1)S(1)} %pad_maximum_fusion.refs_0_), channel_id=1, source_target_pairs={{0,4},{2,6},{4,0},{6,2},{8,12},{10,14},{12,8},{14,10},{16,20},{18,... | collective-permute-start | bytes 98312 | tf_op jit(solution)/shard_map/ppermute | solution.py:39
  14.0 3.9 %collective-permute-start.2 = (bf16[4,4096]{1,0:T(4,128)(2,1)S(1)}, bf16[4,4096]{1,0:T(4,128)(2,1)S(1)}, u32[]{:S(2)}, u32[]{:S(2)}) collective-permute-start(bf16[4,4096]{1,0:T(4,128)(2,1)S(1)} %pad_maximum_fusion.refs_0_), channel_id=1, source_target_pairs={{0,2},{2,0},{4,6},{6,4},{8,10},{10,8},{12,14},{14,12},{16,18},{18,... | collective-permute-start | bytes 98312 | tf_op jit(solution)/shard_map/ppermute | solution.py:39
  22.0 16.9 %copy-start.2 = (bf16[4096,512]{1,0:T(8,128)(2,1)S(1)}, bf16[4096,512]{1,0:T(8,128)(2,1)}, u32[]{:S(2)}) copy-start(bf16[4096,512]{1,0:T(8,128)(2,1)} %refs_4_.3) | copy-start | bytes 12582916
  22.0 6.2 %collective-permute-start.7 = (bf16[288,128]{1,0:T(8,128)(2,1)S(1)}, bf16[288,128]{1,0:T(8,128)(2,1)S(1)}, u32[]{:S(2)}, u32[]{:S(2)}) collective-permute-start(bf16[288,128]{1,0:T(8,128)(2,1)S(1)} %attend.1.refs_0_), channel_id=1, source_target_pairs={{0,18},{2,16},{4,22},{6,20},{8,26},{10,24},{12,30},{14,28},{16,2},... | collective-permute-start | bytes 221192 | tf_op jit(solution)/shard_map/ppermute | solution.py:39
  23.8 5.3 %collective-permute-start.6 = (bf16[288,128]{1,0:T(8,128)(2,1)S(1)}, bf16[288,128]{1,0:T(8,128)(2,1)S(1)}, u32[]{:S(2)}, u32[]{:S(2)}) collective-permute-start(bf16[288,128]{1,0:T(8,128)(2,1)S(1)} %attend.1.refs_0_), channel_id=1, source_target_pairs={{0,16},{2,18},{4,20},{6,22},{8,24},{10,26},{12,28},{14,30},{16,0},... | collective-permute-start | bytes 221192 | tf_op jit(solution)/shard_map/ppermute | solution.py:39
  24.9 4.4 %collective-permute-start.5 = (bf16[288,128]{1,0:T(8,128)(2,1)S(1)}, bf16[288,128]{1,0:T(8,128)(2,1)S(1)}, u32[]{:S(2)}, u32[]{:S(2)}) collective-permute-start(bf16[288,128]{1,0:T(8,128)(2,1)S(1)} %attend.1.refs_0_), channel_id=1, source_target_pairs={{0,2},{2,0},{4,6},{6,4},{8,10},{10,8},{12,14},{14,12},{16,18},{18,... | collective-permute-start | bytes 221192 | tf_op jit(solution)/shard_map/ppermute | solution.py:39
  30.5 6.3 %collective-permute-start.10 = (bf16[544,128]{1,0:T(8,128)(2,1)S(1)}, bf16[544,128]{1,0:T(8,128)(2,1)S(1)}, u32[]{:S(2)}, u32[]{:S(2)}) collective-permute-start(bf16[544,128]{1,0:T(8,128)(2,1)S(1)} %merge_slots.1.refs_0_), channel_id=1, source_target_pairs={{0,12},{2,14},{4,8},{6,10},{8,4},{10,6},{12,0},{14,2},{16,28},{18,... | collective-permute-start | bytes 417800 | tf_op jit(solution)/shard_map/ppermute | solution.py:39
  33.8 5.1 %collective-permute-start.9 = (bf16[544,128]{1,0:T(8,128)(2,1)S(1)}, bf16[544,128]{1,0:T(8,128)(2,1)S(1)}, u32[]{:S(2)}, u32[]{:S(2)}) collective-permute-start(bf16[544,128]{1,0:T(8,128)(2,1)S(1)} %merge_slots.1.refs_0_), channel_id=1, source_target_pairs={{0,8},{2,10},{4,12},{6,14},{8,0},{10,2},{12,4},{14,6},{16,24},{18,... | collective-permute-start | bytes 417800 | tf_op jit(solution)/shard_map/ppermute | solution.py:39
  33.8 5.1 %collective-permute-start.8 = (bf16[544,128]{1,0:T(8,128)(2,1)S(1)}, bf16[544,128]{1,0:T(8,128)(2,1)S(1)}, u32[]{:S(2)}, u32[]{:S(2)}) collective-permute-start(bf16[544,128]{1,0:T(8,128)(2,1)S(1)} %merge_slots.1.refs_0_), channel_id=1, source_target_pairs={{0,4},{2,6},{4,0},{6,2},{8,12},{10,14},{12,8},{14,10},{16,20},{18,... | collective-permute-start | bytes 417800 | tf_op jit(solution)/shard_map/ppermute | solution.py:39
  40.0 1.2 %collective-permute-start.11 = (f32[8,512]{1,0:T(8,128)S(1)}, f32[8,512]{1,0:T(8,128)S(1)}, u32[]{:S(2)}, u32[]{:S(2)}) collective-permute-start(f32[8,512]{1,0:T(8,128)S(1)} %get-tuple-element.26), channel_id=1, source_target_pairs={{0,1},{1,0},{2,3},{3,2},{4,5},{5,4},{6,7},{7,6},{8,9},{9,8},{10,11... | collective-permute-start | bytes 49160 | tf_op jit(solution)/shard_map/ppermute | solution.py:471

commit v5 on v4

--- a/solution.py
+++ b/solution.py
@@ -89,10 +89,14 @@
 
 def locate_kernel(
     bits, near, slots, rows, all_slots, own_rows, tokens,
-    table_ref, place_ref, live_ref, owner_ref, position_of, first_of,
+    table_ref, out_ref, position_of, first_of,
 ):
     me = lax.axis_index("page")
     fills, entries = rows, 2 * rows
+    lane = lane_index((1, LANES))
+    places = jnp.zeros((1, LANES), jnp.int32)
+    lives = jnp.zeros((1, LANES), jnp.int32)
+    owners = jnp.full((1, LANES), -1, jnp.int32)
 
     def note(position, carry):
         position_of[table_ref[entries + position]] = position
@@ -111,16 +115,20 @@
             row = functools.reduce(
                 jnp.add, [(position >= end).astype(jnp.int32) for end in ends[:-1]]
             )
-            owner_ref[index * slots + slot] = row
+            owners = jnp.where(lane == index * slots + slot, row, owners)
             if index == 0:
                 away = jnp.bitwise_xor(row // own_rows, me)
                 place, step_size = row % own_rows, own_rows
                 for bit in bits:
                     place += away // bit % 2 * step_size
                     step_size *= 2
-                place_ref[slot] = place
+                places = jnp.where(lane == slot, place, places)
                 before = position - first_of[row]
-                live_ref[slot] = (table_ref[row] - 1 - before) * tokens + table_ref[fills + row]
+                live = (table_ref[row] - 1 - before) * tokens + table_ref[fills + row]
+                lives = jnp.where(lane == slot, live, lives)
+    out_ref[...] = jnp.concatenate(
+        [places, lives, owners, jnp.zeros((5, LANES), jnp.int32)], axis=0
+    )
 
 
 def columns_kernel(group, factor, *refs):
@@ -143,7 +151,7 @@
 
 def attend_kernel(
     pieces, slots, kv_heads, group, tokens, pages,
-    place_ref, live_ref, key_scale_ref, value_scale_ref, *refs,
+    located_ref, key_scale_ref, value_scale_ref, *refs,
 ):
     query_refs = refs[:pieces]
     key_ref, value_ref, out_ref, queries, outs = refs[pieces:]
@@ -165,6 +173,11 @@
     zero = jnp.zeros((rows, LANES), jnp.bfloat16)
     logs = jnp.zeros((heads, LANES), jnp.float32)
 
+    lives = [
+        jnp.broadcast_to(located_ref[1:2, slot : slot + 1], (heads, page_tokens))
+        for slot in range(slots)
+    ]
+
     def joined(ref, slot, kv):
         if together == 1:
             return ref[slot, kv]
@@ -174,7 +187,7 @@
         dotted = []
         for index in range(each):
             slot = batch * each + index
-            start = pl.multiple_of(place_ref[slot] * heads, 8)
+            start = pl.multiple_of(located_ref[0, slot] * heads, 8)
             query = queries[pl.ds(start, heads), :].astype(jnp.bfloat16)
             for kv in range(0, kv_heads, together):
                 own = query[kv * group : kv * group + rows]
@@ -200,8 +213,8 @@
             masked = []
             for index in range(each):
                 own = part[index * heads : (index + 1) * heads]
-                live = live_ref[batch * each + index] - page * page_tokens
-                masked.append(jnp.where(token < live, own, LOW))
+                live = lives[batch * each + index]
+                masked.append(jnp.where(token + page * page_tokens < live, own, LOW))
             scores.append(jnp.concatenate(masked, axis=0) if each > 1 else masked[0])
         peak = jnp.max(functools.reduce(jnp.maximum, scores), axis=1, keepdims=True)
         total, weights = None, []
@@ -244,13 +257,10 @@
     store_stats(out_ref, slots * heads, logs, slots, heads)
 
 
-def merge_slots_kernel(groups, slots, rows, heads, owner_ref, *refs):
+def merge_slots_kernel(groups, slots, rows, heads, located_ref, *refs):
     out_ref, sums = refs[groups:]
     lane = lane_index((heads, LANES))
-    owner = jnp.full((8, LANES), -1, jnp.int32)
-    for at in range(groups * slots):
-        owner = jnp.where(lane[:8] == at, owner_ref[at], owner)
-    owner = jnp.concatenate([owner] * (heads // 8), axis=0)
+    owner = jnp.broadcast_to(located_ref[2:3, :], (heads, LANES))
     logs = jnp.full((heads, LANES), LOW, jnp.float32)
     for index in range(groups):
         own = load_stats(refs[index], slots * heads, slots, heads)
@@ -277,7 +287,7 @@
     for index in range(groups):
         for slot in range(slots):
             at = index * slots + slot
-            start = pl.multiple_of(owner_ref[at] * heads, 8)
+            start = pl.multiple_of(located_ref[2, at] * heads, 8)
             block = pl.ds(start, heads)
             sums[block, :] += weight[:, at : at + 1] * load_entry(refs[index], slot, heads)
     out_ref[: rows * heads, :] = sums[...].astype(jnp.bfloat16)
@@ -350,14 +360,13 @@
 
     near = [0] + rounds[0]
     tables = jnp.concatenate([range_counts, last_fill, slot_table])
-    own_slots = jax.ShapeDtypeStruct((slots,), jnp.int32)
-    place, live, owner = pl.pallas_call(
+    located = pl.pallas_call(
         functools.partial(
             locate_kernel, sum(spread, []), near, slots, rows, all_slots, own_rows, tokens
         ),
-        out_shape=[own_slots, own_slots, jax.ShapeDtypeStruct((len(near) * slots,), jnp.int32)],
+        out_shape=jax.ShapeDtypeStruct((8, LANES), jnp.int32),
         in_specs=[SMEM],
-        out_specs=[SMEM] * 3,
+        out_specs=VMEM,
         scratch_shapes=[
             pltpu.SMEM((all_slots,), jnp.int32),
             pltpu.SMEM((rows,), jnp.int32),
@@ -388,7 +397,7 @@
     for turn, bits in enumerate(spread):
         block = jnp.concatenate(held, axis=0) if len(held) > 1 else held[0]
         if turn == 1:
-            block, place, live, owner = lax.optimization_barrier((block, place, live, owner))
+            block, located = lax.optimization_barrier((block, located))
         elif turn > 1:
             block = lax.optimization_barrier(block)
         held = [block] + [partner(block, mask, devices) for mask in exchange_masks(bits)]
@@ -400,7 +409,7 @@
                 attend_kernel, len(held), slots, kv_heads, group, tokens, pages
             ),
             out_shape=jax.ShapeDtypeStruct((payload, LANES), jnp.bfloat16),
-            in_specs=[SMEM] * 2 + [VMEM] * (len(held) + 4),
+            in_specs=[VMEM] * (len(held) + 5),
             out_specs=VMEM,
             scratch_shapes=[
                 pltpu.VMEM((rows * heads, LANES), jnp.float32),
@@ -414,8 +423,7 @@
             ),
             name="attend",
         )(
-            place,
-            live,
+            located,
             *scales,
             *held,
             key_codes,
@@ -434,7 +442,7 @@
                 pl.pallas_call(
                     functools.partial(merge_slots_kernel, groups, slots, rows, heads),
                     out_shape=jax.ShapeDtypeStruct((payload, LANES), jnp.bfloat16),
-                    in_specs=[SMEM] + [VMEM] * groups,
+                    in_specs=[VMEM] * (groups + 1),
                     out_specs=VMEM,
                     scratch_shapes=[sums],
                     compiler_params=params,
@@ -442,7 +450,7 @@
                         flops=MERGE_FLOPS, bytes_accessed=2 * payload * LANES, transcendentals=0
                     ),
                     name="merge_slots",
-                )(owner, *held)
+                )(located, *held)
             ]
         elif turn < len(rounds) - 1:
             held = [

time: 41.9 us -> 40.8 us (0.974)
  Pallas kernels: 9.37 us -> 7.84 us
    pallas_call x1, Pallas kernels: 2.19 us -> 1.66 us  [per_device(): pl.pallas_call(functools.partial(locate_kernel, sum(spread, []), near, sl...]
    pallas_call x1, Pallas kernels: 1.28 us -> 0.77 us  [per_device(): pl.pallas_call(functools.partial(merge_slots_kernel, groups, slots, rows,...]
    pallas_call x1, Pallas kernels: 4.07 us -> 3.58 us  [per_device(): pl.pallas_call(functools.partial(attend_kernel, len(held), slots, kv_head...]
  transfers between devices with their start and end apart: 12 -> 12, of which waited for: 10 -> 9; matrix products, arithmetic and copies ran while one was open for 2% -> 2% of each run, Pallas kernels for 7% -> 6%
where the time goes in v5:
time: 40.8 us; the launch traced here: 40.7 us
  starting transfers between devices  17.6 us (43%)
  waiting for transfers between devices  13.6 us (33%)
  Pallas kernels  7.84 us (19%)
  other arithmetic  1.45 us (4%)
    ppermute x11, starting transfers between devices, partner(): return lax.ppermute(value, 'page', [(i, i ^ mask) for i in range(devices)])  17.6 us
    ppermute x11, waiting for transfers between devices, partner(): return lax.ppermute(value, 'page', [(i, i ^ mask) for i in range(devices)])  12.5 us
    pallas_call x1, Pallas kernels, per_device(): pl.pallas_call(functools.partial(attend_kernel, len(held), slots, kv_head...  3.58 us
    pallas_call x1, Pallas kernels, per_device(): pl.pallas_call(functools.partial(locate_kernel, sum(spread, []), near, sl...  1.66 us
    ppermute x1, waiting for transfers between devices, per_device(): mixed = mixed + lax.ppermute(give[0], 'head', [(0, 1), (1, 0)])  1.19 us
    pallas_call x1, Pallas kernels, per_device(): pl.pallas_call(functools.partial(project_kernel, len(held), rows, heads,...  1.13 us
  transfers between devices with their start and end apart: 12, of which 9 were waited for; matrix products, arithmetic and copies ran while one was open for 2% of the time, Pallas kernels for 6%

profile of v5, /device:TPU:0, one launch (start us, length us, event | category | flops | bytes accessed | tf_op | source)
XLA Modules:
  0.0 40.7 jit_solution(13031550258510243099)
XLA Ops:
  0.0 4.0 %collective-permute-start = (bf16[1,4096]{1,0:T(2,128)(2,1)}, bf16[1,4096]{1,0:T(2,128)(2,1)S(1)}, u32[]{:S(2)}, u32[]{:S(2)}) collective-permute-start(bf16[1,4096]{1,0:T(2,128)(2,1)} %param.9), channel_id=1, source_target_pairs={{0,16},{2,18},{4,20},{6,22},{8,24},{10,26},{12,28},{14,30},{16,0},... | collective-permute-start | bytes 24584 | tf_op jit(solution)/shard_map/ppermute | solution.py:39
  4.0 0.8 %pad_add_fusion.table_ref = s32[160]{0:T(256)S(1)} fusion(s32[128]{0:T(128)} %param.17, s32[16]{0:T(128)} %param.16, s32[16]{0:T(128)} %param.15), kind=kLoop, calls=%fused_computation.3 | loop fusion | flops 320 | bytes 1280 | tf_op jit(solution)/shard_map/concatenate | solution.py:362
  4.8 1.7 %locate.1.located_ref = s32[8,128]{1,0:T(8,128)S(1)} custom-call(s32[160]{0:T(256)S(1)} %pad_add_fusion.table_ref), custom_call_target="tpu_custom_call" | custom-call | flops 20000000000 | bytes 512 | tf_op jit(solution)/shard_map/locate/pallas_call | solution.py:363
  6.6 1.6 %collective-permute-start.1 = (bf16[2,4096]{1,0:T(2,128)(2,1)S(1)}, bf16[2,4096]{1,0:T(2,128)(2,1)S(1)}, u32[]{:S(2)}, u32[]{:S(2)}) collective-permute-start(bf16[2,4096]{1,0:T(2,128)(2,1)S(1)} %pad_maximum_fusion.1), channel_id=1, source_target_pairs={{0,8},{2,10},{4,12},{6,14},{8,0},{10,2},{12,4},{14,6},{16,24},{18,... | collective-permute-start | bytes 49160 | tf_op jit(solution)/shard_map/ppermute | solution.py:39
  8.2 2.2 %collective-permute-done.1 = bf16[2,4096]{1,0:T(2,128)(2,1)S(1)} collective-permute-done((bf16[2,4096]{1,0:T(2,128)(2,1)S(1)}, bf16[2,4096]{1,0:T(2,128)(2,1)S(1)}, u32[]{:S(2)}, u32[]{:S(2)}) %collective-permute-start.1) | collective-permute-done | bytes 16416 | tf_op jit(solution)/shard_map/ppermute | solution.py:39
  10.4 2.5 %collective-permute-start.4 = (bf16[4,4096]{1,0:T(4,128)(2,1)S(1)}, bf16[4,4096]{1,0:T(4,128)(2,1)S(1)}, u32[]{:S(2)}, u32[]{:S(2)}) collective-permute-start(bf16[4,4096]{1,0:T(4,128)(2,1)S(1)} %pad_maximum_fusion.refs_0_), channel_id=1, source_target_pairs={{0,6},{2,4},{4,2},{6,0},{8,14},{10,12},{12,10},{14,8},{16,22},{18,... | collective-permute-start | bytes 98312 | tf_op jit(solution)/shard_map/ppermute | solution.py:39
  13.4 0.5 %collective-permute-start.2 = (bf16[4,4096]{1,0:T(4,128)(2,1)S(1)}, bf16[4,4096]{1,0:T(4,128)(2,1)S(1)}, u32[]{:S(2)}, u32[]{:S(2)}) collective-permute-start(bf16[4,4096]{1,0:T(4,128)(2,1)S(1)} %pad_maximum_fusion.refs_0_), channel_id=1, source_target_pairs={{0,2},{2,0},{4,6},{6,4},{8,10},{10,8},{12,14},{14,12},{16,18},{18,... | collective-permute-start | bytes 98312 | tf_op jit(solution)/shard_map/ppermute | solution.py:39
  14.0 0.7 %columns.1 = (f32[4,8,64,128]{3,2,1,0:T(8,128)S(1)}, f32[4,8,64,128]{3,2,1,0:T(8,128)S(1)}) custom-call(f32[8,4,8]{2,1,0:T(4,128)S(1)} %copy-done.3, f32[8,4,8]{2,1,0:T(4,128)S(1)} %copy-done.4), custom_call_target="tpu_custom_call" | custom-call | tf_op jit(solution)/shard_map/columns/pallas_call | solution.py:382
  14.7 0.9 %collective-permute-done.4.refs_3_ = bf16[4,4096]{1,0:T(4,128)(2,1)S(1)} collective-permute-done((bf16[4,4096]{1,0:T(4,128)(2,1)S(1)}, bf16[4,4096]{1,0:T(4,128)(2,1)S(1)}, u32[]{:S(2)}, u32[]{:S(2)}) %collective-permute-start.4) | collective-permute-done | bytes 32800 | tf_op jit(solution)/shard_map/ppermute | solution.py:39
  15.5 1.3 %collective-permute-done.3.refs_2_ = bf16[4,4096]{1,0:T(4,128)(2,1)S(1)} collective-permute-done((bf16[4,4096]{1,0:T(4,128)(2,1)S(1)}, bf16[4,4096]{1,0:T(4,128)(2,1)S(1)}, u32[]{:S(2)}, u32[]{:S(2)}) %collective-permute-start.3) | collective-permute-done | bytes 32800 | tf_op jit(solution)/shard_map/ppermute | solution.py:39
  17.4 3.6 %attend.1.refs_0_ = bf16[288,128]{1,0:T(8,128)(2,1)S(1)} custom-call(s32[8,128]{1,0:T(8,128)S(1)} %locate.1.located_ref, f32[4,8,64,128]{3,2,1,0:T(8,128)S(1)} %get-tuple-element.12.key_scale_ref, f32[4,8,64,128]{3,2,1,0:T(8,128)S(1)} %get-tuple-element.13.value_scale_ref, bf16[4,4096]{1,0:T(4,128)(2,1)S(1)} %pad_maximum_fusion.refs_0_, ...), custom_call_target="tpu_custom_call" | custom-call | flops 5000000000 | bytes 16777216 | tf_op jit(solution)/shard_map/attend/pallas_call | solution.py:407
  20.9 2.3 %collective-permute-start.7 = (bf16[288,128]{1,0:T(8,128)(2,1)S(1)}, bf16[288,128]{1,0:T(8,128)(2,1)S(1)}, u32[]{:S(2)}, u32[]{:S(2)}) collective-permute-start(bf16[288,128]{1,0:T(8,128)(2,1)S(1)} %attend.1.refs_0_), channel_id=1, source_target_pairs={{0,18},{2,16},{4,22},{6,20},{8,26},{10,24},{12,30},{14,28},{16,2},... | collective-permute-start | bytes 221192 | tf_op jit(solution)/shard_map/ppermute | solution.py:39
  23.3 0.6 %collective-permute-start.6 = (bf16[288,128]{1,0:T(8,128)(2,1)S(1)}, bf16[288,128]{1,0:T(8,128)(2,1)S(1)}, u32[]{:S(2)}, u32[]{:S(2)}) collective-permute-start(bf16[288,128]{1,0:T(8,128)(2,1)S(1)} %attend.1.refs_0_), channel_id=1, source_target_pairs={{0,16},{2,18},{4,20},{6,22},{8,24},{10,26},{12,28},{14,30},{16,0},... | collective-permute-start | bytes 221192 | tf_op jit(solution)/shard_map/ppermute | solution.py:39
  23.9 1.5 %collective-permute-start.5 = (bf16[288,128]{1,0:T(8,128)(2,1)S(1)}, bf16[288,128]{1,0:T(8,128)(2,1)S(1)}, u32[]{:S(2)}, u32[]{:S(2)}) collective-permute-start(bf16[288,128]{1,0:T(8,128)(2,1)S(1)} %attend.1.refs_0_), channel_id=1, source_target_pairs={{0,2},{2,0},{4,6},{6,4},{8,10},{10,8},{12,14},{14,12},{16,18},{18,... | collective-permute-start | bytes 221192 | tf_op jit(solution)/shard_map/ppermute | solution.py:39
  25.3 1.8 %collective-permute-done.7.refs_3_ = bf16[288,128]{1,0:T(8,128)(2,1)S(1)} collective-permute-done((bf16[288,128]{1,0:T(8,128)(2,1)S(1)}, bf16[288,128]{1,0:T(8,128)(2,1)S(1)}, u32[]{:S(2)}, u32[]{:S(2)}) %collective-permute-start.7) | collective-permute-done | bytes 73760 | tf_op jit(solution)/shard_map/ppermute | solution.py:39
  27.1 1.4 %collective-permute-done.6.refs_2_ = bf16[288,128]{1,0:T(8,128)(2,1)S(1)} collective-permute-done((bf16[288,128]{1,0:T(8,128)(2,1)S(1)}, bf16[288,128]{1,0:T(8,128)(2,1)S(1)}, u32[]{:S(2)}, u32[]{:S(2)}) %collective-permute-start.6) | collective-permute-done | bytes 73760 | tf_op jit(solution)/shard_map/ppermute | solution.py:39
  28.5 0.8 %merge_slots.1.refs_0_ = bf16[544,128]{1,0:T(8,128)(2,1)S(1)} custom-call(s32[8,128]{1,0:T(8,128)S(1)} %locate.1.located_ref, bf16[288,128]{1,0:T(8,128)(2,1)S(1)} %attend.1.refs_0_, bf16[288,128]{1,0:T(8,128)(2,1)S(1)} %collective-permute-done.5.refs_1_, bf16[288,128]{1,0:T(8,128)(2,1)S(1)} %collective-permute-done.6.refs_2_, ...), custom_call_target="tpu_custom_call" | custom-call | flops 20000000000 | bytes 139264 | tf_op jit(solution)/shard_map/merge_slots/pallas_call | solution.py:442
  29.3 3.4 %collective-permute-start.10 = (bf16[544,128]{1,0:T(8,128)(2,1)S(1)}, bf16[544,128]{1,0:T(8,128)(2,1)S(1)}, u32[]{:S(2)}, u32[]{:S(2)}) collective-permute-start(bf16[544,128]{1,0:T(8,128)(2,1)S(1)} %merge_slots.1.refs_0_), channel_id=1, source_target_pairs={{0,12},{2,14},{4,8},{6,10},{8,4},{10,6},{12,0},{14,2},{16,28},{18,... | collective-permute-start | bytes 417800 | tf_op jit(solution)/shard_map/ppermute | solution.py:39
  32.7 0.6 %collective-permute-start.8 = (bf16[544,128]{1,0:T(8,128)(2,1)S(1)}, bf16[544,128]{1,0:T(8,128)(2,1)S(1)}, u32[]{:S(2)}, u32[]{:S(2)}) collective-permute-start(bf16[544,128]{1,0:T(8,128)(2,1)S(1)} %merge_slots.1.refs_0_), channel_id=1, source_target_pairs={{0,4},{2,6},{4,0},{6,2},{8,12},{10,14},{12,8},{14,10},{16,20},{18,... | collective-permute-start | bytes 417800 | tf_op jit(solution)/shard_map/ppermute | solution.py:39
  33.3 2.4 %collective-permute-done.10.refs_3_ = bf16[544,128]{1,0:T(8,128)(2,1)S(1)} collective-permute-done((bf16[544,128]{1,0:T(8,128)(2,1)S(1)}, bf16[544,128]{1,0:T(8,128)(2,1)S(1)}, u32[]{:S(2)}, u32[]{:S(2)}) %collective-permute-start.10) | collective-permute-done | bytes 139296 | tf_op jit(solution)/shard_map/ppermute | solution.py:39
  35.7 2.0 %collective-permute-done.9.refs_2_ = bf16[544,128]{1,0:T(8,128)(2,1)S(1)} collective-permute-done((bf16[544,128]{1,0:T(8,128)(2,1)S(1)}, bf16[544,128]{1,0:T(8,128)(2,1)S(1)}, u32[]{:S(2)}, u32[]{:S(2)}) %collective-permute-start.9) | collective-permute-done | bytes 139296 | tf_op jit(solution)/shard_map/ppermute | solution.py:39
  37.8 1.1 %project.1 = (f32[8,512]{1,0:T(8,128)S(1)}, f32[8,512]{1,0:T(8,128)S(1)}) custom-call(bf16[544,128]{1,0:T(8,128)(2,1)S(1)} %merge_slots.1.refs_0_, bf16[544,128]{1,0:T(8,128)(2,1)S(1)} %collective-permute-done.8.refs_1_, bf16[544,128]{1,0:T(8,128)(2,1)S(1)} %collective-permute-done.9.refs_2_, bf16[544,128]{1,0:T(8,128)(2,1)S(1)} %collective-permute-done.10.refs_3_, ...), custom_call_target="tpu_custom_call" | custom-call | tf_op jit(solution)/shard_map/project/pallas_call | solution.py:469
  38.9 1.2 %collective-permute-done.11 = f32[8,512]{1,0:T(8,128)S(1)} collective-permute-done((f32[8,512]{1,0:T(8,128)S(1)}, f32[8,512]{1,0:T(8,128)S(1)}, u32[]{:S(2)}, u32[]{:S(2)}) %collective-permute-start.11) | collective-permute-done | bytes 16416 | tf_op jit(solution)/shard_map/ppermute | solution.py:479
  40.1 0.6 %add_convert_fusion = bf16[8,512]{1,0:T(8,128)(2,1)} fusion(f32[8,512]{1,0:T(8,128)S(1)} %get-tuple-element.15, f32[8,512]{1,0:T(8,128)S(1)} %collective-permute-done.11), kind=kLoop, calls=%fused_computation.2 | loop fusion | flops 8192 | bytes 40960 | tf_op jit(solution)/shard_map/convert_element_type | solution.py:482
  (21 shorter events, 1.1 us)
Async XLA Ops:
  0.0 6.5 %collective-permute-start = (bf16[1,4096]{1,0:T(2,128)(2,1)}, bf16[1,4096]{1,0:T(2,128)(2,1)S(1)}, u32[]{:S(2)}, u32[]{:S(2)}) collective-permute-start(bf16[1,4096]{1,0:T(2,128)(2,1)} %param.9), channel_id=1, source_target_pairs={{0,16},{2,18},{4,20},{6,22},{8,24},{10,26},{12,28},{14,30},{16,0},... | collective-permute-start | bytes 24584 | tf_op jit(solution)/shard_map/ppermute | solution.py:39
  4.8 1.7 %copy-start.5 = (bf16[1,4096]{1,0:T(2,128)(2,1)S(1)}, bf16[1,4096]{1,0:T(2,128)(2,1)}, u32[]{:S(2)}) copy-start(bf16[1,4096]{1,0:T(2,128)(2,1)} %param.9) | copy-start | bytes 24580
  4.8 9.2 %copy-start.3 = (f32[8,4,8]{2,1,0:T(4,128)S(1)}, f32[8,4,8]{2,1,0:T(4,128)}, u32[]{:S(2)}) copy-start(f32[8,4,8]{2,1,0:T(4,128)} %refs_0_.1) | copy-start | bytes 3076
  4.8 9.2 %copy-start.4 = (f32[8,4,8]{2,1,0:T(4,128)S(1)}, f32[8,4,8]{2,1,0:T(4,128)}, u32[]{:S(2)}) copy-start(f32[8,4,8]{2,1,0:T(4,128)} %refs_1_.1) | copy-start | bytes 3076
  4.8 12.5 %copy-start = (bf16[8,4,1024,128]{3,2,1,0:T(8,128)(2,1)S(1)}, bf16[8,4,1024,128]{3,2,1,0:T(8,128)(2,1)}, u32[]{:S(2)}) copy-start(bf16[8,4,1024,128]{3,2,1,0:T(8,128)(2,1)} %refs_4_.2) | copy-start | bytes 25165828
  4.8 12.5 %copy-start.1 = (bf16[8,4,1024,128]{3,2,1,0:T(8,128)(2,1)S(1)}, bf16[8,4,1024,128]{3,2,1,0:T(8,128)(2,1)}, u32[]{:S(2)}) copy-start(bf16[8,4,1024,128]{3,2,1,0:T(8,128)(2,1)} %refs_5_.1) | copy-start | bytes 25165828
  6.6 3.8 %collective-permute-start.1 = (bf16[2,4096]{1,0:T(2,128)(2,1)S(1)}, bf16[2,4096]{1,0:T(2,128)(2,1)S(1)}, u32[]{:S(2)}, u32[]{:S(2)}) collective-permute-start(bf16[2,4096]{1,0:T(2,128)(2,1)S(1)} %pad_maximum_fusion.1), channel_id=1, source_target_pairs={{0,8},{2,10},{4,12},{6,14},{8,0},{10,2},{12,4},{14,6},{16,24},{18,... | collective-permute-start | bytes 49160 | tf_op jit(solution)/shard_map/ppermute | solution.py:39
  10.4 5.1 %collective-permute-start.4 = (bf16[4,4096]{1,0:T(4,128)(2,1)S(1)}, bf16[4,4096]{1,0:T(4,128)(2,1)S(1)}, u32[]{:S(2)}, u32[]{:S(2)}) collective-permute-start(bf16[4,4096]{1,0:T(4,128)(2,1)S(1)} %pad_maximum_fusion.refs_0_), channel_id=1, source_target_pairs={{0,6},{2,4},{4,2},{6,0},{8,14},{10,12},{12,10},{14,8},{16,22},{18,... | collective-permute-start | bytes 98312 | tf_op jit(solution)/shard_map/ppermute | solution.py:39
  12.9 3.9 %collective-permute-start.3 = (bf16[4,4096]{1,0:T(4,128)(2,1)S(1)}, bf16[4,4096]{1,0:T(4,128)(2,1)S(1)}, u32[]{:S(2)}, u32[]{:S(2)}) collective-permute-start(bf16[4,4096]{1,0:T(4,128)(2,1)S(1)} %pad_maximum_fusion.refs_0_), channel_id=1, source_target_pairs={{0,4},{2,6},{4,0},{6,2},{8,12},{10,14},{12,8},{14,10},{16,20},{18,... | collective-permute-start | bytes 98312 | tf_op jit(solution)/shard_map/ppermute | solution.py:39
  13.4 3.9 %collective-permute-start.2 = (bf16[4,4096]{1,0:T(4,128)(2,1)S(1)}, bf16[4,4096]{1,0:T(4,128)(2,1)S(1)}, u32[]{:S(2)}, u32[]{:S(2)}) collective-permute-start(bf16[4,4096]{1,0:T(4,128)(2,1)S(1)} %pad_maximum_fusion.refs_0_), channel_id=1, source_target_pairs={{0,2},{2,0},{4,6},{6,4},{8,10},{10,8},{12,14},{14,12},{16,18},{18,... | collective-permute-start | bytes 98312 | tf_op jit(solution)/shard_map/ppermute | solution.py:39
  20.9 16.8 %copy-start.2 = (bf16[4096,512]{1,0:T(8,128)(2,1)S(1)}, bf16[4096,512]{1,0:T(8,128)(2,1)}, u32[]{:S(2)}) copy-start(bf16[4096,512]{1,0:T(8,128)(2,1)} %refs_4_.3) | copy-start | bytes 12582916
  20.9 6.2 %collective-permute-start.7 = (bf16[288,128]{1,0:T(8,128)(2,1)S(1)}, bf16[288,128]{1,0:T(8,128)(2,1)S(1)}, u32[]{:S(2)}, u32[]{:S(2)}) collective-permute-start(bf16[288,128]{1,0:T(8,128)(2,1)S(1)} %attend.1.refs_0_), channel_id=1, source_target_pairs={{0,18},{2,16},{4,22},{6,20},{8,26},{10,24},{12,30},{14,28},{16,2},... | collective-permute-start | bytes 221192 | tf_op jit(solution)/shard_map/ppermute | solution.py:39
  23.3 5.3 %collective-permute-start.6 = (bf16[288,128]{1,0:T(8,128)(2,1)S(1)}, bf16[288,128]{1,0:T(8,128)(2,1)S(1)}, u32[]{:S(2)}, u32[]{:S(2)}) collective-permute-start(bf16[288,128]{1,0:T(8,128)(2,1)S(1)} %attend.1.refs_0_), channel_id=1, source_target_pairs={{0,16},{2,18},{4,20},{6,22},{8,24},{10,26},{12,28},{14,30},{16,0},... | collective-permute-start | bytes 221192 | tf_op jit(solution)/shard_map/ppermute | solution.py:39
  23.9 4.7 %collective-permute-start.5 = (bf16[288,128]{1,0:T(8,128)(2,1)S(1)}, bf16[288,128]{1,0:T(8,128)(2,1)S(1)}, u32[]{:S(2)}, u32[]{:S(2)}) collective-permute-start(bf16[288,128]{1,0:T(8,128)(2,1)S(1)} %attend.1.refs_0_), channel_id=1, source_target_pairs={{0,2},{2,0},{4,6},{6,4},{8,10},{10,8},{12,14},{14,12},{16,18},{18,... | collective-permute-start | bytes 221192 | tf_op jit(solution)/shard_map/ppermute | solution.py:39
  29.3 6.4 %collective-permute-start.10 = (bf16[544,128]{1,0:T(8,128)(2,1)S(1)}, bf16[544,128]{1,0:T(8,128)(2,1)S(1)}, u32[]{:S(2)}, u32[]{:S(2)}) collective-permute-start(bf16[544,128]{1,0:T(8,128)(2,1)S(1)} %merge_slots.1.refs_0_), channel_id=1, source_target_pairs={{0,12},{2,14},{4,8},{6,10},{8,4},{10,6},{12,0},{14,2},{16,28},{18,... | collective-permute-start | bytes 417800 | tf_op jit(solution)/shard_map/ppermute | solution.py:39
  32.7 5.1 %collective-permute-start.9 = (bf16[544,128]{1,0:T(8,128)(2,1)S(1)}, bf16[544,128]{1,0:T(8,128)(2,1)S(1)}, u32[]{:S(2)}, u32[]{:S(2)}) collective-permute-start(bf16[544,128]{1,0:T(8,128)(2,1)S(1)} %merge_slots.1.refs_0_), channel_id=1, source_target_pairs={{0,8},{2,10},{4,12},{6,14},{8,0},{10,2},{12,4},{14,6},{16,24},{18,... | collective-permute-start | bytes 417800 | tf_op jit(solution)/shard_map/ppermute | solution.py:39
  32.7 5.1 %collective-permute-start.8 = (bf16[544,128]{1,0:T(8,128)(2,1)S(1)}, bf16[544,128]{1,0:T(8,128)(2,1)S(1)}, u32[]{:S(2)}, u32[]{:S(2)}) collective-permute-start(bf16[544,128]{1,0:T(8,128)(2,1)S(1)} %merge_slots.1.refs_0_), channel_id=1, source_target_pairs={{0,4},{2,6},{4,0},{6,2},{8,12},{10,14},{12,8},{14,10},{16,20},{18,... | collective-permute-start | bytes 417800 | tf_op jit(solution)/shard_map/ppermute | solution.py:39
  38.9 1.2 %collective-permute-start.11 = (f32[8,512]{1,0:T(8,128)S(1)}, f32[8,512]{1,0:T(8,128)S(1)}, u32[]{:S(2)}, u32[]{:S(2)}) collective-permute-start(f32[8,512]{1,0:T(8,128)S(1)} %get-tuple-element.16), channel_id=1, source_target_pairs={{0,1},{1,0},{2,3},{3,2},{4,5},{5,4},{6,7},{7,6},{8,9},{9,8},{10,11... | collective-permute-start | bytes 49160 | tf_op jit(solution)/shard_map/ppermute | solution.py:479

commit v6 on v5

--- a/solution.py
+++ b/solution.py
@@ -26,12 +26,13 @@
 
 def spread_rounds(devices):
     bits = [1 << k for k in range(devices.bit_length() - 1)]
-    return [[bit] for bit in reversed(bits[2:])] + [bits[:2]]
+    return [bits[:2]] + [bits[k : k + 2] for k in range(2, len(bits), 2)]
 
 
 def merge_rounds(devices):
     bits = [1 << k for k in range(devices.bit_length() - 1)]
-    pairs = [[bits[k], bits[-1 - k]] for k in range(len(bits) // 2)]
+    pairs = [[bits[-1 - k], bits[k]] for k in range(len(bits) // 2)]
+    pairs[0] = pairs[0][::-1]
     return pairs + ([[bits[len(bits) // 2]]] if len(bits) % 2 else [])
 
 

time: 40.8 us -> 39.5 us (0.968)
  starting transfers between devices: 17.6 us -> 16.9 us
  waiting for transfers between devices: 13.6 us -> 13.1 us
    ppermute x11 -> x12, starting transfers between devices: 17.6 us -> 16.9 us  [partner(): return lax.ppermute(value, 'page', [(i, i ^ mask) for i in range(devices)])]
    ppermute x11 -> x12, waiting for transfers between devices: 12.5 us -> 11.9 us  [partner(): return lax.ppermute(value, 'page', [(i, i ^ mask) for i in range(devices)])]
  transfers between devices with their start and end apart: 12 -> 13, of which waited for: 9 -> 8; matrix products, arithmetic and copies ran while one was open for 2% -> 2% of each run, Pallas kernels for 6% -> 6%
where the time goes in v6:
time: 39.5 us; the launch traced here: 39.4 us
  starting transfers between devices  16.9 us (43%)
  waiting for transfers between devices  13.1 us (33%)
  Pallas kernels  7.83 us (20%)
  other arithmetic  1.45 us (4%)
    ppermute x12, starting transfers between devices, partner(): return lax.ppermute(value, 'page', [(i, i ^ mask) for i in range(devices)])  16.9 us
    ppermute x12, waiting for transfers between devices, partner(): return lax.ppermute(value, 'page', [(i, i ^ mask) for i in range(devices)])  11.9 us
    pallas_call x1, Pallas kernels, per_device(): pl.pallas_call(functools.partial(attend_kernel, len(held), slots, kv_head...  3.58 us
    pallas_call x1, Pallas kernels, per_device(): pl.pallas_call(functools.partial(locate_kernel, sum(spread, []), near, sl...  1.66 us
    ppermute x1, waiting for transfers between devices, per_device(): mixed = mixed + lax.ppermute(give[0], 'head', [(0, 1), (1, 0)])  1.19 us
    pallas_call x1, Pallas kernels, per_device(): pl.pallas_call(functools.partial(project_kernel, len(held), rows, heads,...  1.13 us
  transfers between devices with their start and end apart: 13, of which 8 were waited for; matrix products, arithmetic and copies ran while one was open for 2% of the time, Pallas kernels for 6%

profile of v6, /device:TPU:0, one launch (start us, length us, event | category | flops | bytes accessed | tf_op | source)
XLA Modules:
  0.0 39.4 jit_solution(933377112125728112)
XLA Ops:
  0.0 3.0 %collective-permute-start.1 = (bf16[1,4096]{1,0:T(2,128)(2,1)}, bf16[1,4096]{1,0:T(2,128)(2,1)S(1)}, u32[]{:S(2)}, u32[]{:S(2)}) collective-permute-start(bf16[1,4096]{1,0:T(2,128)(2,1)} %param.9), channel_id=1, source_target_pairs={{0,4},{2,6},{4,0},{6,2},{8,12},{10,14},{12,8},{14,10},{16,20},{18,... | collective-permute-start | bytes 24584 | tf_op jit(solution)/shard_map/ppermute | solution.py:40
  3.0 1.5 %collective-permute-start = (bf16[1,4096]{1,0:T(2,128)(2,1)}, bf16[1,4096]{1,0:T(2,128)(2,1)S(1)}, u32[]{:S(2)}, u32[]{:S(2)}) collective-permute-start(bf16[1,4096]{1,0:T(2,128)(2,1)} %param.9), channel_id=1, source_target_pairs={{0,2},{2,0},{4,6},{6,4},{8,10},{10,8},{12,14},{14,12},{16,18},{18,... | collective-permute-start | bytes 24584 | tf_op jit(solution)/shard_map/ppermute | solution.py:40
  4.5 0.8 %pad_add_fusion.table_ref = s32[160]{0:T(256)S(1)} fusion(s32[128]{0:T(128)} %param.17, s32[16]{0:T(128)} %param.16, s32[16]{0:T(128)} %param.15), kind=kLoop, calls=%fused_computation.2 | loop fusion | flops 320 | bytes 1280 | tf_op jit(solution)/shard_map/concatenate | solution.py:363
  5.3 1.7 %locate.1.located_ref = s32[8,128]{1,0:T(8,128)S(1)} custom-call(s32[160]{0:T(256)S(1)} %pad_add_fusion.table_ref), custom_call_target="tpu_custom_call" | custom-call | flops 20000000000 | bytes 512 | tf_op jit(solution)/shard_map/locate/pallas_call | solution.py:364
  7.0 2.4 %collective-permute-done.2 = bf16[1,4096]{1,0:T(2,128)(2,1)S(1)} collective-permute-done((bf16[1,4096]{1,0:T(2,128)(2,1)}, bf16[1,4096]{1,0:T(2,128)(2,1)S(1)}, u32[]{:S(2)}, u32[]{:S(2)}) %collective-permute-start.2) | collective-permute-done | bytes 8224 | tf_op jit(solution)/shard_map/ppermute | solution.py:40
  9.4 3.7 %collective-permute-start.5 = (bf16[4,4096]{1,0:T(4,128)(2,1)S(1)}, bf16[4,4096]{1,0:T(4,128)(2,1)S(1)}, u32[]{:S(2)}, u32[]{:S(2)}) collective-permute-start(bf16[4,4096]{1,0:T(4,128)(2,1)S(1)} %pad_maximum_fusion.refs_0_), channel_id=1, source_target_pairs={{0,24},{2,26},{4,28},{6,30},{8,16},{10,18},{12,20},{14,22},{16,8},... | collective-permute-start | bytes 98312 | tf_op jit(solution)/shard_map/ppermute | solution.py:40
  13.1 0.8 %collective-permute-start.3 = (bf16[4,4096]{1,0:T(4,128)(2,1)S(1)}, bf16[4,4096]{1,0:T(4,128)(2,1)S(1)}, u32[]{:S(2)}, u32[]{:S(2)}) collective-permute-start(bf16[4,4096]{1,0:T(4,128)(2,1)S(1)} %pad_maximum_fusion.refs_0_), channel_id=1, source_target_pairs={{0,8},{2,10},{4,12},{6,14},{8,0},{10,2},{12,4},{14,6},{16,24},{18,... | collective-permute-start | bytes 98312 | tf_op jit(solution)/shard_map/ppermute | solution.py:40
  13.9 0.7 %columns.1 = (f32[4,8,64,128]{3,2,1,0:T(8,128)S(1)}, f32[4,8,64,128]{3,2,1,0:T(8,128)S(1)}) custom-call(f32[8,4,8]{2,1,0:T(4,128)S(1)} %copy-done.3, f32[8,4,8]{2,1,0:T(4,128)S(1)} %copy-done.4), custom_call_target="tpu_custom_call" | custom-call | tf_op jit(solution)/shard_map/columns/pallas_call | solution.py:383
  14.6 0.6 %collective-permute-done.5.refs_3_ = bf16[4,4096]{1,0:T(4,128)(2,1)S(1)} collective-permute-done((bf16[4,4096]{1,0:T(4,128)(2,1)S(1)}, bf16[4,4096]{1,0:T(4,128)(2,1)S(1)}, u32[]{:S(2)}, u32[]{:S(2)}) %collective-permute-start.5) | collective-permute-done | bytes 32800 | tf_op jit(solution)/shard_map/ppermute | solution.py:40
  15.2 2.7 %collective-permute-done.4.refs_2_ = bf16[4,4096]{1,0:T(4,128)(2,1)S(1)} collective-permute-done((bf16[4,4096]{1,0:T(4,128)(2,1)S(1)}, bf16[4,4096]{1,0:T(4,128)(2,1)S(1)}, u32[]{:S(2)}, u32[]{:S(2)}) %collective-permute-start.4) | collective-permute-done | bytes 32800 | tf_op jit(solution)/shard_map/ppermute | solution.py:40
  17.9 3.6 %attend.1.refs_0_ = bf16[288,128]{1,0:T(8,128)(2,1)S(1)} custom-call(s32[8,128]{1,0:T(8,128)S(1)} %locate.1.located_ref, f32[4,8,64,128]{3,2,1,0:T(8,128)S(1)} %get-tuple-element.12.key_scale_ref, f32[4,8,64,128]{3,2,1,0:T(8,128)S(1)} %get-tuple-element.13.value_scale_ref, bf16[4,4096]{1,0:T(4,128)(2,1)S(1)} %pad_maximum_fusion.refs_0_, ...), custom_call_target="tpu_custom_call" | custom-call | flops 5000000000 | bytes 16777216 | tf_op jit(solution)/shard_map/attend/pallas_call | solution.py:408
  21.5 2.0 %collective-permute-start.8 = (bf16[288,128]{1,0:T(8,128)(2,1)S(1)}, bf16[288,128]{1,0:T(8,128)(2,1)S(1)}, u32[]{:S(2)}, u32[]{:S(2)}) collective-permute-start(bf16[288,128]{1,0:T(8,128)(2,1)S(1)} %attend.1.refs_0_), channel_id=1, source_target_pairs={{0,18},{2,16},{4,22},{6,20},{8,26},{10,24},{12,30},{14,28},{16,2},... | collective-permute-start | bytes 221192 | tf_op jit(solution)/shard_map/ppermute | solution.py:40
  23.5 0.9 %collective-permute-start.7 = (bf16[288,128]{1,0:T(8,128)(2,1)S(1)}, bf16[288,128]{1,0:T(8,128)(2,1)S(1)}, u32[]{:S(2)}, u32[]{:S(2)}) collective-permute-start(bf16[288,128]{1,0:T(8,128)(2,1)S(1)} %attend.1.refs_0_), channel_id=1, source_target_pairs={{0,16},{2,18},{4,20},{6,22},{8,24},{10,26},{12,28},{14,30},{16,0},... | collective-permute-start | bytes 221192 | tf_op jit(solution)/shard_map/ppermute | solution.py:40
  24.4 1.5 %collective-permute-start.6 = (bf16[288,128]{1,0:T(8,128)(2,1)S(1)}, bf16[288,128]{1,0:T(8,128)(2,1)S(1)}, u32[]{:S(2)}, u32[]{:S(2)}) collective-permute-start(bf16[288,128]{1,0:T(8,128)(2,1)S(1)} %attend.1.refs_0_), channel_id=1, source_target_pairs={{0,2},{2,0},{4,6},{6,4},{8,10},{10,8},{12,14},{14,12},{16,18},{18,... | collective-permute-start | bytes 221192 | tf_op jit(solution)/shard_map/ppermute | solution.py:40
  25.9 1.9 %collective-permute-done.8.refs_3_ = bf16[288,128]{1,0:T(8,128)(2,1)S(1)} collective-permute-done((bf16[288,128]{1,0:T(8,128)(2,1)S(1)}, bf16[288,128]{1,0:T(8,128)(2,1)S(1)}, u32[]{:S(2)}, u32[]{:S(2)}) %collective-permute-start.8) | collective-permute-done | bytes 73760 | tf_op jit(solution)/shard_map/ppermute | solution.py:40
  27.7 1.2 %collective-permute-done.7.refs_2_ = bf16[288,128]{1,0:T(8,128)(2,1)S(1)} collective-permute-done((bf16[288,128]{1,0:T(8,128)(2,1)S(1)}, bf16[288,128]{1,0:T(8,128)(2,1)S(1)}, u32[]{:S(2)}, u32[]{:S(2)}) %collective-permute-start.7) | collective-permute-done | bytes 73760 | tf_op jit(solution)/shard_map/ppermute | solution.py:40
  29.0 0.8 %merge_slots.1.refs_0_ = bf16[544,128]{1,0:T(8,128)(2,1)S(1)} custom-call(s32[8,128]{1,0:T(8,128)S(1)} %locate.1.located_ref, bf16[288,128]{1,0:T(8,128)(2,1)S(1)} %attend.1.refs_0_, bf16[288,128]{1,0:T(8,128)(2,1)S(1)} %collective-permute-done.6.refs_1_, bf16[288,128]{1,0:T(8,128)(2,1)S(1)} %collective-permute-done.7.refs_2_, ...), custom_call_target="tpu_custom_call" | custom-call | flops 20000000000 | bytes 139264 | tf_op jit(solution)/shard_map/merge_slots/pallas_call | solution.py:443
  29.8 1.2 %collective-permute-start.10 = (bf16[544,128]{1,0:T(8,128)(2,1)S(1)}, bf16[544,128]{1,0:T(8,128)(2,1)S(1)}, u32[]{:S(2)}, u32[]{:S(2)}) collective-permute-start(bf16[544,128]{1,0:T(8,128)(2,1)S(1)} %merge_slots.1.refs_0_), channel_id=1, source_target_pairs={{0,4},{2,6},{4,0},{6,2},{8,12},{10,14},{12,8},{14,10},{16,20},{18,... | collective-permute-start | bytes 417800 | tf_op jit(solution)/shard_map/ppermute | solution.py:40
  31.1 2.2 %collective-permute-start.9 = (bf16[544,128]{1,0:T(8,128)(2,1)S(1)}, bf16[544,128]{1,0:T(8,128)(2,1)S(1)}, u32[]{:S(2)}, u32[]{:S(2)}) collective-permute-start(bf16[544,128]{1,0:T(8,128)(2,1)S(1)} %merge_slots.1.refs_0_), channel_id=1, source_target_pairs={{0,8},{2,10},{4,12},{6,14},{8,0},{10,2},{12,4},{14,6},{16,24},{18,... | collective-permute-start | bytes 417800 | tf_op jit(solution)/shard_map/ppermute | solution.py:40
  33.3 2.6 %collective-permute-done.11.refs_3_ = bf16[544,128]{1,0:T(8,128)(2,1)S(1)} collective-permute-done((bf16[544,128]{1,0:T(8,128)(2,1)S(1)}, bf16[544,128]{1,0:T(8,128)(2,1)S(1)}, u32[]{:S(2)}, u32[]{:S(2)}) %collective-permute-start.11) | collective-permute-done | bytes 139296 | tf_op jit(solution)/shard_map/ppermute | solution.py:40
  35.9 0.6 %collective-permute-done.10.refs_2_ = bf16[544,128]{1,0:T(8,128)(2,1)S(1)} collective-permute-done((bf16[544,128]{1,0:T(8,128)(2,1)S(1)}, bf16[544,128]{1,0:T(8,128)(2,1)S(1)}, u32[]{:S(2)}, u32[]{:S(2)}) %collective-permute-start.10) | collective-permute-done | bytes 139296 | tf_op jit(solution)/shard_map/ppermute | solution.py:40
  36.5 1.1 %project.1 = (f32[8,512]{1,0:T(8,128)S(1)}, f32[8,512]{1,0:T(8,128)S(1)}) custom-call(bf16[544,128]{1,0:T(8,128)(2,1)S(1)} %merge_slots.1.refs_0_, bf16[544,128]{1,0:T(8,128)(2,1)S(1)} %collective-permute-done.9.refs_1_, bf16[544,128]{1,0:T(8,128)(2,1)S(1)} %collective-permute-done.10.refs_2_, bf16[544,128]{1,0:T(8,128)(2,1)S(1)} %collective-permute-done.11.refs_3_, ...), custom_call_target="tpu_custom_call" | custom-call | tf_op jit(solution)/shard_map/project/pallas_call | solution.py:470
  37.6 1.2 %collective-permute-done.12 = f32[8,512]{1,0:T(8,128)S(1)} collective-permute-done((f32[8,512]{1,0:T(8,128)S(1)}, f32[8,512]{1,0:T(8,128)S(1)}, u32[]{:S(2)}, u32[]{:S(2)}) %collective-permute-start.12) | collective-permute-done | bytes 16416 | tf_op jit(solution)/shard_map/ppermute | solution.py:480
  38.8 0.6 %add_convert_fusion = bf16[8,512]{1,0:T(8,128)(2,1)} fusion(f32[8,512]{1,0:T(8,128)S(1)} %get-tuple-element.15, f32[8,512]{1,0:T(8,128)S(1)} %collective-permute-done.12), kind=kLoop, calls=%fused_computation.1 | loop fusion | flops 8192 | bytes 40960 | tf_op jit(solution)/shard_map/convert_element_type | solution.py:483
  (22 shorter events, 0.2 us)
Async XLA Ops:
  0.0 6.9 %collective-permute-start.1 = (bf16[1,4096]{1,0:T(2,128)(2,1)}, bf16[1,4096]{1,0:T(2,128)(2,1)S(1)}, u32[]{:S(2)}, u32[]{:S(2)}) collective-permute-start(bf16[1,4096]{1,0:T(2,128)(2,1)} %param.9), channel_id=1, source_target_pairs={{0,4},{2,6},{4,0},{6,2},{8,12},{10,14},{12,8},{14,10},{16,20},{18,... | collective-permute-start | bytes 24584 | tf_op jit(solution)/shard_map/ppermute | solution.py:40
  3.0 4.0 %collective-permute-start = (bf16[1,4096]{1,0:T(2,128)(2,1)}, bf16[1,4096]{1,0:T(2,128)(2,1)S(1)}, u32[]{:S(2)}, u32[]{:S(2)}) collective-permute-start(bf16[1,4096]{1,0:T(2,128)(2,1)} %param.9), channel_id=1, source_target_pairs={{0,2},{2,0},{4,6},{6,4},{8,10},{10,8},{12,14},{14,12},{16,18},{18,... | collective-permute-start | bytes 24584 | tf_op jit(solution)/shard_map/ppermute | solution.py:40
  4.5 4.8 %collective-permute-start.2 = (bf16[1,4096]{1,0:T(2,128)(2,1)}, bf16[1,4096]{1,0:T(2,128)(2,1)S(1)}, u32[]{:S(2)}, u32[]{:S(2)}) collective-permute-start(bf16[1,4096]{1,0:T(2,128)(2,1)} %param.9), channel_id=1, source_target_pairs={{0,6},{2,4},{4,2},{6,0},{8,14},{10,12},{12,10},{14,8},{16,22},{18,... | collective-permute-start | bytes 24584 | tf_op jit(solution)/shard_map/ppermute | solution.py:40
  5.2 4.1 %copy-start.5 = (bf16[1,4096]{1,0:T(2,128)(2,1)S(1)}, bf16[1,4096]{1,0:T(2,128)(2,1)}, u32[]{:S(2)}) copy-start(bf16[1,4096]{1,0:T(2,128)(2,1)} %param.9) | copy-start | bytes 24580
  5.2 8.6 %copy-start.3 = (f32[8,4,8]{2,1,0:T(4,128)S(1)}, f32[8,4,8]{2,1,0:T(4,128)}, u32[]{:S(2)}) copy-start(f32[8,4,8]{2,1,0:T(4,128)} %refs_0_.1) | copy-start | bytes 3076
  5.2 8.6 %copy-start.4 = (f32[8,4,8]{2,1,0:T(4,128)S(1)}, f32[8,4,8]{2,1,0:T(4,128)}, u32[]{:S(2)}) copy-start(f32[8,4,8]{2,1,0:T(4,128)} %refs_1_.1) | copy-start | bytes 3076
  5.2 12.7 %copy-start = (bf16[8,4,1024,128]{3,2,1,0:T(8,128)(2,1)S(1)}, bf16[8,4,1024,128]{3,2,1,0:T(8,128)(2,1)}, u32[]{:S(2)}) copy-start(bf16[8,4,1024,128]{3,2,1,0:T(8,128)(2,1)} %refs_4_.2) | copy-start | bytes 25165828
  5.2 12.6 %copy-start.1 = (bf16[8,4,1024,128]{3,2,1,0:T(8,128)(2,1)S(1)}, bf16[8,4,1024,128]{3,2,1,0:T(8,128)(2,1)}, u32[]{:S(2)}) copy-start(bf16[8,4,1024,128]{3,2,1,0:T(8,128)(2,1)} %refs_5_.1) | copy-start | bytes 25165828
  9.4 5.8 %collective-permute-start.5 = (bf16[4,4096]{1,0:T(4,128)(2,1)S(1)}, bf16[4,4096]{1,0:T(4,128)(2,1)S(1)}, u32[]{:S(2)}, u32[]{:S(2)}) collective-permute-start(bf16[4,4096]{1,0:T(4,128)(2,1)S(1)} %pad_maximum_fusion.refs_0_), channel_id=1, source_target_pairs={{0,24},{2,26},{4,28},{6,30},{8,16},{10,18},{12,20},{14,22},{16,8},... | collective-permute-start | bytes 98312 | tf_op jit(solution)/shard_map/ppermute | solution.py:40
  13.1 4.8 %collective-permute-start.4 = (bf16[4,4096]{1,0:T(4,128)(2,1)S(1)}, bf16[4,4096]{1,0:T(4,128)(2,1)S(1)}, u32[]{:S(2)}, u32[]{:S(2)}) collective-permute-start(bf16[4,4096]{1,0:T(4,128)(2,1)S(1)} %pad_maximum_fusion.refs_0_), channel_id=1, source_target_pairs={{0,16},{2,18},{4,20},{6,22},{8,24},{10,26},{12,28},{14,30},{16,0},... | collective-permute-start | bytes 98312 | tf_op jit(solution)/shard_map/ppermute | solution.py:40
  13.1 4.8 %collective-permute-start.3 = (bf16[4,4096]{1,0:T(4,128)(2,1)S(1)}, bf16[4,4096]{1,0:T(4,128)(2,1)S(1)}, u32[]{:S(2)}, u32[]{:S(2)}) collective-permute-start(bf16[4,4096]{1,0:T(4,128)(2,1)S(1)} %pad_maximum_fusion.refs_0_), channel_id=1, source_target_pairs={{0,8},{2,10},{4,12},{6,14},{8,0},{10,2},{12,4},{14,6},{16,24},{18,... | collective-permute-start | bytes 98312 | tf_op jit(solution)/shard_map/ppermute | solution.py:40
  21.5 15.0 %copy-start.2 = (bf16[4096,512]{1,0:T(8,128)(2,1)S(1)}, bf16[4096,512]{1,0:T(8,128)(2,1)}, u32[]{:S(2)}) copy-start(bf16[4096,512]{1,0:T(8,128)(2,1)} %refs_4_.3) | copy-start | bytes 12582916
  21.5 6.3 %collective-permute-start.8 = (bf16[288,128]{1,0:T(8,128)(2,1)S(1)}, bf16[288,128]{1,0:T(8,128)(2,1)S(1)}, u32[]{:S(2)}, u32[]{:S(2)}) collective-permute-start(bf16[288,128]{1,0:T(8,128)(2,1)S(1)} %attend.1.refs_0_), channel_id=1, source_target_pairs={{0,18},{2,16},{4,22},{6,20},{8,26},{10,24},{12,30},{14,28},{16,2},... | collective-permute-start | bytes 221192 | tf_op jit(solution)/shard_map/ppermute | solution.py:40
  23.5 5.5 %collective-permute-start.7 = (bf16[288,128]{1,0:T(8,128)(2,1)S(1)}, bf16[288,128]{1,0:T(8,128)(2,1)S(1)}, u32[]{:S(2)}, u32[]{:S(2)}) collective-permute-start(bf16[288,128]{1,0:T(8,128)(2,1)S(1)} %attend.1.refs_0_), channel_id=1, source_target_pairs={{0,16},{2,18},{4,20},{6,22},{8,24},{10,26},{12,28},{14,30},{16,0},... | collective-permute-start | bytes 221192 | tf_op jit(solution)/shard_map/ppermute | solution.py:40
  24.4 4.6 %collective-permute-start.6 = (bf16[288,128]{1,0:T(8,128)(2,1)S(1)}, bf16[288,128]{1,0:T(8,128)(2,1)S(1)}, u32[]{:S(2)}, u32[]{:S(2)}) collective-permute-start(bf16[288,128]{1,0:T(8,128)(2,1)S(1)} %attend.1.refs_0_), channel_id=1, source_target_pairs={{0,2},{2,0},{4,6},{6,4},{8,10},{10,8},{12,14},{14,12},{16,18},{18,... | collective-permute-start | bytes 221192 | tf_op jit(solution)/shard_map/ppermute | solution.py:40
  29.7 6.1 %collective-permute-start.11 = (bf16[544,128]{1,0:T(8,128)(2,1)S(1)}, bf16[544,128]{1,0:T(8,128)(2,1)S(1)}, u32[]{:S(2)}, u32[]{:S(2)}) collective-permute-start(bf16[544,128]{1,0:T(8,128)(2,1)S(1)} %merge_slots.1.refs_0_), channel_id=1, source_target_pairs={{0,12},{2,14},{4,8},{6,10},{8,4},{10,6},{12,0},{14,2},{16,28},{18,... | collective-permute-start | bytes 417800 | tf_op jit(solution)/shard_map/ppermute | solution.py:40
  29.8 6.6 %collective-permute-start.10 = (bf16[544,128]{1,0:T(8,128)(2,1)S(1)}, bf16[544,128]{1,0:T(8,128)(2,1)S(1)}, u32[]{:S(2)}, u32[]{:S(2)}) collective-permute-start(bf16[544,128]{1,0:T(8,128)(2,1)S(1)} %merge_slots.1.refs_0_), channel_id=1, source_target_pairs={{0,4},{2,6},{4,0},{6,2},{8,12},{10,14},{12,8},{14,10},{16,20},{18,... | collective-permute-start | bytes 417800 | tf_op jit(solution)/shard_map/ppermute | solution.py:40
  31.1 5.4 %collective-permute-start.9 = (bf16[544,128]{1,0:T(8,128)(2,1)S(1)}, bf16[544,128]{1,0:T(8,128)(2,1)S(1)}, u32[]{:S(2)}, u32[]{:S(2)}) collective-permute-start(bf16[544,128]{1,0:T(8,128)(2,1)S(1)} %merge_slots.1.refs_0_), channel_id=1, source_target_pairs={{0,8},{2,10},{4,12},{6,14},{8,0},{10,2},{12,4},{14,6},{16,24},{18,... | collective-permute-start | bytes 417800 | tf_op jit(solution)/shard_map/ppermute | solution.py:40
  37.6 1.2 %collective-permute-start.12 = (f32[8,512]{1,0:T(8,128)S(1)}, f32[8,512]{1,0:T(8,128)S(1)}, u32[]{:S(2)}, u32[]{:S(2)}) collective-permute-start(f32[8,512]{1,0:T(8,128)S(1)} %get-tuple-element.16), channel_id=1, source_target_pairs={{0,1},{1,0},{2,3},{3,2},{4,5},{5,4},{6,7},{7,6},{8,9},{9,8},{10,11... | collective-permute-start | bytes 49160 | tf_op jit(solution)/shard_map/ppermute | solution.py:480

commit v7 on v6

--- a/solution.py
+++ b/solution.py
@@ -49,6 +49,19 @@
     return stat_place(2, entries)[0] + 1
 
 
+def stat_fold(entries, heads):
+    width = LANES
+    if stat_blocks(entries) == 1 and heads % 32 == 0:
+        while width // 2 >= 3 * entries and width > LANES // 4:
+            width //= 2
+    return LANES // width, width
+
+
+def stat_rows(entries, heads):
+    rows = stat_blocks(entries) * heads // stat_fold(entries, heads)[0]
+    return (rows + 15) // 16 * 16
+
+
 def lane_index(shape):
     return lax.broadcasted_iota(jnp.int32, shape, 1)
 
@@ -57,27 +70,40 @@
     high = logs.astype(jnp.bfloat16).astype(jnp.float32)
     middle = (logs - high).astype(jnp.bfloat16).astype(jnp.float32)
     low = logs - high - middle
-    lane = lane_index((heads, LANES))
-    blocks = [jnp.zeros((heads, LANES), jnp.float32) for _ in range(stat_blocks(entries))]
+    fold, width = stat_fold(entries, heads)
+    size = heads // fold
+    lane = lane_index((size, LANES))
+    blocks = [jnp.zeros((size, LANES), jnp.float32) for _ in range(stat_blocks(entries))]
     for piece, value in enumerate((high, middle, low)):
         block, offset = stat_place(piece, entries)
-        moved = pltpu.roll(value, offset, 1) if offset else value
-        inside = (lane >= offset) & (lane < offset + entries)
-        blocks[block] = jnp.where(inside, moved, blocks[block])
+        for k in range(fold):
+            first = offset + k * width
+            slab = value[k * size : (k + 1) * size]
+            slab = pltpu.roll(slab, first, 1) if first else slab
+            inside = (lane >= first) & (lane < first + entries)
+            blocks[block] = jnp.where(inside, slab, blocks[block])
+    rest = stat_rows(entries, heads) - size * len(blocks)
+    if rest:
+        blocks.append(jnp.zeros((rest, LANES), jnp.float32))
     table = jnp.concatenate(blocks, axis=0) if len(blocks) > 1 else blocks[0]
     out_ref[base : base + table.shape[0], :] = table.astype(jnp.bfloat16)
 
 
-def load_stats(ref, base, entries, heads):
-    rows = stat_blocks(entries) * heads
-    table = ref[base : base + rows, :].astype(jnp.float32)
-    total = None
-    for piece in range(3):
-        block, offset = stat_place(piece, entries)
-        value = table[block * heads : (block + 1) * heads]
-        value = pltpu.roll(value, LANES - offset, 1) if offset else value
-        total = value if total is None else total + value
-    return total
+def load_stats(ref, base, entries, heads, shift=0):
+    table = ref[base : base + stat_rows(entries, heads), :].astype(jnp.float32)
+    fold, width = stat_fold(entries, heads)
+    size = heads // fold
+    slabs = []
+    for k in range(fold):
+        total = None
+        for piece in range(3):
+            block, offset = stat_place(piece, entries)
+            value = table[block * size : (block + 1) * size]
+            move = (shift - offset - k * width) % LANES
+            value = pltpu.roll(value, move, 1) if move else value
+            total = value if total is None else total + value
+        slabs.append(total)
+    return jnp.concatenate(slabs, axis=0) if fold > 1 else slabs[0]
 
 
 def load_entry(ref, index, heads):
@@ -264,8 +290,7 @@
     owner = jnp.broadcast_to(located_ref[2:3, :], (heads, LANES))
     logs = jnp.full((heads, LANES), LOW, jnp.float32)
     for index in range(groups):
-        own = load_stats(refs[index], slots * heads, slots, heads)
-        own = pltpu.roll(own, index * slots, 1) if index else own
+        own = load_stats(refs[index], slots * heads, slots, heads, index * slots)
         inside = (lane >= index * slots) & (lane < (index + 1) * slots)
         logs = jnp.where(inside, own, logs)
     tops = jnp.zeros((heads, LANES), jnp.float32)
@@ -403,7 +428,7 @@
             block = lax.optimization_barrier(block)
         held = [block] + [partner(block, mask, devices) for mask in exchange_masks(bits)]
 
-    payload = (slots + stat_blocks(slots)) * heads
+    payload = slots * heads + stat_rows(slots, heads)
     held = [
         pl.pallas_call(
             functools.partial(
@@ -432,7 +457,7 @@
         )
     ]
 
-    payload = (rows + stat_blocks(rows)) * heads
+    payload = rows * heads + stat_rows(rows, heads)
     sums = pltpu.VMEM((rows * heads, LANES), jnp.float32)
     for turn, masks in enumerate(rounds):
         held = held + [partner(held[0], mask, devices) for mask in masks]

time: 39.5 us -> 39.4 us (level)
  no operation moved by 1% of the time
where the time goes in v7:
time: 39.4 us; the launch traced here: 39.2 us
  starting transfers between devices  16.9 us (43%)
  waiting for transfers between devices  13 us (33%)
  Pallas kernels  7.82 us (20%)
  other arithmetic  1.45 us (4%)
    ppermute x12, starting transfers between devices, partner(): return lax.ppermute(value, 'page', [(i, i ^ mask) for i in range(devices)])  16.9 us
    ppermute x12, waiting for transfers between devices, partner(): return lax.ppermute(value, 'page', [(i, i ^ mask) for i in range(devices)])  11.8 us
    pallas_call x1, Pallas kernels, per_device(): pl.pallas_call(functools.partial(attend_kernel, len(held), slots, kv_head...  3.58 us
    pallas_call x1, Pallas kernels, per_device(): pl.pallas_call(functools.partial(locate_kernel, sum(spread, []), near, sl...  1.66 us
    ppermute x1, waiting for transfers between devices, per_device(): mixed = mixed + lax.ppermute(give[0], 'head', [(0, 1), (1, 0)])  1.19 us
    pallas_call x1, Pallas kernels, per_device(): pl.pallas_call(functools.partial(project_kernel, len(held), rows, heads,...  1.14 us
  transfers between devices with their start and end apart: 13, of which 8 were waited for; matrix products, arithmetic and copies ran while one was open for 2% of the time, Pallas kernels for 6%

profile of v7, /device:TPU:0, one launch (start us, length us, event | category | flops | bytes accessed | tf_op | source)
XLA Modules:
  0.0 39.2 jit_solution(7399517782252095714)
XLA Ops:
  0.0 3.0 %collective-permute-start.1 = (bf16[1,4096]{1,0:T(2,128)(2,1)}, bf16[1,4096]{1,0:T(2,128)(2,1)S(1)}, u32[]{:S(2)}, u32[]{:S(2)}) collective-permute-start(bf16[1,4096]{1,0:T(2,128)(2,1)} %param.9), channel_id=1, source_target_pairs={{0,4},{2,6},{4,0},{6,2},{8,12},{10,14},{12,8},{14,10},{16,20},{18,... | collective-permute-start | bytes 24584 | tf_op jit(solution)/shard_map/ppermute | solution.py:40
  3.0 1.5 %collective-permute-start = (bf16[1,4096]{1,0:T(2,128)(2,1)}, bf16[1,4096]{1,0:T(2,128)(2,1)S(1)}, u32[]{:S(2)}, u32[]{:S(2)}) collective-permute-start(bf16[1,4096]{1,0:T(2,128)(2,1)} %param.9), channel_id=1, source_target_pairs={{0,2},{2,0},{4,6},{6,4},{8,10},{10,8},{12,14},{14,12},{16,18},{18,... | collective-permute-start | bytes 24584 | tf_op jit(solution)/shard_map/ppermute | solution.py:40
  4.5 0.8 %pad_add_fusion.table_ref = s32[160]{0:T(256)S(1)} fusion(s32[128]{0:T(128)} %param.17, s32[16]{0:T(128)} %param.16, s32[16]{0:T(128)} %param.15), kind=kLoop, calls=%fused_computation.2 | loop fusion | flops 320 | bytes 1280 | tf_op jit(solution)/shard_map/concatenate | solution.py:388
  5.3 1.7 %locate.1.located_ref = s32[8,128]{1,0:T(8,128)S(1)} custom-call(s32[160]{0:T(256)S(1)} %pad_add_fusion.table_ref), custom_call_target="tpu_custom_call" | custom-call | flops 20000000000 | bytes 512 | tf_op jit(solution)/shard_map/locate/pallas_call | solution.py:389
  7.0 2.4 %collective-permute-done.2 = bf16[1,4096]{1,0:T(2,128)(2,1)S(1)} collective-permute-done((bf16[1,4096]{1,0:T(2,128)(2,1)}, bf16[1,4096]{1,0:T(2,128)(2,1)S(1)}, u32[]{:S(2)}, u32[]{:S(2)}) %collective-permute-start.2) | collective-permute-done | bytes 8224 | tf_op jit(solution)/shard_map/ppermute | solution.py:40
  9.4 3.7 %collective-permute-start.5 = (bf16[4,4096]{1,0:T(4,128)(2,1)S(1)}, bf16[4,4096]{1,0:T(4,128)(2,1)S(1)}, u32[]{:S(2)}, u32[]{:S(2)}) collective-permute-start(bf16[4,4096]{1,0:T(4,128)(2,1)S(1)} %pad_maximum_fusion.refs_0_), channel_id=1, source_target_pairs={{0,24},{2,26},{4,28},{6,30},{8,16},{10,18},{12,20},{14,22},{16,8},... | collective-permute-start | bytes 98312 | tf_op jit(solution)/shard_map/ppermute | solution.py:40
  13.1 0.8 %collective-permute-start.3 = (bf16[4,4096]{1,0:T(4,128)(2,1)S(1)}, bf16[4,4096]{1,0:T(4,128)(2,1)S(1)}, u32[]{:S(2)}, u32[]{:S(2)}) collective-permute-start(bf16[4,4096]{1,0:T(4,128)(2,1)S(1)} %pad_maximum_fusion.refs_0_), channel_id=1, source_target_pairs={{0,8},{2,10},{4,12},{6,14},{8,0},{10,2},{12,4},{14,6},{16,24},{18,... | collective-permute-start | bytes 98312 | tf_op jit(solution)/shard_map/ppermute | solution.py:40
  13.9 0.7 %columns.1 = (f32[4,8,64,128]{3,2,1,0:T(8,128)S(1)}, f32[4,8,64,128]{3,2,1,0:T(8,128)S(1)}) custom-call(f32[8,4,8]{2,1,0:T(4,128)S(1)} %copy-done.3, f32[8,4,8]{2,1,0:T(4,128)S(1)} %copy-done.4), custom_call_target="tpu_custom_call" | custom-call | tf_op jit(solution)/shard_map/columns/pallas_call | solution.py:408
  14.6 0.6 %collective-permute-done.5.refs_3_ = bf16[4,4096]{1,0:T(4,128)(2,1)S(1)} collective-permute-done((bf16[4,4096]{1,0:T(4,128)(2,1)S(1)}, bf16[4,4096]{1,0:T(4,128)(2,1)S(1)}, u32[]{:S(2)}, u32[]{:S(2)}) %collective-permute-start.5) | collective-permute-done | bytes 32800 | tf_op jit(solution)/shard_map/ppermute | solution.py:40
  15.2 2.7 %collective-permute-done.4.refs_2_ = bf16[4,4096]{1,0:T(4,128)(2,1)S(1)} collective-permute-done((bf16[4,4096]{1,0:T(4,128)(2,1)S(1)}, bf16[4,4096]{1,0:T(4,128)(2,1)S(1)}, u32[]{:S(2)}, u32[]{:S(2)}) %collective-permute-start.4) | collective-permute-done | bytes 32800 | tf_op jit(solution)/shard_map/ppermute | solution.py:40
  17.9 3.6 %attend.1.refs_0_ = bf16[272,128]{1,0:T(8,128)(2,1)S(1)} custom-call(s32[8,128]{1,0:T(8,128)S(1)} %locate.1.located_ref, f32[4,8,64,128]{3,2,1,0:T(8,128)S(1)} %get-tuple-element.12.key_scale_ref, f32[4,8,64,128]{3,2,1,0:T(8,128)S(1)} %get-tuple-element.13.value_scale_ref, bf16[4,4096]{1,0:T(4,128)(2,1)S(1)} %pad_maximum_fusion.refs_0_, ...), custom_call_target="tpu_custom_call" | custom-call | flops 5000000000 | bytes 16777216 | tf_op jit(solution)/shard_map/attend/pallas_call | solution.py:433
  21.5 2.0 %collective-permute-start.8 = (bf16[272,128]{1,0:T(8,128)(2,1)S(1)}, bf16[272,128]{1,0:T(8,128)(2,1)S(1)}, u32[]{:S(2)}, u32[]{:S(2)}) collective-permute-start(bf16[272,128]{1,0:T(8,128)(2,1)S(1)} %attend.1.refs_0_), channel_id=1, source_target_pairs={{0,18},{2,16},{4,22},{6,20},{8,26},{10,24},{12,30},{14,28},{16,2},... | collective-permute-start | bytes 208904 | tf_op jit(solution)/shard_map/ppermute | solution.py:40
  23.5 0.9 %collective-permute-start.7 = (bf16[272,128]{1,0:T(8,128)(2,1)S(1)}, bf16[272,128]{1,0:T(8,128)(2,1)S(1)}, u32[]{:S(2)}, u32[]{:S(2)}) collective-permute-start(bf16[272,128]{1,0:T(8,128)(2,1)S(1)} %attend.1.refs_0_), channel_id=1, source_target_pairs={{0,16},{2,18},{4,20},{6,22},{8,24},{10,26},{12,28},{14,30},{16,0},... | collective-permute-start | bytes 208904 | tf_op jit(solution)/shard_map/ppermute | solution.py:40
  24.4 1.5 %collective-permute-start.6 = (bf16[272,128]{1,0:T(8,128)(2,1)S(1)}, bf16[272,128]{1,0:T(8,128)(2,1)S(1)}, u32[]{:S(2)}, u32[]{:S(2)}) collective-permute-start(bf16[272,128]{1,0:T(8,128)(2,1)S(1)} %attend.1.refs_0_), channel_id=1, source_target_pairs={{0,2},{2,0},{4,6},{6,4},{8,10},{10,8},{12,14},{14,12},{16,18},{18,... | collective-permute-start | bytes 208904 | tf_op jit(solution)/shard_map/ppermute | solution.py:40
  25.9 1.8 %collective-permute-done.8.refs_3_ = bf16[272,128]{1,0:T(8,128)(2,1)S(1)} collective-permute-done((bf16[272,128]{1,0:T(8,128)(2,1)S(1)}, bf16[272,128]{1,0:T(8,128)(2,1)S(1)}, u32[]{:S(2)}, u32[]{:S(2)}) %collective-permute-start.8) | collective-permute-done | bytes 69664 | tf_op jit(solution)/shard_map/ppermute | solution.py:40
  27.7 1.2 %collective-permute-done.7.refs_2_ = bf16[272,128]{1,0:T(8,128)(2,1)S(1)} collective-permute-done((bf16[272,128]{1,0:T(8,128)(2,1)S(1)}, bf16[272,128]{1,0:T(8,128)(2,1)S(1)}, u32[]{:S(2)}, u32[]{:S(2)}) %collective-permute-start.7) | collective-permute-done | bytes 69664 | tf_op jit(solution)/shard_map/ppermute | solution.py:40
  28.9 0.7 %merge_slots.1.refs_0_ = bf16[528,128]{1,0:T(8,128)(2,1)S(1)} custom-call(s32[8,128]{1,0:T(8,128)S(1)} %locate.1.located_ref, bf16[272,128]{1,0:T(8,128)(2,1)S(1)} %attend.1.refs_0_, bf16[272,128]{1,0:T(8,128)(2,1)S(1)} %collective-permute-done.6.refs_1_, bf16[272,128]{1,0:T(8,128)(2,1)S(1)} %collective-permute-done.7.refs_2_, ...), custom_call_target="tpu_custom_call" | custom-call | flops 20000000000 | bytes 135168 | tf_op jit(solution)/shard_map/merge_slots/pallas_call | solution.py:468
  29.7 1.3 %collective-permute-start.10 = (bf16[528,128]{1,0:T(8,128)(2,1)S(1)}, bf16[528,128]{1,0:T(8,128)(2,1)S(1)}, u32[]{:S(2)}, u32[]{:S(2)}) collective-permute-start(bf16[528,128]{1,0:T(8,128)(2,1)S(1)} %merge_slots.1.refs_0_), channel_id=1, source_target_pairs={{0,4},{2,6},{4,0},{6,2},{8,12},{10,14},{12,8},{14,10},{16,20},{18,... | collective-permute-start | bytes 405512 | tf_op jit(solution)/shard_map/ppermute | solution.py:40
  31.0 2.2 %collective-permute-start.9 = (bf16[528,128]{1,0:T(8,128)(2,1)S(1)}, bf16[528,128]{1,0:T(8,128)(2,1)S(1)}, u32[]{:S(2)}, u32[]{:S(2)}) collective-permute-start(bf16[528,128]{1,0:T(8,128)(2,1)S(1)} %merge_slots.1.refs_0_), channel_id=1, source_target_pairs={{0,8},{2,10},{4,12},{6,14},{8,0},{10,2},{12,4},{14,6},{16,24},{18,... | collective-permute-start | bytes 405512 | tf_op jit(solution)/shard_map/ppermute | solution.py:40
  33.2 2.5 %collective-permute-done.11.refs_3_ = bf16[528,128]{1,0:T(8,128)(2,1)S(1)} collective-permute-done((bf16[528,128]{1,0:T(8,128)(2,1)S(1)}, bf16[528,128]{1,0:T(8,128)(2,1)S(1)}, u32[]{:S(2)}, u32[]{:S(2)}) %collective-permute-start.11) | collective-permute-done | bytes 135200 | tf_op jit(solution)/shard_map/ppermute | solution.py:40
  35.7 0.5 %collective-permute-done.10.refs_2_ = bf16[528,128]{1,0:T(8,128)(2,1)S(1)} collective-permute-done((bf16[528,128]{1,0:T(8,128)(2,1)S(1)}, bf16[528,128]{1,0:T(8,128)(2,1)S(1)}, u32[]{:S(2)}, u32[]{:S(2)}) %collective-permute-start.10) | collective-permute-done | bytes 135200 | tf_op jit(solution)/shard_map/ppermute | solution.py:40
  36.3 1.1 %project.1 = (f32[8,512]{1,0:T(8,128)S(1)}, f32[8,512]{1,0:T(8,128)S(1)}) custom-call(bf16[528,128]{1,0:T(8,128)(2,1)S(1)} %merge_slots.1.refs_0_, bf16[528,128]{1,0:T(8,128)(2,1)S(1)} %collective-permute-done.9.refs_1_, bf16[528,128]{1,0:T(8,128)(2,1)S(1)} %collective-permute-done.10.refs_2_, bf16[528,128]{1,0:T(8,128)(2,1)S(1)} %collective-permute-done.11.refs_3_, ...), custom_call_target="tpu_custom_call" | custom-call | tf_op jit(solution)/shard_map/project/pallas_call | solution.py:495
  37.4 1.2 %collective-permute-done.12 = f32[8,512]{1,0:T(8,128)S(1)} collective-permute-done((f32[8,512]{1,0:T(8,128)S(1)}, f32[8,512]{1,0:T(8,128)S(1)}, u32[]{:S(2)}, u32[]{:S(2)}) %collective-permute-start.12) | collective-permute-done | bytes 16416 | tf_op jit(solution)/shard_map/ppermute | solution.py:505
  38.6 0.6 %add_convert_fusion = bf16[8,512]{1,0:T(8,128)(2,1)} fusion(f32[8,512]{1,0:T(8,128)S(1)} %get-tuple-element.15, f32[8,512]{1,0:T(8,128)S(1)} %collective-permute-done.12), kind=kLoop, calls=%fused_computation.1 | loop fusion | flops 8192 | bytes 40960 | tf_op jit(solution)/shard_map/convert_element_type | solution.py:508
  (22 shorter events, 0.2 us)
Async XLA Ops:
  0.0 6.9 %collective-permute-start.1 = (bf16[1,4096]{1,0:T(2,128)(2,1)}, bf16[1,4096]{1,0:T(2,128)(2,1)S(1)}, u32[]{:S(2)}, u32[]{:S(2)}) collective-permute-start(bf16[1,4096]{1,0:T(2,128)(2,1)} %param.9), channel_id=1, source_target_pairs={{0,4},{2,6},{4,0},{6,2},{8,12},{10,14},{12,8},{14,10},{16,20},{18,... | collective-permute-start | bytes 24584 | tf_op jit(solution)/shard_map/ppermute | solution.py:40
  3.0 4.0 %collective-permute-start = (bf16[1,4096]{1,0:T(2,128)(2,1)}, bf16[1,4096]{1,0:T(2,128)(2,1)S(1)}, u32[]{:S(2)}, u32[]{:S(2)}) collective-permute-start(bf16[1,4096]{1,0:T(2,128)(2,1)} %param.9), channel_id=1, source_target_pairs={{0,2},{2,0},{4,6},{6,4},{8,10},{10,8},{12,14},{14,12},{16,18},{18,... | collective-permute-start | bytes 24584 | tf_op jit(solution)/shard_map/ppermute | solution.py:40
  4.5 4.8 %collective-permute-start.2 = (bf16[1,4096]{1,0:T(2,128)(2,1)}, bf16[1,4096]{1,0:T(2,128)(2,1)S(1)}, u32[]{:S(2)}, u32[]{:S(2)}) collective-permute-start(bf16[1,4096]{1,0:T(2,128)(2,1)} %param.9), channel_id=1, source_target_pairs={{0,6},{2,4},{4,2},{6,0},{8,14},{10,12},{12,10},{14,8},{16,22},{18,... | collective-permute-start | bytes 24584 | tf_op jit(solution)/shard_map/ppermute | solution.py:40
  5.2 4.1 %copy-start.5 = (bf16[1,4096]{1,0:T(2,128)(2,1)S(1)}, bf16[1,4096]{1,0:T(2,128)(2,1)}, u32[]{:S(2)}) copy-start(bf16[1,4096]{1,0:T(2,128)(2,1)} %param.9) | copy-start | bytes 24580
  5.2 8.6 %copy-start.3 = (f32[8,4,8]{2,1,0:T(4,128)S(1)}, f32[8,4,8]{2,1,0:T(4,128)}, u32[]{:S(2)}) copy-start(f32[8,4,8]{2,1,0:T(4,128)} %refs_0_.1) | copy-start | bytes 3076
  5.2 8.6 %copy-start.4 = (f32[8,4,8]{2,1,0:T(4,128)S(1)}, f32[8,4,8]{2,1,0:T(4,128)}, u32[]{:S(2)}) copy-start(f32[8,4,8]{2,1,0:T(4,128)} %refs_1_.1) | copy-start | bytes 3076
  5.2 12.7 %copy-start = (bf16[8,4,1024,128]{3,2,1,0:T(8,128)(2,1)S(1)}, bf16[8,4,1024,128]{3,2,1,0:T(8,128)(2,1)}, u32[]{:S(2)}) copy-start(bf16[8,4,1024,128]{3,2,1,0:T(8,128)(2,1)} %refs_4_.2) | copy-start | bytes 25165828
  5.2 12.6 %copy-start.1 = (bf16[8,4,1024,128]{3,2,1,0:T(8,128)(2,1)S(1)}, bf16[8,4,1024,128]{3,2,1,0:T(8,128)(2,1)}, u32[]{:S(2)}) copy-start(bf16[8,4,1024,128]{3,2,1,0:T(8,128)(2,1)} %refs_5_.1) | copy-start | bytes 25165828
  9.4 5.8 %collective-permute-start.5 = (bf16[4,4096]{1,0:T(4,128)(2,1)S(1)}, bf16[4,4096]{1,0:T(4,128)(2,1)S(1)}, u32[]{:S(2)}, u32[]{:S(2)}) collective-permute-start(bf16[4,4096]{1,0:T(4,128)(2,1)S(1)} %pad_maximum_fusion.refs_0_), channel_id=1, source_target_pairs={{0,24},{2,26},{4,28},{6,30},{8,16},{10,18},{12,20},{14,22},{16,8},... | collective-permute-start | bytes 98312 | tf_op jit(solution)/shard_map/ppermute | solution.py:40
  13.1 4.8 %collective-permute-start.4 = (bf16[4,4096]{1,0:T(4,128)(2,1)S(1)}, bf16[4,4096]{1,0:T(4,128)(2,1)S(1)}, u32[]{:S(2)}, u32[]{:S(2)}) collective-permute-start(bf16[4,4096]{1,0:T(4,128)(2,1)S(1)} %pad_maximum_fusion.refs_0_), channel_id=1, source_target_pairs={{0,16},{2,18},{4,20},{6,22},{8,24},{10,26},{12,28},{14,30},{16,0},... | collective-permute-start | bytes 98312 | tf_op jit(solution)/shard_map/ppermute | solution.py:40
  13.1 4.8 %collective-permute-start.3 = (bf16[4,4096]{1,0:T(4,128)(2,1)S(1)}, bf16[4,4096]{1,0:T(4,128)(2,1)S(1)}, u32[]{:S(2)}, u32[]{:S(2)}) collective-permute-start(bf16[4,4096]{1,0:T(4,128)(2,1)S(1)} %pad_maximum_fusion.refs_0_), channel_id=1, source_target_pairs={{0,8},{2,10},{4,12},{6,14},{8,0},{10,2},{12,4},{14,6},{16,24},{18,... | collective-permute-start | bytes 98312 | tf_op jit(solution)/shard_map/ppermute | solution.py:40
  21.5 14.8 %copy-start.2 = (bf16[4096,512]{1,0:T(8,128)(2,1)S(1)}, bf16[4096,512]{1,0:T(8,128)(2,1)}, u32[]{:S(2)}) copy-start(bf16[4096,512]{1,0:T(8,128)(2,1)} %refs_4_.3) | copy-start | bytes 12582916
  21.5 6.2 %collective-permute-start.8 = (bf16[272,128]{1,0:T(8,128)(2,1)S(1)}, bf16[272,128]{1,0:T(8,128)(2,1)S(1)}, u32[]{:S(2)}, u32[]{:S(2)}) collective-permute-start(bf16[272,128]{1,0:T(8,128)(2,1)S(1)} %attend.1.refs_0_), channel_id=1, source_target_pairs={{0,18},{2,16},{4,22},{6,20},{8,26},{10,24},{12,30},{14,28},{16,2},... | collective-permute-start | bytes 208904 | tf_op jit(solution)/shard_map/ppermute | solution.py:40
  23.5 5.4 %collective-permute-start.7 = (bf16[272,128]{1,0:T(8,128)(2,1)S(1)}, bf16[272,128]{1,0:T(8,128)(2,1)S(1)}, u32[]{:S(2)}, u32[]{:S(2)}) collective-permute-start(bf16[272,128]{1,0:T(8,128)(2,1)S(1)} %attend.1.refs_0_), channel_id=1, source_target_pairs={{0,16},{2,18},{4,20},{6,22},{8,24},{10,26},{12,28},{14,30},{16,0},... | collective-permute-start | bytes 208904 | tf_op jit(solution)/shard_map/ppermute | solution.py:40
  24.4 4.5 %collective-permute-start.6 = (bf16[272,128]{1,0:T(8,128)(2,1)S(1)}, bf16[272,128]{1,0:T(8,128)(2,1)S(1)}, u32[]{:S(2)}, u32[]{:S(2)}) collective-permute-start(bf16[272,128]{1,0:T(8,128)(2,1)S(1)} %attend.1.refs_0_), channel_id=1, source_target_pairs={{0,2},{2,0},{4,6},{6,4},{8,10},{10,8},{12,14},{14,12},{16,18},{18,... | collective-permute-start | bytes 208904 | tf_op jit(solution)/shard_map/ppermute | solution.py:40
  29.7 6.1 %collective-permute-start.11 = (bf16[528,128]{1,0:T(8,128)(2,1)S(1)}, bf16[528,128]{1,0:T(8,128)(2,1)S(1)}, u32[]{:S(2)}, u32[]{:S(2)}) collective-permute-start(bf16[528,128]{1,0:T(8,128)(2,1)S(1)} %merge_slots.1.refs_0_), channel_id=1, source_target_pairs={{0,12},{2,14},{4,8},{6,10},{8,4},{10,6},{12,0},{14,2},{16,28},{18,... | collective-permute-start | bytes 405512 | tf_op jit(solution)/shard_map/ppermute | solution.py:40
  29.7 6.5 %collective-permute-start.10 = (bf16[528,128]{1,0:T(8,128)(2,1)S(1)}, bf16[528,128]{1,0:T(8,128)(2,1)S(1)}, u32[]{:S(2)}, u32[]{:S(2)}) collective-permute-start(bf16[528,128]{1,0:T(8,128)(2,1)S(1)} %merge_slots.1.refs_0_), channel_id=1, source_target_pairs={{0,4},{2,6},{4,0},{6,2},{8,12},{10,14},{12,8},{14,10},{16,20},{18,... | collective-permute-start | bytes 405512 | tf_op jit(solution)/shard_map/ppermute | solution.py:40
  31.0 5.3 %collective-permute-start.9 = (bf16[528,128]{1,0:T(8,128)(2,1)S(1)}, bf16[528,128]{1,0:T(8,128)(2,1)S(1)}, u32[]{:S(2)}, u32[]{:S(2)}) collective-permute-start(bf16[528,128]{1,0:T(8,128)(2,1)S(1)} %merge_slots.1.refs_0_), channel_id=1, source_target_pairs={{0,8},{2,10},{4,12},{6,14},{8,0},{10,2},{12,4},{14,6},{16,24},{18,... | collective-permute-start | bytes 405512 | tf_op jit(solution)/shard_map/ppermute | solution.py:40
  37.4 1.2 %collective-permute-start.12 = (f32[8,512]{1,0:T(8,128)S(1)}, f32[8,512]{1,0:T(8,128)S(1)}, u32[]{:S(2)}, u32[]{:S(2)}) collective-permute-start(f32[8,512]{1,0:T(8,128)S(1)} %get-tuple-element.16), channel_id=1, source_target_pairs={{0,1},{1,0},{2,3},{3,2},{4,5},{5,4},{6,7},{7,6},{8,9},{9,8},{10,11... | collective-permute-start | bytes 49160 | tf_op jit(solution)/shard_map/ppermute | solution.py:505
